TPU v7x, 512 devices: a whole 4x4x16 slice. The times are simulated.
512 devices in a mesh: cells: 128 (over y, z, core), per: 4 (over x).
Axes of the slice: x: 4, y: 4, z: 16, core: 2. Of those that a mesh axis runs over, the one named last changes fastest.
Arguments:
- field: float32 [128, 2, 8, 65536], P('per', None, None, 'cells'), may hold values from -12 to 12
- period_gain: float32 [128], replicated, may hold values from 0.3 to 3
- start_basis: float32 [128, 32], replicated, may hold values from -0.5 to 0.5
Outputs:
- projected: float32 [128, 2, 8, 65536], P('per', None, None, 'cells')
All inputs are finite; a program needn't handle non-finite values.
Results may differ from a plain program's by a relative error of at most 0.0003.
Values sent between devices are 32-bit elements; how exact they have to be, the bound alone decides.
No kernel may reach another device: no remote copies, remote signals or barrier semaphores. Data moves between devices by JAX's collectives and lax.ppermute only.
A program may use at most 192 MiB of HBM per device.

v0:
```python
import jax
import jax.numpy as jnp
from jax import lax
from jax.sharding import PartitionSpec as P

ITERS = 3


HIGH = lax.Precision.HIGHEST


def refine(gram, basis):
    for step in range(ITERS):
        grown = jnp.dot(gram, basis, precision=HIGH)
        inner = jnp.dot(grown.T, grown, precision=HIGH)
        lower = jnp.linalg.cholesky(inner)
        basis = lax.linalg.triangular_solve(
            lower, grown, left_side=False, lower=True, transpose_a=True
        )
    return basis


def per_device(field, period_gain, start_basis):
    group_index = lax.axis_index("per")
    local_periods = field.shape[0]
    gains = lax.dynamic_slice_in_dim(period_gain, group_index * local_periods, local_periods)
    scaled = field * gains[:, None, None, None]
    total_rows = 2.0 * field.shape[2] * field.shape[3] * lax.axis_size("cells")
    rows = lax.all_to_all(scaled, "per", split_axis=2, concat_axis=0, tiled=True)
    flat = rows.reshape(rows.shape[0], -1)
    local_gram = lax.dot_general(flat, flat, (((1,), (1,)), ((), ())), precision=HIGH) / total_rows
    gram = lax.psum(local_gram, ("cells", "per"))
    basis = refine(gram, start_basis)
    projector = jnp.dot(basis, basis.T, precision=HIGH)
    result = lax.dot_general(projector, flat, (((0,), (0,)), ((), ())), precision=HIGH)
    result = result.reshape(rows.shape)
    return lax.all_to_all(result, "per", split_axis=0, concat_axis=2, tiled=True)


def solution(mesh):
    in_specs = (P("per", None, None, "cells"), P(), P())
    out_specs = P("per", None, None, "cells")
    return jax.shard_map(
        per_device, mesh=mesh, in_specs=in_specs, out_specs=out_specs, check_vma=False
    )
```

profile of v0, /device:TPU:1, one launch (start us, length us, event | category | flops | bytes accessed | tf_op | source)
XLA Modules:
  0.0 527.2 jit_solution(264155576138425697)
XLA Ops:
  6.5 0.0 copy-start
  6.5 0.0 all-reduce.2.cloned.1.call-start
  6.5 0.0 copy-start.2
  6.5 0.7 copy-done.2
  7.2 0.1 dynamic_slice.3
  7.3 1.8 copy_multiply_fusion
  9.1 15.1 %all_to_all.33 = f32[32,2,8,512]{3,0,1,2:T(8,128)S(1)} all-to-all(f32[32,2,8,512]{3,0,1,2:T(8,128)S(1)} %copy_multiply_fusion), channel_id=1, replica_groups=mesh['cells'=128,'per'=4] {'per'}, dimensions={2} | all-to-all | bytes 2097152 | tf_op jit(solution)/shard_map/all_to_all | solution.py:29
  24.2 0.8 copy.37
  25.1 0.9 reshape.18
  26.0 1.6 convolution_multiply_fusion
  27.6 0.0 all-reduce.2.cloned.1.call-update
  27.6 0.3 copy.29
  27.9 447.9 %all-reduce.2.cloned.1.call-done = f32[128,128]{1,0:T(8,128)} async-done(((f32[128,128]{1,0:T(8,128)}), f32[128,128]{1,0:T(8,128)}) %all-reduce.2.cloned.1.call-update) | async-done | bytes 65552 | tf_op jit(solution)/shard_map/psum | solution.py:32
  475.8 0.0 copy-done
  475.8 1.0 fusion.13
  476.8 0.2 fusion.14
  477.0 0.1 copy.26
  477.1 0.0 copy-start.1
  477.1 2.9 cholesky.59
  480.1 0.6 compare_reduce_fusion.2
  480.7 0.7 fusion
  481.4 2.4 custom-call.7
  483.8 0.2 convolution_bitcast_fusion.3
  484.0 0.0 copy-done.1
  484.0 0.2 fusion.15
  484.2 0.2 fusion.16
  484.4 0.1 copy.27
  484.5 2.9 cholesky.70
  487.5 0.6 compare_reduce_fusion.1
  488.1 0.7 fusion.1
  488.8 2.4 custom-call.8
  491.2 0.2 convolution_bitcast_fusion.2
  491.4 0.2 fusion.17
  491.6 0.2 fusion.18
  491.8 0.1 copy.28
  491.9 2.9 cholesky.81
  494.9 0.6 compare_reduce_fusion
  495.5 0.7 fusion.2
  496.2 2.4 custom-call.9
  498.6 0.2 convolution_bitcast_fusion.1
  498.8 0.3 convolution_bitcast_fusion
  499.2 1.0 fusion.19
  500.2 0.8 copy.31
  501.0 17.0 %all_to_all.34 = f32[128,2,2,512]{3,2,1,0:T(2,128)S(1)} all-to-all(f32[128,2,2,512]{3,2,1,0:T(2,128)S(1)} %copy.31), channel_id=1, replica_groups=mesh['cells'=128,'per'=4] {'per'}, dimensions={0} | all-to-all | bytes 2097152 | tf_op jit(solution)/shard_map/all_to_all | solution.py:37
  518.0 0.6 copy.32
  518.6 1.7 all_to_all.30
  (6 shorter events, 0.1 us)
Async XLA Ops:
  6.5 469.3 %copy-start = (f32[128,32]{0,1:T(8,128)S(1)}, f32[128,32]{0,1:T(8,128)}, u32[]{:S(2)}) copy-start(f32[128,32]{0,1:T(8,128)} %param.8) | copy-start | bytes 49156
  6.5 469.3 %all-reduce.2.cloned.1.call-start = ((), (), s32[]{:S(2)}) async-start(), calls=%async_computation.2 | async-start | bytes 131072 | tf_op jit(solution)/shard_map/psum | solution.py:32
  6.5 0.7 copy-start.2
  477.1 7.0 %copy-start.1 = (f32[128,128]{1,0:T(8,128)S(1)}, f32[128,128]{1,0:T(8,128)}, u32[]{:S(2)}) copy-start(f32[128,128]{1,0:T(8,128)} %all-reduce.2.cloned.1.call-done) | copy-start | bytes 196612
Sparse Core Ops, SparseCore 0:
  27.7 448.0 all-reduce.1
where the time goes:
time: 528 us; the launch traced here: 527 us
  waiting for transfers between devices  448 us (85%)
  blocking collectives  32.1 us (6%)
  other arithmetic  21.9 us (4%)
  between operations  13.6 us (3%)
  local copies, waits for them, and re-layouts  6.11 us (1%)
  matrix products  5.55 us (1%)
    psum x1, waiting for transfers between devices, per_device(): gram = lax.psum(local_gram, ('cells', 'per'))  448 us
    all_to_all x1, blocking collectives, per_device(): lax.all_to_all(result, 'per', split_axis=0, concat_axis=2, tiled=True)  17 us
    all_to_all x1, blocking collectives, per_device(): lax.all_to_all(scaled, 'per', split_axis=2, concat_axis=0, tiled=True)  15.1 us
    another operation x9, other arithmetic, refine(): lower = jnp.linalg.cholesky(inner)  10.8 us
  transfers between devices with their start and end apart: 1, of which 1 were waited for; matrix products, arithmetic and copies ran while one was open for 0% of the time, Pallas kernels for 0%

commit v1 on v0

v1 whole, which is shorter than its diff:
```python
import functools

import jax
import jax.numpy as jnp
from jax import lax
from jax.experimental import pallas as pl
from jax.experimental.pallas import tpu as pltpu
from jax.sharding import Mesh, PartitionSpec as P

ITERS = 3
HIGH = lax.Precision.HIGHEST
PLANE = ("y", "c", "x")
VMEM = pl.BlockSpec(memory_space=pltpu.VMEM)
ANY = pl.BlockSpec(memory_space=pl.ANY)


def dot(a, b, ca, cb):
    return lax.dot_general(
        a, b, (((ca,), (cb,)), ((), ())), precision=HIGH, preferred_element_type=jnp.float32
    )


def pack_kernel(groups, field_ref, out_ref, sems):
    width = field_ref.shape[3] // groups
    copies = [
        pltpu.make_async_copy(
            field_ref.at[:, :, :, pl.ds(g * width, width)], out_ref.at[g], sems.at[g]
        )
        for g in range(groups)
    ]
    for copy in copies:
        copy.start()
    for copy in copies:
        copy.wait()


def pack(field, groups):
    local, parts, layers, cells = field.shape
    return pl.pallas_call(
        functools.partial(pack_kernel, groups),
        out_shape=jax.ShapeDtypeStruct((groups, local, parts, layers, cells // groups), field.dtype),
        in_specs=[ANY],
        out_specs=VMEM,
        scratch_shapes=[pltpu.SemaphoreType.DMA((groups,))],
        name="pack",
    )(field)


def gram_kernel(rows_ref, out_ref):
    periods = out_ref.shape[0]
    per_period = rows_ref.shape[0] // periods
    acc = None
    for s in range(0, per_period, 2):
        block = jnp.concatenate(
            [rows_ref[pl.ds(s + t, periods, stride=per_period), :] for t in range(2)], axis=1
        )
        part = dot(block, block, 1, 1)
        acc = part if acc is None else acc + part
    out_ref[...] = acc


def gram_of(rows, periods):
    return pl.pallas_call(
        gram_kernel,
        out_shape=jax.ShapeDtypeStruct((periods, periods), jnp.float32),
        in_specs=[VMEM],
        out_specs=VMEM,
        name="gram",
    )(rows)


def inverse_factor(inner):
    rank = inner.shape[0]
    row = lax.broadcasted_iota(jnp.int32, (rank, rank), 0)
    col = lax.broadcasted_iota(jnp.int32, (rank, rank), 1)
    eye = jnp.where(row == col, 1.0, 0.0)
    work = jnp.concatenate([inner, eye], axis=1)
    sub = lax.broadcasted_iota(jnp.int32, (rank, 1), 0)
    pivots = jnp.ones((rank, 1), jnp.float32)
    for k in range(rank):
        column = work[:, k : k + 1]
        line = work[k : k + 1, :]
        pivot = line[:, k : k + 1]
        pivots = jnp.where(sub == k, pivot, pivots)
        if k + 1 < rank:
            factor = jnp.where(sub > k, column * (1.0 / pivot), 0.0)
            work = work - factor * line
    return work[:, rank:] * lax.rsqrt(pivots)


def refine_kernel(raw_ref, gain_row_ref, gain_col_ref, start_ref, group_ref, out_ref, full_ref, *, rows):
    local = out_ref.shape[0]
    gram = raw_ref[...] * (gain_col_ref[...] * gain_row_ref[...]) * (1.0 / rows)
    basis = start_ref[...]
    for _ in range(ITERS):
        grown = dot(basis, gram, 1, 0)
        basis = dot(inverse_factor(dot(grown, grown, 1, 1)), grown, 1, 0)
    full_ref[...] = dot(basis, basis, 0, 0) * gain_row_ref[...]
    out_ref[...] = full_ref[pl.ds(pl.multiple_of(group_ref[0] * local, local), local), :]


def refine(raw, gain, start_basis, group, local, rows):
    periods = raw.shape[0]
    return pl.pallas_call(
        functools.partial(refine_kernel, rows=rows),
        out_shape=jax.ShapeDtypeStruct((local, periods), jnp.float32),
        in_specs=[VMEM, VMEM, VMEM, VMEM, pl.BlockSpec(memory_space=pltpu.SMEM)],
        out_specs=VMEM,
        scratch_shapes=[pltpu.VMEM(raw.shape, jnp.float32)],
        name="refine",
    )(raw, gain[None, :], gain[:, None], start_basis.T, group[None])


def project_kernel(mix_ref, whole_ref, out_ref):
    mix = mix_ref[...]
    for layer in range(out_ref.shape[2]):
        out_ref[:, 0, layer, :] = dot(mix, whole_ref[:, 0, layer, :], 1, 0)


def project(mix, whole):
    local, periods = mix.shape
    _, parts, layers, cells = whole.shape
    width = cells // 2
    return pl.pallas_call(
        project_kernel,
        out_shape=jax.ShapeDtypeStruct((local, parts, layers, cells), jnp.float32),
        grid=(parts, cells // width),
        in_specs=[
            pl.BlockSpec((local, periods), lambda i, j: (0, 0)),
            pl.BlockSpec((periods, 1, layers, width), lambda i, j: (0, i, 0, j)),
        ],
        out_specs=pl.BlockSpec((local, 1, layers, width), lambda i, j: (0, i, 0, j)),
        name="project",
    )(mix, whole)


def spread(block, axes, count):
    copies = lax.optimization_barrier(jnp.broadcast_to(block[None], (count,) + block.shape))
    return lax.all_to_all(copies, axes, 0, 0, tiled=True)


def total(value):
    rows = value.shape[0]
    plane = lax.axis_size("y") * lax.axis_size("c") * lax.axis_size("x")
    pieces = lax.all_to_all(value.reshape(plane, rows // plane, -1), PLANE, 0, 0, tiled=True)
    piece = spread(jnp.sum(pieces, 0), "z", lax.axis_size("z"))
    return spread(jnp.sum(piece, 0), PLANE, plane).reshape(value.shape)


def per_device(field, gain, start_basis):
    groups = lax.axis_size("x")
    local, parts, layers, cells = field.shape
    periods = gain.shape[0]
    devices = lax.axis_size("y") * lax.axis_size("z") * lax.axis_size("c")
    total_rows = float(parts * layers * cells * devices)
    blocks = pack(field, groups).reshape(groups, -1, cells // groups)
    rows = lax.all_to_all(blocks, "x", 0, 0, tiled=True)
    later, rows = lax.optimization_barrier((field, rows))
    whole = lax.all_gather(later, "x", axis=0, tiled=True)
    raw = total(gram_of(rows.reshape(-1, cells // groups), periods))
    mix = refine(raw, gain, start_basis, lax.axis_index("x"), local, total_rows)
    return project(mix, whole)


def solution(mesh):
    cells, per = mesh.devices.shape
    split = Mesh(mesh.devices.reshape(4, cells // 8, 2, per), ("y", "z", "c", "x"))
    spec = P("x", None, None, ("y", "z", "c"))
    return jax.shard_map(
        per_device, mesh=split, in_specs=(spec, P(), P()), out_specs=spec, check_vma=False
    )
```

time: 528 us -> 112 us (0.21)
  waiting for transfers between devices: 448 us -> 7.21 us
  blocking collectives: 32.1 us -> 59.9 us
  Pallas kernels: 0 us -> 23.2 us
  other arithmetic: 21.9 us -> 0.07 us
  matrix products: 5.55 us -> 0 us
  starting transfers between devices: 0.01 us -> 5.31 us
    psum x1 -> x0, waiting for transfers between devices: 448 us -> none  [per_device(): gram = lax.psum(local_gram, ('cells', 'per'))]
    all_to_all x2 -> x3, blocking collectives: 32.1 us -> 59.9 us  [the longest x1 26.2 us: spread(): return lax.all_to_all(copies, axes, 0, 0, tiled=True)]
    pallas_call x0 -> x4, Pallas kernels: none -> 23.2 us  [the longest x1 11.8 us: refine(): pl.pallas_call(functools.partial(refine_kernel, rows=rows), out_shape=jax...]
    another operation x15 -> x0, other arithmetic: 20 us -> none  [the longest x9 10.8 us: refine(): lower = jnp.linalg.cholesky(inner)]
    all_to_all x0 -> x1, waiting for transfers between devices: none -> 7.19 us  [spread(): return lax.all_to_all(copies, axes, 0, 0, tiled=True)]
    all_to_all x0 -> x1, starting transfers between devices: none -> 5.3 us  [spread(): return lax.all_to_all(copies, axes, 0, 0, tiled=True)]
  transfers between devices with their start and end apart: 1 -> 2, of which waited for: 1 -> 1; matrix products, arithmetic and copies ran while one was open for 0% -> 1% of each run, Pallas kernels for 0% -> 13%
where the time goes in v1:
time: 112 us; the launch traced here: 111 us
  blocking collectives  59.9 us (53%)
  Pallas kernels  23.2 us (21%)
  between operations  13.4 us (12%)
  waiting for transfers between devices  7.21 us (6%)
  starting transfers between devices  5.31 us (5%)
  local copies, waits for them, and re-layouts  2.03 us (2%)
    all_to_all x1, blocking collectives, spread(): return lax.all_to_all(copies, axes, 0, 0, tiled=True)  26.2 us
    all_to_all x1, blocking collectives, total(): lax.all_to_all(value.reshape(plane, rows // plane, -1), PLANE, 0, 0, tile...  19 us
    all_to_all x1, blocking collectives, per_device(): rows = lax.all_to_all(blocks, 'x', 0, 0, tiled=True)  14.7 us
    pallas_call x1, Pallas kernels, refine(): pl.pallas_call(functools.partial(refine_kernel, rows=rows), out_shape=jax...  11.8 us
    all_to_all x1, waiting for transfers between devices, spread(): return lax.all_to_all(copies, axes, 0, 0, tiled=True)  7.19 us
    pallas_call x1, Pallas kernels, project(): pl.pallas_call(project_kernel, out_shape=jax.ShapeDtypeStruct((local, par...  6.18 us
    all_to_all x1, starting transfers between devices, spread(): return lax.all_to_all(copies, axes, 0, 0, tiled=True)  5.3 us
    pallas_call x1, Pallas kernels, gram_of(): pl.pallas_call(gram_kernel, out_shape=jax.ShapeDtypeStruct((periods, peri...  3.02 us
  transfers between devices with their start and end apart: 2, of which 1 were waited for; matrix products, arithmetic and copies ran while one was open for 1% of the time, Pallas kernels for 13%

profile of v1, /device:TPU:1, one launch (start us, length us, event | category | flops | bytes accessed | tf_op | source)
XLA Modules:
  0.0 111.1 jit_solution(2223420959395505998)
XLA Ops:
  6.5 0.0 copy-start.1
  6.5 0.0 all-gather.2.cloned.1.call-start
  6.5 2.2 %pack.1 = f32[4,32,2,8,128]{4,3,2,1,0:T(8,128)} custom-call(f32[32,2,8,512]{3,2,1,0:T(8,128)} %field_ref.1), custom_call_target="tpu_custom_call" | custom-call | tf_op jit(solution)/shard_map/pack/pallas_call | solution.py:39
  8.8 14.7 %all_to_all.20 = f32[4,512,128]{2,1,0:T(8,128)} all-to-all(f32[4,512,128]{2,1,0:T(8,128)} %bitcast.9), channel_id=1, replica_groups=mesh['y'=4,'z'=16,'c'=2,'x'=4] {'x'}, dimensions={0} | all-to-all | bytes 2097152 | tf_op jit(solution)/shard_map/all_to_all | solution.py:157
  23.5 0.0 all-gather.2.cloned.1.call-update
  23.5 3.0 %gram.1 = f32[128,128]{1,0:T(8,128)} custom-call(f32[2048,128]{1,0:T(8,128)} %bitcast.8), custom_call_target="tpu_custom_call" | custom-call | tf_op jit(solution)/shard_map/gram/pallas_call | solution.py:63
  26.5 19.0 %all_to_all.21 = f32[32,4,128]{2,1,0:T(4,128)S(1)} all-to-all(f32[32,4,128]{2,1,0:T(4,128)} %bitcast.10), channel_id=1, replica_groups=mesh['y'=4,'z'=16,'c'=2,'x'=4] {'y','c','x'}, dimensions={0} | all-to-all | bytes 131072 | tf_op jit(solution)/shard_map/all_to_all | solution.py:145
  45.5 26.2 %all_to_all.22 = f32[16,4,128]{2,1,0:T(4,128)S(1)} all-to-all(f32[16,4,128]{2,1,0:T(4,128)S(1)} %broadcast_in_dim.10), channel_id=1, replica_groups=mesh['y'=4,'z'=16,'c'=2,'x'=4] {'z'}, dimensions={0} | all-to-all | bytes 65536 | tf_op jit(solution)/shard_map/all_to_all | solution.py:139
  71.8 0.6 broadcast_in_dim.22
  72.4 5.3 %all-to-all-start.3 = ((f32[32,4,128]{2,1,0:T(4,128)}), f32[32,4,128]{2,1,0:T(4,128)S(1)}, u32[]{:S(2)}, u32[]{:S(2)}) async-start(f32[32,4,128]{2,1,0:T(4,128)} %broadcast_in_dim.22), calls=%async_computation.3 | async-start | bytes 131072 | tf_op jit(solution)/shard_map/all_to_all | solution.py:139
  77.7 0.0 copy-done.1
  77.7 0.7 copy.8.gain_col_ref
  78.5 7.2 %all-to-all-done.3 = f32[32,4,128]{2,1,0:T(4,128)S(1)} async-done(((f32[32,4,128]{2,1,0:T(4,128)}), f32[32,4,128]{2,1,0:T(4,128)S(1)}, u32[]{:S(2)}, u32[]{:S(2)}) %all-to-all-start.3) | async-done | bytes 65568 | tf_op jit(solution)/shard_map/all_to_all | solution.py:139
  85.7 0.0 copy-start
  85.7 0.6 copy-done
  86.3 11.8 %refine.1.mix_ref = f32[32,128]{1,0:T(8,128)} custom-call(f32[128,128]{1,0:T(8,128)} %bitcast.11, f32[1,128]{1,0:T(1,128)} %bitcast.13, f32[128,1]{1,0:T(8,128)} %copy.8.gain_col_ref, f32[32,128]{1,0:T(8,128)} %bitcast.12, s32[1]{0:T(128)} %bitcast.7.group_ref), custom_call_target="tpu_custom_call" | custom-call | tf_op jit(solution)/shard_map/refine/pallas_call | solution.py:104
  98.1 0.0 all-gather.2.cloned.1.call-done.whole_ref
  98.1 6.2 %project.1 = f32[32,2,8,512]{3,2,1,0:T(8,128)} custom-call(f32[32,128]{1,0:T(8,128)} %refine.1.mix_ref, f32[128,2,8,512]{3,2,1,0:T(8,128)} %all-gather.2.cloned.1.call-done.whole_ref), custom_call_target="tpu_custom_call" | custom-call | tf_op jit(solution)/shard_map/project/pallas_call | solution.py:124
  (3 shorter events, 0.1 us)
Async XLA Ops:
  6.5 71.2 %copy-start.1 = (f32[128]{0:T(128)S(1)}, f32[128]{0:T(128)}, u32[]{:S(2)}) copy-start(f32[128]{0:T(128)} %param.4) | copy-start | bytes 1540
  6.5 91.6 %all-gather.2.cloned.1.call-start = ((), (), s32[]{:S(2)}) async-start(), calls=%async_computation.4 | async-start | bytes 5242880 | tf_op jit(solution)/shard_map/all_gather | solution.py:159
  72.4 13.3 %all-to-all-start.3 = ((f32[32,4,128]{2,1,0:T(4,128)}), f32[32,4,128]{2,1,0:T(4,128)S(1)}, u32[]{:S(2)}, u32[]{:S(2)}) async-start(f32[32,4,128]{2,1,0:T(4,128)} %broadcast_in_dim.22), calls=%async_computation.3 | async-start | bytes 131072 | tf_op jit(solution)/shard_map/all_to_all | solution.py:139
  85.7 0.6 copy-start
Sparse Core Ops, SparseCore 0:
  23.6 65.5 all-gather.1

commit v2 on v1

v2 whole, which is shorter than its diff:
```python
import functools

import jax
import jax.numpy as jnp
from jax import lax
from jax.experimental import pallas as pl
from jax.experimental.pallas import tpu as pltpu
from jax.sharding import Mesh, PartitionSpec as P

ITERS = 3
PIVOTS = 4
HIGH = lax.Precision.HIGHEST
PLANE = ("y", "c", "x")
VMEM = pl.BlockSpec(memory_space=pltpu.VMEM)
ANY = pl.BlockSpec(memory_space=pl.ANY)


def dot(a, b, ca, cb, precision=HIGH):
    return lax.dot_general(
        a, b, (((ca,), (cb,)), ((), ())), precision=precision, preferred_element_type=jnp.float32
    )


def halves(value):
    high = value.astype(jnp.bfloat16)
    return high, (value - high.astype(jnp.float32)).astype(jnp.bfloat16)


def run_copies(copies):
    for copy in copies:
        copy.start()
    for copy in copies:
        copy.wait()


def pack_kernel(groups, field_ref, out_ref, sems):
    width = field_ref.shape[3] // groups
    run_copies([
        pltpu.make_async_copy(
            field_ref.at[:, :, :, pl.ds(g * width, width)], out_ref.at[g], sems.at[g]
        )
        for g in range(groups)
    ])


def pack(field, groups):
    local, parts, layers, cells = field.shape
    return pl.pallas_call(
        functools.partial(pack_kernel, groups),
        out_shape=jax.ShapeDtypeStruct((groups, local, parts, layers, cells // groups), field.dtype),
        in_specs=[ANY],
        out_specs=ANY,
        scratch_shapes=[pltpu.SemaphoreType.DMA((groups,))],
        name="pack",
    )(field)


def unpack_kernel(groups, blocks_ref, out_ref, sems):
    width = out_ref.shape[3] // groups
    run_copies([
        pltpu.make_async_copy(
            blocks_ref.at[g], out_ref.at[:, :, :, pl.ds(g * width, width)], sems.at[g]
        )
        for g in range(groups)
    ])


def unpack(blocks):
    groups, local, parts, layers, width = blocks.shape
    return pl.pallas_call(
        functools.partial(unpack_kernel, groups),
        out_shape=jax.ShapeDtypeStruct((local, parts, layers, groups * width), blocks.dtype),
        in_specs=[ANY],
        out_specs=ANY,
        scratch_shapes=[pltpu.SemaphoreType.DMA((groups,))],
        name="unpack",
    )(blocks)


def period_block(rows_ref, periods, s):
    per_period = rows_ref.shape[0] // periods
    return jnp.concatenate(
        [rows_ref[pl.ds(s + t, periods, stride=per_period), :] for t in range(2)], axis=1
    )


def gram_kernel(rows_ref, out_ref):
    periods = out_ref.shape[0]
    acc = None
    for s in range(0, rows_ref.shape[0] // periods, 2):
        both = jnp.concatenate(halves(period_block(rows_ref, periods, s)), axis=0)
        part = dot(both, both, 1, 1, None)
        acc = part if acc is None else acc + part
    cross = acc[:periods, periods:] + acc[periods:, :periods]
    out_ref[...] = acc[:periods, :periods] + (cross + acc[periods:, periods:])


def gram_of(rows, periods):
    return pl.pallas_call(
        gram_kernel,
        out_shape=jax.ShapeDtypeStruct((periods, periods), jnp.float32),
        in_specs=[VMEM],
        out_specs=VMEM,
        name="gram",
    )(rows)


def inverse_factor(inner):
    rank = inner.shape[0]
    row = lax.broadcasted_iota(jnp.int32, (rank, rank), 0)
    col = lax.broadcasted_iota(jnp.int32, (rank, rank), 1)
    work = jnp.concatenate([inner, jnp.where(row == col, 1.0, 0.0)], axis=1)
    shape = work.shape
    sub = lax.broadcasted_iota(jnp.int32, shape, 0)
    pivots = jnp.ones(shape, jnp.float32)
    for start in range(0, rank, PIVOTS):
        ks = range(start, start + PIVOTS)
        columns = [jnp.broadcast_to(work[:, k : k + 1], shape) for k in ks]
        lines = [work[k : k + 1, :] for k in ks]
        for j, k in enumerate(ks):
            pivot = columns[j][k : k + 1, :]
            pivots = jnp.where(sub == k, pivot, pivots)
            factor = jnp.where(sub > k, columns[j] * (1.0 / pivot), 0.0)
            for i in range(j + 1, PIVOTS):
                columns[i] = columns[i] - factor * columns[i][k : k + 1, :]
                lines[i] = lines[i] - factor[start + i : start + i + 1, :] * lines[j]
            work = work - factor * lines[j]
    return work[:, rank:] * lax.rsqrt(pivots[:, rank:])


def project_kernel(count, raw_ref, gain_ref, start_ref, rows_ref, out_ref, held, sem):
    fetch = pltpu.make_async_copy(rows_ref, held, sem)
    fetch.start()
    raw = raw_ref[...]
    gain = gain_ref[...]
    periods = raw.shape[0]

    def grow(basis):
        return dot(basis * gain, raw, 1, 0) * (gain * (1.0 / count))

    grown = grow(start_ref[...])
    for _ in range(ITERS - 1):
        later = grow(grown)
        grown = dot(inverse_factor(dot(grown, grown, 1, 1)), later, 1, 0)
    basis = dot(inverse_factor(dot(grown, grown, 1, 1)), grown, 1, 0)
    mix_high, mix_low = halves(dot(basis, basis, 0, 0) * gain)
    fetch.wait()
    per_period = held.shape[0] // periods
    width = held.shape[1]
    for s in range(0, per_period, 2):
        high, low = halves(period_block(held, periods, s))
        result = dot(mix_high, high, 1, 0, None) + (
            dot(mix_high, low, 1, 0, None) + dot(mix_low, high, 1, 0, None)
        )
        for t in range(2):
            out_ref[pl.ds(s + t, periods, stride=per_period), :] = result[:, t * width : (t + 1) * width]


def project(raw, gain, start_basis, rows, count):
    return pl.pallas_call(
        functools.partial(project_kernel, count),
        out_shape=jax.ShapeDtypeStruct(rows.shape, jnp.float32),
        in_specs=[VMEM, VMEM, VMEM, ANY],
        out_specs=VMEM,
        scratch_shapes=[pltpu.VMEM(rows.shape, jnp.float32), pltpu.SemaphoreType.DMA(())],
        name="project",
    )(raw, gain[None, :], start_basis.T, rows)


def spread(block, axes, count):
    copies = lax.optimization_barrier(jnp.broadcast_to(block[None], (count,) + block.shape))
    return lax.all_to_all(copies, axes, 0, 0, tiled=True)


def total(value):
    rows = value.shape[0]
    plane = lax.axis_size("y") * lax.axis_size("c") * lax.axis_size("x")
    pieces = lax.all_to_all(value.reshape(plane, rows // plane, -1), PLANE, 0, 0, tiled=True)
    piece = spread(jnp.sum(pieces, 0), "z", lax.axis_size("z"))
    return spread(jnp.sum(piece, 0), PLANE, plane).reshape(value.shape)


def per_device(field, gain, start_basis):
    groups = lax.axis_size("x")
    local, parts, layers, cells = field.shape
    periods = gain.shape[0]
    devices = lax.axis_size("y") * lax.axis_size("z") * lax.axis_size("c")
    count = float(parts * layers * cells * devices)
    width = cells // groups
    blocks = pack(field, groups).reshape(groups, -1, width)
    rows = lax.all_to_all(blocks, "x", 0, 0, tiled=True).reshape(-1, width)
    raw = total(gram_of(rows, periods))
    result = project(raw, gain, start_basis, rows, count).reshape(groups, -1, width)
    result = lax.all_to_all(result, "x", 0, 0, tiled=True)
    return unpack(result.reshape(groups, local, parts, layers, width))


def solution(mesh):
    cells, per = mesh.devices.shape
    split = Mesh(mesh.devices.reshape(4, cells // 8, 2, per), ("y", "z", "c", "x"))
    spec = P("x", None, None, ("y", "z", "c"))
    return jax.shard_map(
        per_device, mesh=split, in_specs=(spec, P(), P()), out_specs=spec, check_vma=False
    )
```

time: 112 us -> 169 us (1.51)
  Pallas kernels: 23.2 us -> 77 us
  blocking collectives: 59.9 us -> 91.5 us
  between operations: 13.4 us -> 0.02 us
  waiting for transfers between devices: 7.21 us -> 0 us
  starting transfers between devices: 5.31 us -> 0 us
  local copies, waits for them, and re-layouts: 2.03 us -> 0.02 us
    pallas_call x1, Pallas kernels: 2.21 us -> 32.9 us  [pack(): pl.pallas_call(functools.partial(pack_kernel, groups), out_shape=jax.Shap...]
    pallas_call x2, Pallas kernels: 18 us -> 41.6 us  [the longest x1 32.9 us: unpack(): pl.pallas_call(functools.partial(unpack_kernel, groups), out_shape=jax.Sh...]
    all_to_all x1 -> x2, blocking collectives: 14.7 us -> 33.8 us  [the longest x1 19.1 us: per_device(): result = lax.all_to_all(result, 'x', 0, 0, tiled=True)]
    all_to_all x1 -> x2, blocking collectives: 26.2 us -> 38.7 us  [spread(): return lax.all_to_all(copies, axes, 0, 0, tiled=True)]
    all_to_all x1 -> x0, waiting for transfers between devices: 7.19 us -> none  [spread(): return lax.all_to_all(copies, axes, 0, 0, tiled=True)]
    all_to_all x1 -> x0, starting transfers between devices: 5.3 us -> none  [spread(): return lax.all_to_all(copies, axes, 0, 0, tiled=True)]
  transfers between devices with their start and end apart: 2 -> 0, of which waited for: 1 -> 0; matrix products, arithmetic and copies ran while one was open for 1% -> 0% of each run, Pallas kernels for 13% -> 0%
where the time goes in v2:
time: 169 us
  blocking collectives  91.5 us (54%)
  Pallas kernels  77 us (46%)
    all_to_all x2, blocking collectives, spread(): return lax.all_to_all(copies, axes, 0, 0, tiled=True)  38.7 us
    pallas_call x1, Pallas kernels, unpack(): pl.pallas_call(functools.partial(unpack_kernel, groups), out_shape=jax.Sh...  32.9 us
    pallas_call x1, Pallas kernels, pack(): pl.pallas_call(functools.partial(pack_kernel, groups), out_shape=jax.Shap...  32.9 us
    all_to_all x1, blocking collectives, per_device(): result = lax.all_to_all(result, 'x', 0, 0, tiled=True)  19.1 us
    all_to_all x1, blocking collectives, total(): lax.all_to_all(value.reshape(plane, rows // plane, -1), PLANE, 0, 0, tile...  19 us
    all_to_all x1, blocking collectives, per_device(): rows = lax.all_to_all(blocks, 'x', 0, 0, tiled=True).reshape(-1, width)  14.7 us
    pallas_call x1, Pallas kernels, project(): pl.pallas_call(functools.partial(project_kernel, count), out_shape=jax.Sh...  8.75 us

profile of v2, /device:TPU:1, one launch (start us, length us, event | category | flops | bytes accessed | tf_op | source)
XLA Modules:
  0.0 168.6 jit_solution(270167157564779599)
XLA Ops:
  0.0 32.9 %pack.1 = f32[4,32,2,8,128]{4,3,2,1,0:T(8,128)} custom-call(f32[32,2,8,512]{3,2,1,0:T(8,128)} %field_ref.1), custom_call_target="tpu_custom_call" | custom-call | tf_op jit(solution)/shard_map/pack/pallas_call | solution.py:48
  32.9 14.7 %all_to_all.25 = f32[4,512,128]{2,1,0:T(8,128)} all-to-all(f32[4,512,128]{2,1,0:T(8,128)} %bitcast.12), channel_id=1, replica_groups=mesh['y'=4,'z'=16,'c'=2,'x'=4] {'x'}, dimensions={0} | all-to-all | bytes 2097152 | tf_op jit(solution)/shard_map/all_to_all | solution.py:191
  47.6 2.5 %gram.1 = f32[128,128]{1,0:T(8,128)} custom-call(f32[2048,128]{1,0:T(8,128)} %bitcast.8), custom_call_target="tpu_custom_call" | custom-call | tf_op jit(solution)/shard_map/gram/pallas_call | solution.py:99
  50.1 19.0 %all_to_all.26 = f32[32,4,128]{2,1,0:T(4,128)S(1)} all-to-all(f32[32,4,128]{2,1,0:T(4,128)} %bitcast.14), channel_id=1, replica_groups=mesh['y'=4,'z'=16,'c'=2,'x'=4] {'y','c','x'}, dimensions={0} | all-to-all | bytes 131072 | tf_op jit(solution)/shard_map/all_to_all | solution.py:178
  69.1 26.2 %all_to_all.27 = f32[16,4,128]{2,1,0:T(4,128)S(1)} all-to-all(f32[16,4,128]{2,1,0:T(4,128)S(1)} %broadcast_in_dim.6), channel_id=1, replica_groups=mesh['y'=4,'z'=16,'c'=2,'x'=4] {'z'}, dimensions={0} | all-to-all | bytes 65536 | tf_op jit(solution)/shard_map/all_to_all | solution.py:172
  95.4 12.5 %all_to_all.28 = f32[32,4,128]{2,1,0:T(4,128)} all-to-all(f32[32,4,128]{2,1,0:T(4,128)S(1)} %broadcast_in_dim.7), channel_id=1, replica_groups=mesh['y'=4,'z'=16,'c'=2,'x'=4] {'y','c','x'}, dimensions={0} | all-to-all | bytes 131072 | tf_op jit(solution)/shard_map/all_to_all | solution.py:172
  107.8 8.7 %project.1 = f32[2048,128]{1,0:T(8,128)} custom-call(f32[128,128]{1,0:T(8,128)} %bitcast.13, f32[1,128]{1,0:T(1,128)} %bitcast.16, f32[32,128]{1,0:T(8,128)} %bitcast.15, f32[2048,128]{1,0:T(8,128)} %bitcast.9), custom_call_target="tpu_custom_call" | custom-call | tf_op jit(solution)/shard_map/project/pallas_call | solution.py:160
  116.6 19.1 %all_to_all.29 = f32[4,512,128]{2,1,0:T(8,128)} all-to-all(f32[4,512,128]{2,1,0:T(8,128)} %bitcast.10), channel_id=1, replica_groups=mesh['y'=4,'z'=16,'c'=2,'x'=4] {'x'}, dimensions={0} | all-to-all | bytes 2097152 | tf_op jit(solution)/shard_map/all_to_all | solution.py:194
  135.7 32.9 %unpack.1 = f32[32,2,8,512]{3,2,1,0:T(8,128)} custom-call(f32[4,32,2,8,128]{4,3,2,1,0:T(8,128)} %bitcast.11), custom_call_target="tpu_custom_call" | custom-call | tf_op jit(solution)/shard_map/unpack/pallas_call | solution.py:70
  (4 shorter events, 0.1 us)

commit v3 on v2

--- a/solution.py
+++ b/solution.py
@@ -9,6 +9,7 @@
 
 ITERS = 3
 PIVOTS = 4
+LANES = 128
 HIGH = lax.Precision.HIGHEST
 PLANE = ("y", "c", "x")
 VMEM = pl.BlockSpec(memory_space=pltpu.VMEM)
@@ -49,32 +50,10 @@
         functools.partial(pack_kernel, groups),
         out_shape=jax.ShapeDtypeStruct((groups, local, parts, layers, cells // groups), field.dtype),
         in_specs=[ANY],
-        out_specs=ANY,
+        out_specs=VMEM,
         scratch_shapes=[pltpu.SemaphoreType.DMA((groups,))],
         name="pack",
     )(field)
-
-
-def unpack_kernel(groups, blocks_ref, out_ref, sems):
-    width = out_ref.shape[3] // groups
-    run_copies([
-        pltpu.make_async_copy(
-            blocks_ref.at[g], out_ref.at[:, :, :, pl.ds(g * width, width)], sems.at[g]
-        )
-        for g in range(groups)
-    ])
-
-
-def unpack(blocks):
-    groups, local, parts, layers, width = blocks.shape
-    return pl.pallas_call(
-        functools.partial(unpack_kernel, groups),
-        out_shape=jax.ShapeDtypeStruct((local, parts, layers, groups * width), blocks.dtype),
-        in_specs=[ANY],
-        out_specs=ANY,
-        scratch_shapes=[pltpu.SemaphoreType.DMA((groups,))],
-        name="unpack",
-    )(blocks)
 
 
 def period_block(rows_ref, periods, s):
@@ -128,12 +107,30 @@
     return work[:, rank:] * lax.rsqrt(pivots[:, rank:])
 
 
-def project_kernel(count, raw_ref, gain_ref, start_ref, rows_ref, out_ref, held, sem):
-    fetch = pltpu.make_async_copy(rows_ref, held, sem)
-    fetch.start()
+def project_kernel(count, raw_ref, gain_ref, start_ref, group_ref, *refs):
+    blocks, (out_ref, held, ready, full_ref, in_sems, out_sems) = refs[:-6], refs[-6:]
+    height, cells = out_ref.shape
+    lanes = held.shape[1]
+    tiles = cells // lanes
+    rows = held.shape[0] // tiles
+    fetches, at = [], 0
+    for block in blocks:
+        for c in range(tiles):
+            fetches.append(
+                pltpu.make_async_copy(
+                    block.at[:, pl.ds(c * lanes, lanes)],
+                    held.at[pl.ds(c * rows + at, block.shape[0])],
+                    in_sems.at[len(fetches)],
+                )
+            )
+        at += block.shape[0]
+    for fetch in fetches:
+        fetch.start()
     raw = raw_ref[...]
     gain = gain_ref[...]
     periods = raw.shape[0]
+    per_period = rows // periods
+    local = height // per_period
 
     def grow(basis):
         return dot(basis * gain, raw, 1, 0) * (gain * (1.0 / count))
@@ -143,28 +140,63 @@
         later = grow(grown)
         grown = dot(inverse_factor(dot(grown, grown, 1, 1)), later, 1, 0)
     basis = dot(inverse_factor(dot(grown, grown, 1, 1)), grown, 1, 0)
-    mix_high, mix_low = halves(dot(basis, basis, 0, 0) * gain)
-    fetch.wait()
-    per_period = held.shape[0] // periods
-    width = held.shape[1]
-    for s in range(0, per_period, 2):
-        high, low = halves(period_block(held, periods, s))
-        result = dot(mix_high, high, 1, 0, None) + (
-            dot(mix_high, low, 1, 0, None) + dot(mix_low, high, 1, 0, None)
-        )
-        for t in range(2):
-            out_ref[pl.ds(s + t, periods, stride=per_period), :] = result[:, t * width : (t + 1) * width]
-
-
-def project(raw, gain, start_basis, rows, count):
+    full_ref[...] = dot(basis, basis, 0, 0) * gain
+    first = group_ref[0] * local
+    own = full_ref[pl.ds(pl.multiple_of(first, local), local), :]
+    high, low = halves(pltpu.roll(own, lax.rem(periods - first, periods), 1))
+    mix = jnp.concatenate(
+        [jnp.concatenate([high, high], axis=1), jnp.concatenate([low, jnp.zeros_like(low)], axis=1)],
+        axis=0,
+    )
+    for fetch in fetches:
+        fetch.wait()
+    sends = []
+    for pair in range(0, tiles, 2):
+        for s in range(per_period):
+            line = jnp.concatenate(
+                [
+                    held[pl.ds(c * rows + s, periods, stride=per_period), :]
+                    for c in range(pair, pair + 2)
+                ],
+                axis=1,
+            )
+            result = dot(mix, jnp.concatenate(halves(line), axis=0), 1, 0, None)
+            result = result[:local] + result[local:]
+            for c in range(2):
+                ready[pl.ds((pair + c) * height + s, local, stride=per_period), :] = result[
+                    :, c * lanes : (c + 1) * lanes
+                ]
+        for c in range(pair, pair + 2):
+            sends.append(
+                pltpu.make_async_copy(
+                    ready.at[pl.ds(c * height, height)],
+                    out_ref.at[:, pl.ds(c * lanes, lanes)],
+                    out_sems.at[c],
+                )
+            )
+            sends[-1].start()
+    for send in sends:
+        send.wait()
+
+
+def project(raw, gain, start_basis, group, blocks, count):
+    rows = sum(block.shape[0] for block in blocks)
+    tiles = blocks[0].shape[1] // LANES
     return pl.pallas_call(
         functools.partial(project_kernel, count),
-        out_shape=jax.ShapeDtypeStruct(rows.shape, jnp.float32),
-        in_specs=[VMEM, VMEM, VMEM, ANY],
-        out_specs=VMEM,
-        scratch_shapes=[pltpu.VMEM(rows.shape, jnp.float32), pltpu.SemaphoreType.DMA(())],
+        out_shape=jax.ShapeDtypeStruct(blocks[0].shape, jnp.float32),
+        in_specs=[VMEM, VMEM, VMEM, pl.BlockSpec(memory_space=pltpu.SMEM)] + [ANY] * len(blocks),
+        out_specs=ANY,
+        scratch_shapes=[
+            pltpu.VMEM((tiles * rows, LANES), jnp.float32),
+            pltpu.VMEM((tiles * blocks[0].shape[0], LANES), jnp.float32),
+            pltpu.VMEM(raw.shape, jnp.float32),
+            pltpu.SemaphoreType.DMA((len(blocks) * tiles,)),
+            pltpu.SemaphoreType.DMA((tiles,)),
+        ],
+        compiler_params=pltpu.CompilerParams(vmem_limit_bytes=32 * 2**20),
         name="project",
-    )(raw, gain[None, :], start_basis.T, rows)
+    )(raw, gain[None, :], start_basis.T, group[None], *blocks)
 
 
 def spread(block, axes, count):
@@ -172,12 +204,9 @@
     return lax.all_to_all(copies, axes, 0, 0, tiled=True)
 
 
-def total(value):
-    rows = value.shape[0]
-    plane = lax.axis_size("y") * lax.axis_size("c") * lax.axis_size("x")
-    pieces = lax.all_to_all(value.reshape(plane, rows // plane, -1), PLANE, 0, 0, tiled=True)
-    piece = spread(jnp.sum(pieces, 0), "z", lax.axis_size("z"))
-    return spread(jnp.sum(piece, 0), PLANE, plane).reshape(value.shape)
+def shift(value, step):
+    count = lax.axis_size("x")
+    return lax.ppermute(value, "x", [(i, (i + step) % count) for i in range(count)])
 
 
 def per_device(field, gain, start_basis):
@@ -185,14 +214,24 @@
     local, parts, layers, cells = field.shape
     periods = gain.shape[0]
     devices = lax.axis_size("y") * lax.axis_size("z") * lax.axis_size("c")
+    plane = lax.axis_size("y") * lax.axis_size("c") * groups
     count = float(parts * layers * cells * devices)
     width = cells // groups
     blocks = pack(field, groups).reshape(groups, -1, width)
-    rows = lax.all_to_all(blocks, "x", 0, 0, tiled=True).reshape(-1, width)
-    raw = total(gram_of(rows, periods))
-    result = project(raw, gain, start_basis, rows, count).reshape(groups, -1, width)
-    result = lax.all_to_all(result, "x", 0, 0, tiled=True)
-    return unpack(result.reshape(groups, local, parts, layers, width))
+    rows = lax.all_to_all(blocks, "x", 0, 0, tiled=True)
+    own, rows = lax.optimization_barrier((field.reshape(-1, cells), rows))
+    before = shift(own, 1)
+    after = shift(own, -1)
+    gram = gram_of(rows.reshape(-1, width), periods)
+    pieces = lax.all_to_all(gram.reshape(plane, periods // plane, -1), PLANE, 0, 0, tiled=True)
+    piece = jnp.sum(spread(jnp.sum(pieces, 0), "z", lax.axis_size("z")), 0)
+    before, after, piece = lax.optimization_barrier((before, after, piece))
+    half = own.shape[0] // 2
+    opposite = [shift(before[:half], 1), shift(after[half:], -1)]
+    raw = spread(piece, PLANE, plane).reshape(gram.shape)
+    blocks = [own, after, *opposite, before]
+    result = project(raw, gain, start_basis, lax.axis_index("x"), blocks, count)
+    return result.reshape(field.shape)
 
 
 def solution(mesh):

time: 169 us -> 115 us (0.68)
  Pallas kernels: 77 us -> 13.6 us
  blocking collectives: 91.5 us -> 71.9 us
  starting transfers between devices: 0 us -> 18 us
  waiting for transfers between devices: 0 us -> 7.36 us
  local copies, waits for them, and re-layouts: 0.02 us -> 2.94 us
    pallas_call x1 -> x0, Pallas kernels: 32.9 us -> none  [unpack(): pl.pallas_call(functools.partial(unpack_kernel, groups), out_shape=jax.Sh...]
    pallas_call x1, Pallas kernels: 32.9 us -> 2.2 us  [pack(): pl.pallas_call(functools.partial(pack_kernel, groups), out_shape=jax.Shap...]
    all_to_all x2 -> x1, blocking collectives: 38.7 us -> 26.2 us  [spread(): return lax.all_to_all(copies, axes, 0, 0, tiled=True)]
    ppermute x0 -> x4, starting transfers between devices: none -> 11.8 us  [shift(): lax.ppermute(value, 'x', [(i, (i + step) % count) for i in range(count)])]
    all_to_all x0 -> x1, waiting for transfers between devices: none -> 7.35 us  [spread(): return lax.all_to_all(copies, axes, 0, 0, tiled=True)]
    all_to_all x3 -> x2, blocking collectives: 52.8 us -> 45.7 us  [the longest x1 30.9 us: per_device(): lax.all_to_all(gram.reshape(plane, periods // plane, -1), PLANE, 0, 0, ti...]
    all_to_all x0 -> x1, starting transfers between devices: none -> 6.24 us  [spread(): return lax.all_to_all(copies, axes, 0, 0, tiled=True)]
  transfers between devices with their start and end apart: 0 -> 5, of which waited for: 0 -> 1; matrix products, arithmetic and copies ran while one was open for 0% -> 1% of each run, Pallas kernels for 0% -> 2%
where the time goes in v3:
time: 115 us; the launch traced here: 114 us
  blocking collectives  71.9 us (63%)
  starting transfers between devices  18 us (16%)
  Pallas kernels  13.6 us (12%)
  waiting for transfers between devices  7.36 us (6%)
  local copies, waits for them, and re-layouts  2.94 us (3%)
    all_to_all x1, blocking collectives, per_device(): lax.all_to_all(gram.reshape(plane, periods // plane, -1), PLANE, 0, 0, ti...  30.9 us
    all_to_all x1, blocking collectives, spread(): return lax.all_to_all(copies, axes, 0, 0, tiled=True)  26.2 us
    all_to_all x1, blocking collectives, per_device(): rows = lax.all_to_all(blocks, 'x', 0, 0, tiled=True)  14.8 us
    ppermute x4, starting transfers between devices, shift(): lax.ppermute(value, 'x', [(i, (i + step) % count) for i in range(count)])  11.8 us
    pallas_call x1, Pallas kernels, project(): pl.pallas_call(functools.partial(project_kernel, count), out_shape=jax.Sh...  8.94 us
    all_to_all x1, waiting for transfers between devices, spread(): return lax.all_to_all(copies, axes, 0, 0, tiled=True)  7.35 us
    all_to_all x1, starting transfers between devices, spread(): return lax.all_to_all(copies, axes, 0, 0, tiled=True)  6.24 us
    pallas_call x1, Pallas kernels, gram_of(): pl.pallas_call(gram_kernel, out_shape=jax.ShapeDtypeStruct((periods, peri...  2.5 us
  transfers between devices with their start and end apart: 5, of which 1 were waited for; matrix products, arithmetic and copies ran while one was open for 1% of the time, Pallas kernels for 2%

profile of v3, /device:TPU:1, one launch (start us, length us, event | category | flops | bytes accessed | tf_op | source)
XLA Modules:
  0.0 114.0 jit_solution(2488070007335498691)
XLA Ops:
  0.0 2.2 %pack.1 = f32[4,32,2,8,128]{4,3,2,1,0:T(8,128)} custom-call(f32[32,2,8,512]{3,2,1,0:T(8,128)} %field_ref.1), custom_call_target="tpu_custom_call" | custom-call | tf_op jit(solution)/shard_map/pack/pallas_call | solution.py:49
  2.2 0.0 copy-start
  2.2 14.8 %all_to_all.20 = f32[4,512,128]{2,1,0:T(8,128)} all-to-all(f32[4,512,128]{2,1,0:T(8,128)} %bitcast.16), channel_id=1, replica_groups=mesh['y'=4,'z'=16,'c'=2,'x'=4] {'x'}, dimensions={0} | all-to-all | bytes 2097152 | tf_op jit(solution)/shard_map/all_to_all | solution.py:221
  17.1 0.0 copy-done
  17.1 2.8 %collective-permute-start.1 = (f32[512,512]{1,0:T(8,128)S(1)}, f32[512,512]{1,0:T(8,128)S(1)}, u32[]{:S(2)}, u32[]{:S(2)}) collective-permute-start(f32[512,512]{1,0:T(8,128)S(1)} %bitcast.9), channel_id=1, source_target_pairs={{0,3},{1,0},{2,1},{3,2},{4,7},{5,4},{6,5},{7,6},{8,11},{9,8},{10,9... | collective-permute-start | bytes 3145736 | tf_op jit(solution)/shard_map/ppermute | solution.py:209
  19.9 2.4 %collective-permute-start = (f32[512,512]{1,0:T(8,128)S(1)}, f32[512,512]{1,0:T(8,128)S(1)}, u32[]{:S(2)}, u32[]{:S(2)}) collective-permute-start(f32[512,512]{1,0:T(8,128)S(1)} %bitcast.10), channel_id=1, source_target_pairs={{0,1},{1,2},{2,3},{3,0},{4,5},{5,6},{6,7},{7,4},{8,9},{9,10},{10,1... | collective-permute-start | bytes 3145736 | tf_op jit(solution)/shard_map/ppermute | solution.py:209
  22.3 2.5 %gram.1 = f32[128,128]{1,0:T(8,128)} custom-call(f32[2048,128]{1,0:T(8,128)} %bitcast.15), custom_call_target="tpu_custom_call" | custom-call | tf_op jit(solution)/shard_map/gram/pallas_call | solution.py:78
  24.8 30.9 %all_to_all.21 = f32[32,4,128]{2,1,0:T(4,128)S(1)} all-to-all(f32[32,4,128]{2,1,0:T(4,128)} %bitcast.17), channel_id=1, replica_groups=mesh['y'=4,'z'=16,'c'=2,'x'=4] {'y','c','x'}, dimensions={0} | all-to-all | bytes 131072 | tf_op jit(solution)/shard_map/all_to_all | solution.py:226
  55.8 26.2 %all_to_all.22 = f32[16,4,128]{2,1,0:T(4,128)S(1)} all-to-all(f32[16,4,128]{2,1,0:T(4,128)S(1)} %broadcast_in_dim.8), channel_id=1, replica_groups=mesh['y'=4,'z'=16,'c'=2,'x'=4] {'z'}, dimensions={0} | all-to-all | bytes 65536 | tf_op jit(solution)/shard_map/all_to_all | solution.py:204
  82.0 0.0 collective-permute-done.1.refs_1_
  82.0 0.0 collective-permute-done.refs_4_
  82.0 0.8 slice.7
  82.8 0.8 slice.6
  83.7 1.9 %collective-permute-start.2 = (f32[256,512]{1,0:T(8,128)}, f32[256,512]{1,0:T(8,128)}, u32[]{:S(2)}, u32[]{:S(2)}) collective-permute-start(f32[256,512]{1,0:T(8,128)} %slice.6), channel_id=1, source_target_pairs={{0,1},{1,2},{2,3},{3,0},{4,5},{5,6},{6,7},{7,4},{8,9},{9,10},{10,1... | collective-permute-start | bytes 1572872 | tf_op jit(solution)/shard_map/ppermute | solution.py:209
  85.6 4.6 %collective-permute-start.3 = (f32[256,512]{1,0:T(8,128)}, f32[256,512]{1,0:T(8,128)}, u32[]{:S(2)}, u32[]{:S(2)}) collective-permute-start(f32[256,512]{1,0:T(8,128)} %slice.7), channel_id=1, source_target_pairs={{0,3},{1,0},{2,1},{3,2},{4,7},{5,4},{6,5},{7,6},{8,11},{9,8},{10,9... | collective-permute-start | bytes 1572872 | tf_op jit(solution)/shard_map/ppermute | solution.py:209
  90.2 0.6 broadcast_in_dim.9
  90.8 0.0 copy-start.1
  90.8 6.2 %all-to-all-start.3 = ((f32[32,4,128]{2,1,0:T(4,128)}), f32[32,4,128]{2,1,0:T(4,128)S(1)}, u32[]{:S(2)}, u32[]{:S(2)}) async-start(f32[32,4,128]{2,1,0:T(4,128)} %broadcast_in_dim.9), calls=%async_computation.3 | async-start | bytes 131072 | tf_op jit(solution)/shard_map/all_to_all | solution.py:204
  97.0 7.4 %all-to-all-done.3 = f32[32,4,128]{2,1,0:T(4,128)S(1)} async-done(((f32[32,4,128]{2,1,0:T(4,128)}), f32[32,4,128]{2,1,0:T(4,128)S(1)}, u32[]{:S(2)}, u32[]{:S(2)}) %all-to-all-start.3) | async-done | bytes 65568 | tf_op jit(solution)/shard_map/all_to_all | solution.py:204
  104.4 0.0 collective-permute-done.2.refs_2_
  104.4 0.0 collective-permute-done.3.refs_3_
  104.4 0.0 copy-start.2
  104.4 0.0 copy-done.1
  104.4 0.6 copy-done.2
  105.1 8.9 %project.1 = f32[512,512]{1,0:T(8,128)} custom-call(f32[128,128]{1,0:T(8,128)S(1)} %bitcast.12, f32[1,128]{1,0:T(1,128)S(1)} %bitcast.14, f32[32,128]{1,0:T(8,128)S(1)} %bitcast.13, s32[1]{0:T(128)} %bitcast.7.group_ref, f32[512,512]{1,0:T(8,128)S(1)} %bitcast.11, f32[512,512]{1,0:T(8,128)S(1)} %collective-permute-done.1.refs_1_, ...), custom_call_target="tpu_custom_call" | custom-call | tf_op jit(solution)/shard_map/project/pallas_call | solution.py:185
  (3 shorter events, 0.1 us)
Async XLA Ops:
  2.2 14.8 %copy-start = (f32[32,2,8,512]{3,2,1,0:T(8,128)S(1)}, f32[32,2,8,512]{3,2,1,0:T(8,128)}, u32[]{:S(2)}) copy-start(f32[32,2,8,512]{3,2,1,0:T(8,128)} %field_ref.1) | copy-start | bytes 3145732
  17.1 64.9 %collective-permute-start.1 = (f32[512,512]{1,0:T(8,128)S(1)}, f32[512,512]{1,0:T(8,128)S(1)}, u32[]{:S(2)}, u32[]{:S(2)}) collective-permute-start(f32[512,512]{1,0:T(8,128)S(1)} %bitcast.9), channel_id=1, source_target_pairs={{0,3},{1,0},{2,1},{3,2},{4,7},{5,4},{6,5},{7,6},{8,11},{9,8},{10,9... | collective-permute-start | bytes 3145736 | tf_op jit(solution)/shard_map/ppermute | solution.py:209
  19.9 62.1 %collective-permute-start = (f32[512,512]{1,0:T(8,128)S(1)}, f32[512,512]{1,0:T(8,128)S(1)}, u32[]{:S(2)}, u32[]{:S(2)}) collective-permute-start(f32[512,512]{1,0:T(8,128)S(1)} %bitcast.10), channel_id=1, source_target_pairs={{0,1},{1,2},{2,3},{3,0},{4,5},{5,6},{6,7},{7,4},{8,9},{9,10},{10,1... | collective-permute-start | bytes 3145736 | tf_op jit(solution)/shard_map/ppermute | solution.py:209
  83.7 20.7 %collective-permute-start.2 = (f32[256,512]{1,0:T(8,128)}, f32[256,512]{1,0:T(8,128)}, u32[]{:S(2)}, u32[]{:S(2)}) collective-permute-start(f32[256,512]{1,0:T(8,128)} %slice.6), channel_id=1, source_target_pairs={{0,1},{1,2},{2,3},{3,0},{4,5},{5,6},{6,7},{7,4},{8,9},{9,10},{10,1... | collective-permute-start | bytes 1572872 | tf_op jit(solution)/shard_map/ppermute | solution.py:209
  85.6 18.8 %collective-permute-start.3 = (f32[256,512]{1,0:T(8,128)}, f32[256,512]{1,0:T(8,128)}, u32[]{:S(2)}, u32[]{:S(2)}) collective-permute-start(f32[256,512]{1,0:T(8,128)} %slice.7), channel_id=1, source_target_pairs={{0,3},{1,0},{2,1},{3,2},{4,7},{5,4},{6,5},{7,6},{8,11},{9,8},{10,9... | collective-permute-start | bytes 1572872 | tf_op jit(solution)/shard_map/ppermute | solution.py:209
  90.8 13.6 %copy-start.1 = (f32[128,32]{0,1:T(8,128)S(1)}, f32[128,32]{0,1:T(8,128)}, u32[]{:S(2)}) copy-start(f32[128,32]{0,1:T(8,128)} %param.5) | copy-start | bytes 49156
  90.8 13.6 %all-to-all-start.3 = ((f32[32,4,128]{2,1,0:T(4,128)}), f32[32,4,128]{2,1,0:T(4,128)S(1)}, u32[]{:S(2)}, u32[]{:S(2)}) async-start(f32[32,4,128]{2,1,0:T(4,128)} %broadcast_in_dim.9), calls=%async_computation.3 | async-start | bytes 131072 | tf_op jit(solution)/shard_map/all_to_all | solution.py:204
  104.4 0.7 copy-start.2

commit v4 on v3

--- a/solution.py
+++ b/solution.py
@@ -11,7 +11,7 @@
 PIVOTS = 4
 LANES = 128
 HIGH = lax.Precision.HIGHEST
-PLANE = ("y", "c", "x")
+PAIRS = ("y", "c")
 VMEM = pl.BlockSpec(memory_space=pltpu.VMEM)
 ANY = pl.BlockSpec(memory_space=pl.ANY)
 
@@ -126,9 +126,9 @@
         at += block.shape[0]
     for fetch in fetches:
         fetch.start()
-    raw = raw_ref[...]
+    periods = raw_ref.shape[1]
+    raw = sum(raw_ref[pl.ds(at, periods), :] for at in range(0, raw_ref.shape[0], periods))
     gain = gain_ref[...]
-    periods = raw.shape[0]
     per_period = rows // periods
     local = height // per_period
 
@@ -190,7 +190,7 @@
         scratch_shapes=[
             pltpu.VMEM((tiles * rows, LANES), jnp.float32),
             pltpu.VMEM((tiles * blocks[0].shape[0], LANES), jnp.float32),
-            pltpu.VMEM(raw.shape, jnp.float32),
+            pltpu.VMEM((raw.shape[1], raw.shape[1]), jnp.float32),
             pltpu.SemaphoreType.DMA((len(blocks) * tiles,)),
             pltpu.SemaphoreType.DMA((tiles,)),
         ],
@@ -214,7 +214,7 @@
     local, parts, layers, cells = field.shape
     periods = gain.shape[0]
     devices = lax.axis_size("y") * lax.axis_size("z") * lax.axis_size("c")
-    plane = lax.axis_size("y") * lax.axis_size("c") * groups
+    pairs = lax.axis_size("y") * lax.axis_size("c")
     count = float(parts * layers * cells * devices)
     width = cells // groups
     blocks = pack(field, groups).reshape(groups, -1, width)
@@ -223,12 +223,11 @@
     before = shift(own, 1)
     after = shift(own, -1)
     gram = gram_of(rows.reshape(-1, width), periods)
-    pieces = lax.all_to_all(gram.reshape(plane, periods // plane, -1), PLANE, 0, 0, tiled=True)
+    pieces = lax.all_to_all(gram.reshape(pairs, periods // pairs, -1), PAIRS, 0, 0, tiled=True)
     piece = jnp.sum(spread(jnp.sum(pieces, 0), "z", lax.axis_size("z")), 0)
-    before, after, piece = lax.optimization_barrier((before, after, piece))
     half = own.shape[0] // 2
     opposite = [shift(before[:half], 1), shift(after[half:], -1)]
-    raw = spread(piece, PLANE, plane).reshape(gram.shape)
+    raw = spread(piece, ("x",) + PAIRS, groups * pairs).reshape(-1, periods)
     blocks = [own, after, *opposite, before]
     result = project(raw, gain, start_basis, lax.axis_index("x"), blocks, count)
     return result.reshape(field.shape)

time: 115 us -> 97.5 us (0.85)
  blocking collectives: 71.9 us -> 32.4 us
  starting transfers between devices: 18 us -> 34 us
  waiting for transfers between devices: 7.36 us -> 12.9 us
    all_to_all x2 -> x1, blocking collectives: 57.1 us -> 17.6 us  [per_device(): lax.all_to_all(gram.reshape(pairs, periods // pairs, -1), PAIRS, 0, 0, ti...]
    all_to_all x1 -> x2, starting transfers between devices: 6.24 us -> 21.1 us  [spread(): return lax.all_to_all(copies, axes, 0, 0, tiled=True)]
    all_to_all x1 -> x2, waiting for transfers between devices: 7.35 us -> 12.9 us  [spread(): return lax.all_to_all(copies, axes, 0, 0, tiled=True)]
    ppermute x4, starting transfers between devices: 11.8 us -> 13 us  [shift(): lax.ppermute(value, 'x', [(i, (i + step) % count) for i in range(count)])]
  transfers between devices with their start and end apart: 5 -> 6, of which waited for: 1 -> 2; matrix products, arithmetic and copies ran while one was open for 1% -> 3% of each run, Pallas kernels for 2% -> 3%
where the time goes in v4:
time: 97.5 us; the launch traced here: 96.9 us
  starting transfers between devices  34 us (35%)
  blocking collectives  32.4 us (33%)
  Pallas kernels  13.6 us (14%)
  waiting for transfers between devices  12.9 us (13%)
  local copies, waits for them, and re-layouts  3.7 us (4%)
    all_to_all x2, starting transfers between devices, spread(): return lax.all_to_all(copies, axes, 0, 0, tiled=True)  21.1 us
    all_to_all x1, blocking collectives, per_device(): lax.all_to_all(gram.reshape(pairs, periods // pairs, -1), PAIRS, 0, 0, ti...  17.6 us
    all_to_all x1, blocking collectives, per_device(): rows = lax.all_to_all(blocks, 'x', 0, 0, tiled=True)  14.8 us
    ppermute x4, starting transfers between devices, shift(): lax.ppermute(value, 'x', [(i, (i + step) % count) for i in range(count)])  13 us
    all_to_all x2, waiting for transfers between devices, spread(): return lax.all_to_all(copies, axes, 0, 0, tiled=True)  12.9 us
    pallas_call x1, Pallas kernels, project(): pl.pallas_call(functools.partial(project_kernel, count), out_shape=jax.Sh...  8.94 us
    pallas_call x1, Pallas kernels, gram_of(): pl.pallas_call(gram_kernel, out_shape=jax.ShapeDtypeStruct((periods, peri...  2.49 us
    pallas_call x1, Pallas kernels, pack(): pl.pallas_call(functools.partial(pack_kernel, groups), out_shape=jax.Shap...  2.2 us
  transfers between devices with their start and end apart: 6, of which 2 were waited for; matrix products, arithmetic and copies ran while one was open for 3% of the time, Pallas kernels for 3%

profile of v4, /device:TPU:1, one launch (start us, length us, event | category | flops | bytes accessed | tf_op | source)
XLA Modules:
  0.0 96.9 jit_solution(12230024678331917951)
XLA Ops:
  0.0 2.2 %pack.1 = f32[4,32,2,8,128]{4,3,2,1,0:T(8,128)} custom-call(f32[32,2,8,512]{3,2,1,0:T(8,128)} %field_ref.1), custom_call_target="tpu_custom_call" | custom-call | tf_op jit(solution)/shard_map/pack/pallas_call | solution.py:49
  2.2 0.0 copy-start
  2.2 14.8 %all_to_all.20 = f32[4,512,128]{2,1,0:T(8,128)} all-to-all(f32[4,512,128]{2,1,0:T(8,128)} %bitcast.16), channel_id=1, replica_groups=mesh['y'=4,'z'=16,'c'=2,'x'=4] {'x'}, dimensions={0} | all-to-all | bytes 2097152 | tf_op jit(solution)/shard_map/all_to_all | solution.py:221
  17.1 0.0 copy-done
  17.1 2.2 %collective-permute-start.1 = (f32[512,512]{1,0:T(8,128)S(1)}, f32[512,512]{1,0:T(8,128)S(1)}, u32[]{:S(2)}, u32[]{:S(2)}) collective-permute-start(f32[512,512]{1,0:T(8,128)S(1)} %bitcast.9), channel_id=1, source_target_pairs={{0,1},{1,2},{2,3},{3,0},{4,5},{5,6},{6,7},{7,4},{8,9},{9,10},{10,1... | collective-permute-start | bytes 3145736 | tf_op jit(solution)/shard_map/ppermute | solution.py:209
  19.3 4.3 %collective-permute-start = (f32[512,512]{1,0:T(8,128)S(1)}, f32[512,512]{1,0:T(8,128)S(1)}, u32[]{:S(2)}, u32[]{:S(2)}) collective-permute-start(f32[512,512]{1,0:T(8,128)S(1)} %bitcast.10), channel_id=1, source_target_pairs={{0,3},{1,0},{2,1},{3,2},{4,7},{5,4},{6,5},{7,6},{8,11},{9,8},{10,9... | collective-permute-start | bytes 3145736 | tf_op jit(solution)/shard_map/ppermute | solution.py:209
  23.6 2.5 %gram.1 = f32[128,128]{1,0:T(8,128)} custom-call(f32[2048,128]{1,0:T(8,128)} %bitcast.15), custom_call_target="tpu_custom_call" | custom-call | tf_op jit(solution)/shard_map/gram/pallas_call | solution.py:78
  26.0 17.6 %all_to_all.21 = f32[8,16,128]{2,1,0:T(8,128)S(1)} all-to-all(f32[8,16,128]{2,1,0:T(8,128)} %bitcast.17), channel_id=1, replica_groups=mesh['y'=4,'z'=16,'c'=2,'x'=4] {'y','c'}, dimensions={0} | all-to-all | bytes 131072 | tf_op jit(solution)/shard_map/all_to_all | solution.py:226
  43.7 0.7 broadcast_in_dim.8
  44.3 13.7 %all-to-all-start.2 = ((f32[16,16,128]{2,1,0:T(8,128)}), f32[16,16,128]{2,1,0:T(8,128)S(1)}, u32[]{:S(2)}, u32[]{:S(2)}) async-start(f32[16,16,128]{2,1,0:T(8,128)} %broadcast_in_dim.8), calls=%async_computation.2 | async-start | bytes 262144 | tf_op jit(solution)/shard_map/all_to_all | solution.py:204
  58.0 0.0 collective-permute-done.1.refs_4_
  58.0 0.8 slice.8
  58.9 1.9 %collective-permute-start.2 = (f32[256,512]{1,0:T(8,128)}, f32[256,512]{1,0:T(8,128)}, u32[]{:S(2)}, u32[]{:S(2)}) collective-permute-start(f32[256,512]{1,0:T(8,128)} %slice.8), channel_id=1, source_target_pairs={{0,1},{1,2},{2,3},{3,0},{4,5},{5,6},{6,7},{7,4},{8,9},{9,10},{10,1... | collective-permute-start | bytes 1572872 | tf_op jit(solution)/shard_map/ppermute | solution.py:209
  60.8 0.0 collective-permute-done.refs_1_
  60.8 0.8 slice.9
  61.6 4.6 %collective-permute-start.3 = (f32[256,512]{1,0:T(8,128)}, f32[256,512]{1,0:T(8,128)}, u32[]{:S(2)}, u32[]{:S(2)}) collective-permute-start(f32[256,512]{1,0:T(8,128)} %slice.9), channel_id=1, source_target_pairs={{0,3},{1,0},{2,1},{3,2},{4,7},{5,4},{6,5},{7,6},{8,11},{9,8},{10,9... | collective-permute-start | bytes 1572872 | tf_op jit(solution)/shard_map/ppermute | solution.py:209
  66.2 3.8 %all-to-all-done.2 = f32[16,16,128]{2,1,0:T(8,128)S(1)} async-done(((f32[16,16,128]{2,1,0:T(8,128)}), f32[16,16,128]{2,1,0:T(8,128)S(1)}, u32[]{:S(2)}, u32[]{:S(2)}) %all-to-all-start.2) | async-done | bytes 131104 | tf_op jit(solution)/shard_map/all_to_all | solution.py:204
  70.0 0.7 broadcast_in_dim.9
  70.7 0.0 copy-start.1
  70.7 7.4 %all-to-all-start.3 = ((f32[32,16,128]{2,1,0:T(8,128)}), f32[32,16,128]{2,1,0:T(8,128)S(1)}, u32[]{:S(2)}, u32[]{:S(2)}) async-start(f32[32,16,128]{2,1,0:T(8,128)} %broadcast_in_dim.9), calls=%async_computation.3 | async-start | bytes 524288 | tf_op jit(solution)/shard_map/all_to_all | solution.py:204
  78.2 9.1 %all-to-all-done.3 = f32[32,16,128]{2,1,0:T(8,128)S(1)} async-done(((f32[32,16,128]{2,1,0:T(8,128)}), f32[32,16,128]{2,1,0:T(8,128)S(1)}, u32[]{:S(2)}, u32[]{:S(2)}) %all-to-all-start.3) | async-done | bytes 262176 | tf_op jit(solution)/shard_map/all_to_all | solution.py:204
  87.2 0.0 collective-permute-done.2.refs_2_
  87.3 0.0 collective-permute-done.3.refs_3_
  87.3 0.0 copy-start.2
  87.3 0.0 copy-done.1
  87.3 0.6 copy-done.2
  87.9 8.9 %project.1 = f32[512,512]{1,0:T(8,128)} custom-call(f32[512,128]{1,0:T(8,128)S(1)} %bitcast.12, f32[1,128]{1,0:T(1,128)S(1)} %bitcast.14, f32[32,128]{1,0:T(8,128)S(1)} %bitcast.13, s32[1]{0:T(128)} %bitcast.7.group_ref, f32[512,512]{1,0:T(8,128)S(1)} %bitcast.11, f32[512,512]{1,0:T(8,128)S(1)} %collective-permute-done.refs_1_, ...), custom_call_target="tpu_custom_call" | custom-call | tf_op jit(solution)/shard_map/project/pallas_call | solution.py:185
  (2 shorter events, 0.0 us)
Async XLA Ops:
  2.2 14.8 %copy-start = (f32[32,2,8,512]{3,2,1,0:T(8,128)S(1)}, f32[32,2,8,512]{3,2,1,0:T(8,128)}, u32[]{:S(2)}) copy-start(f32[32,2,8,512]{3,2,1,0:T(8,128)} %field_ref.1) | copy-start | bytes 3145732
  17.1 41.0 %collective-permute-start.1 = (f32[512,512]{1,0:T(8,128)S(1)}, f32[512,512]{1,0:T(8,128)S(1)}, u32[]{:S(2)}, u32[]{:S(2)}) collective-permute-start(f32[512,512]{1,0:T(8,128)S(1)} %bitcast.9), channel_id=1, source_target_pairs={{0,1},{1,2},{2,3},{3,0},{4,5},{5,6},{6,7},{7,4},{8,9},{9,10},{10,1... | collective-permute-start | bytes 3145736 | tf_op jit(solution)/shard_map/ppermute | solution.py:209
  19.3 41.5 %collective-permute-start = (f32[512,512]{1,0:T(8,128)S(1)}, f32[512,512]{1,0:T(8,128)S(1)}, u32[]{:S(2)}, u32[]{:S(2)}) collective-permute-start(f32[512,512]{1,0:T(8,128)S(1)} %bitcast.10), channel_id=1, source_target_pairs={{0,3},{1,0},{2,1},{3,2},{4,7},{5,4},{6,5},{7,6},{8,11},{9,8},{10,9... | collective-permute-start | bytes 3145736 | tf_op jit(solution)/shard_map/ppermute | solution.py:209
  44.3 25.7 %all-to-all-start.2 = ((f32[16,16,128]{2,1,0:T(8,128)}), f32[16,16,128]{2,1,0:T(8,128)S(1)}, u32[]{:S(2)}, u32[]{:S(2)}) async-start(f32[16,16,128]{2,1,0:T(8,128)} %broadcast_in_dim.8), calls=%async_computation.2 | async-start | bytes 262144 | tf_op jit(solution)/shard_map/all_to_all | solution.py:204
  58.9 28.4 %collective-permute-start.2 = (f32[256,512]{1,0:T(8,128)}, f32[256,512]{1,0:T(8,128)}, u32[]{:S(2)}, u32[]{:S(2)}) collective-permute-start(f32[256,512]{1,0:T(8,128)} %slice.8), channel_id=1, source_target_pairs={{0,1},{1,2},{2,3},{3,0},{4,5},{5,6},{6,7},{7,4},{8,9},{9,10},{10,1... | collective-permute-start | bytes 1572872 | tf_op jit(solution)/shard_map/ppermute | solution.py:209
  61.6 25.6 %collective-permute-start.3 = (f32[256,512]{1,0:T(8,128)}, f32[256,512]{1,0:T(8,128)}, u32[]{:S(2)}, u32[]{:S(2)}) collective-permute-start(f32[256,512]{1,0:T(8,128)} %slice.9), channel_id=1, source_target_pairs={{0,3},{1,0},{2,1},{3,2},{4,7},{5,4},{6,5},{7,6},{8,11},{9,8},{10,9... | collective-permute-start | bytes 1572872 | tf_op jit(solution)/shard_map/ppermute | solution.py:209
  70.7 16.5 %copy-start.1 = (f32[128,32]{0,1:T(8,128)S(1)}, f32[128,32]{0,1:T(8,128)}, u32[]{:S(2)}) copy-start(f32[128,32]{0,1:T(8,128)} %param.5) | copy-start | bytes 49156
  70.7 16.5 %all-to-all-start.3 = ((f32[32,16,128]{2,1,0:T(8,128)}), f32[32,16,128]{2,1,0:T(8,128)S(1)}, u32[]{:S(2)}, u32[]{:S(2)}) async-start(f32[32,16,128]{2,1,0:T(8,128)} %broadcast_in_dim.9), calls=%async_computation.3 | async-start | bytes 524288 | tf_op jit(solution)/shard_map/all_to_all | solution.py:204
  87.3 0.7 copy-start.2

commit v5 on v4

--- a/solution.py
+++ b/solution.py
@@ -10,10 +10,12 @@
 ITERS = 3
 PIVOTS = 4
 LANES = 128
+EXTRA = 8
 HIGH = lax.Precision.HIGHEST
 PAIRS = ("y", "c")
 VMEM = pl.BlockSpec(memory_space=pltpu.VMEM)
 ANY = pl.BlockSpec(memory_space=pl.ANY)
+LONG = pl.CostEstimate(flops=4 * 10**10, bytes_accessed=0, transcendentals=0)
 
 
 def dot(a, b, ca, cb, precision=HIGH):
@@ -56,6 +58,10 @@
     )(field)
 
 
+def positions(shape):
+    return lax.broadcasted_iota(jnp.int32, shape, 0), lax.broadcasted_iota(jnp.int32, shape, 1)
+
+
 def period_block(rows_ref, periods, s):
     per_period = rows_ref.shape[0] // periods
     return jnp.concatenate(
@@ -64,20 +70,40 @@
 
 
 def gram_kernel(rows_ref, out_ref):
-    periods = out_ref.shape[0]
+    periods = out_ref.shape[1]
     acc = None
     for s in range(0, rows_ref.shape[0] // periods, 2):
         both = jnp.concatenate(halves(period_block(rows_ref, periods, s)), axis=0)
         part = dot(both, both, 1, 1, None)
         acc = part if acc is None else acc + part
     cross = acc[:periods, periods:] + acc[periods:, :periods]
-    out_ref[...] = acc[:periods, :periods] + (cross + acc[periods:, periods:])
+    gram = acc[:periods, :periods] + (cross + acc[periods:, periods:])
+    half = periods // 2
+    low = gram[half:]
+    row, lane = positions(low.shape)
+    folded = jnp.where(row >= lane - half, pltpu.roll(gram[:half], half, 1), low)
+    out_ref[:half] = jnp.where(lane < half, low, folded)
+    corner = jnp.sum(jnp.where(row == lane - half, low, 0.0), axis=0, keepdims=True)
+    out_ref[half:] = jnp.broadcast_to(corner, (EXTRA, periods))
+
+
+def unfold(packed):
+    periods = packed.shape[1]
+    half = periods // 2
+    body = packed[:half]
+    row, lane = positions(body.shape)
+    high = jnp.where(row >= lane, pltpu.roll(body, half, 1), 0.0)
+    high = jnp.where(lane < half, high, 0.0) * jnp.where(row == lane, 0.5, 1.0)
+    low = jnp.where((lane < half) | (row < lane - half), body, 0.0)
+    low = jnp.where(row == lane - half, 0.5 * packed[half : half + 1], low)
+    triangle = jnp.concatenate([high, low], axis=0)
+    return triangle + triangle.T
 
 
 def gram_of(rows, periods):
     return pl.pallas_call(
         gram_kernel,
-        out_shape=jax.ShapeDtypeStruct((periods, periods), jnp.float32),
+        out_shape=jax.ShapeDtypeStruct((periods // 2 + EXTRA, periods), jnp.float32),
         in_specs=[VMEM],
         out_specs=VMEM,
         name="gram",
@@ -107,30 +133,12 @@
     return work[:, rank:] * lax.rsqrt(pivots[:, rank:])
 
 
-def project_kernel(count, raw_ref, gain_ref, start_ref, group_ref, *refs):
-    blocks, (out_ref, held, ready, full_ref, in_sems, out_sems) = refs[:-6], refs[-6:]
-    height, cells = out_ref.shape
-    lanes = held.shape[1]
-    tiles = cells // lanes
-    rows = held.shape[0] // tiles
-    fetches, at = [], 0
-    for block in blocks:
-        for c in range(tiles):
-            fetches.append(
-                pltpu.make_async_copy(
-                    block.at[:, pl.ds(c * lanes, lanes)],
-                    held.at[pl.ds(c * rows + at, block.shape[0])],
-                    in_sems.at[len(fetches)],
-                )
-            )
-        at += block.shape[0]
-    for fetch in fetches:
-        fetch.start()
+def refine_kernel(count, raw_ref, gain_ref, start_ref, group_ref, out_ref, full_ref):
     periods = raw_ref.shape[1]
-    raw = sum(raw_ref[pl.ds(at, periods), :] for at in range(0, raw_ref.shape[0], periods))
+    local = out_ref.shape[0]
+    size = periods // 2 + EXTRA
+    raw = unfold(sum(raw_ref[pl.ds(at, size), :] for at in range(0, raw_ref.shape[0], size)))
     gain = gain_ref[...]
-    per_period = rows // periods
-    local = height // per_period
 
     def grow(basis):
         return dot(basis * gain, raw, 1, 0) * (gain * (1.0 / count))
@@ -143,15 +151,53 @@
     full_ref[...] = dot(basis, basis, 0, 0) * gain
     first = group_ref[0] * local
     own = full_ref[pl.ds(pl.multiple_of(first, local), local), :]
-    high, low = halves(pltpu.roll(own, lax.rem(periods - first, periods), 1))
+    out_ref[...] = pltpu.roll(own, lax.rem(periods - first, periods), 1)
+
+
+def refine(raw, gain, start_basis, group, local, count):
+    periods = gain.shape[0]
+    return pl.pallas_call(
+        functools.partial(refine_kernel, count),
+        out_shape=jax.ShapeDtypeStruct((local, periods), jnp.float32),
+        in_specs=[VMEM, VMEM, VMEM, pl.BlockSpec(memory_space=pltpu.SMEM)],
+        out_specs=VMEM,
+        scratch_shapes=[pltpu.VMEM((periods, periods), jnp.float32)],
+        cost_estimate=LONG,
+        name="refine",
+    )(raw, gain[None, :], start_basis.T, group[None])
+
+
+def project_kernel(mix_ref, *refs):
+    blocks, (out_ref, held, ready, in_sems, out_sems) = refs[:-5], refs[-5:]
+    height, cells = out_ref.shape
+    lanes = held.shape[1]
+    tiles = cells // lanes
+    rows = held.shape[0] // tiles
+    fetches = []
+    for c in range(tiles):
+        at = 0
+        for block in blocks:
+            fetches.append(
+                pltpu.make_async_copy(
+                    block.at[:, pl.ds(c * lanes, lanes)],
+                    held.at[pl.ds(c * rows + at, block.shape[0])],
+                    in_sems.at[len(fetches)],
+                )
+            )
+            at += block.shape[0]
+    for fetch in fetches:
+        fetch.start()
+    local, periods = mix_ref.shape
+    per_period = rows // periods
+    high, low = halves(mix_ref[...])
     mix = jnp.concatenate(
         [jnp.concatenate([high, high], axis=1), jnp.concatenate([low, jnp.zeros_like(low)], axis=1)],
         axis=0,
     )
-    for fetch in fetches:
-        fetch.wait()
     sends = []
     for pair in range(0, tiles, 2):
+        for fetch in fetches[pair * len(blocks) : (pair + 2) * len(blocks)]:
+            fetch.wait()
         for s in range(per_period):
             line = jnp.concatenate(
                 [
@@ -179,29 +225,42 @@
         send.wait()
 
 
-def project(raw, gain, start_basis, group, blocks, count):
+def project(mix, blocks):
     rows = sum(block.shape[0] for block in blocks)
     tiles = blocks[0].shape[1] // LANES
     return pl.pallas_call(
-        functools.partial(project_kernel, count),
+        project_kernel,
         out_shape=jax.ShapeDtypeStruct(blocks[0].shape, jnp.float32),
-        in_specs=[VMEM, VMEM, VMEM, pl.BlockSpec(memory_space=pltpu.SMEM)] + [ANY] * len(blocks),
+        in_specs=[VMEM] + [ANY] * len(blocks),
         out_specs=ANY,
         scratch_shapes=[
             pltpu.VMEM((tiles * rows, LANES), jnp.float32),
             pltpu.VMEM((tiles * blocks[0].shape[0], LANES), jnp.float32),
-            pltpu.VMEM((raw.shape[1], raw.shape[1]), jnp.float32),
             pltpu.SemaphoreType.DMA((len(blocks) * tiles,)),
             pltpu.SemaphoreType.DMA((tiles,)),
         ],
         compiler_params=pltpu.CompilerParams(vmem_limit_bytes=32 * 2**20),
         name="project",
-    )(raw, gain[None, :], start_basis.T, group[None], *blocks)
-
-
-def spread(block, axes, count):
-    copies = lax.optimization_barrier(jnp.broadcast_to(block[None], (count,) + block.shape))
-    return lax.all_to_all(copies, axes, 0, 0, tiled=True)
+    )(mix, *blocks)
+
+
+def sum_kernel(pieces_ref, out_ref):
+    piece = pieces_ref[0]
+    for i in range(1, pieces_ref.shape[0]):
+        piece = piece + pieces_ref[i]
+    for i in range(out_ref.shape[0]):
+        out_ref[i] = piece
+
+
+def sum_and_copy(pieces, copies, cost):
+    return pl.pallas_call(
+        sum_kernel,
+        out_shape=jax.ShapeDtypeStruct((copies,) + pieces.shape[1:], jnp.float32),
+        in_specs=[VMEM],
+        out_specs=VMEM,
+        cost_estimate=cost,
+        name="sum_and_copy",
+    )(pieces)
 
 
 def shift(value, step):
@@ -219,18 +278,20 @@
     width = cells // groups
     blocks = pack(field, groups).reshape(groups, -1, width)
     rows = lax.all_to_all(blocks, "x", 0, 0, tiled=True)
-    own, rows = lax.optimization_barrier((field.reshape(-1, cells), rows))
+    gram = gram_of(rows.reshape(-1, width), periods)
+    own, gram = lax.optimization_barrier((field.reshape(-1, cells), gram))
     before = shift(own, 1)
     after = shift(own, -1)
-    gram = gram_of(rows.reshape(-1, width), periods)
-    pieces = lax.all_to_all(gram.reshape(pairs, periods // pairs, -1), PAIRS, 0, 0, tiled=True)
-    piece = jnp.sum(spread(jnp.sum(pieces, 0), "z", lax.axis_size("z")), 0)
+    pieces = lax.all_to_all(gram.reshape(pairs, -1, 1, periods), PAIRS, 0, 0, tiled=True)
+    copies = sum_and_copy(pieces, lax.axis_size("z"), LONG)
+    pieces = lax.all_to_all(copies, "z", 0, 0, tiled=True)
+    copies = sum_and_copy(pieces, groups * pairs, None)
+    raw = lax.all_to_all(copies, ("x",) + PAIRS, 0, 0, tiled=True).reshape(-1, periods)
+    before, after, _ = lax.optimization_barrier((before, after, copies))
     half = own.shape[0] // 2
     opposite = [shift(before[:half], 1), shift(after[half:], -1)]
-    raw = spread(piece, ("x",) + PAIRS, groups * pairs).reshape(-1, periods)
-    blocks = [own, after, *opposite, before]
-    result = project(raw, gain, start_basis, lax.axis_index("x"), blocks, count)
-    return result.reshape(field.shape)
+    mix = refine(raw, gain, start_basis, lax.axis_index("x"), local, count)
+    return project(mix, [own, after, *opposite, before]).reshape(field.shape)
 
 
 def solution(mesh):

time: 97.5 us -> 101 us (1.036)
  blocking collectives: 32.4 us -> 41.4 us
  waiting for transfers between devices: 12.9 us -> 3.97 us
  Pallas kernels: 13.6 us -> 19.3 us
  starting transfers between devices: 34 us -> 31.5 us
    all_to_all x2, waiting for transfers between devices: 12.9 us -> 0.01 us  [the longest x1 0.01 us: per_device(): lax.all_to_all(gram.reshape(pairs, -1, 1, periods), PAIRS, 0, 0, tiled=True)]
    all_to_all x1, blocking collectives: 17.6 us -> 26.7 us  [per_device(): pieces = lax.all_to_all(copies, 'z', 0, 0, tiled=True)]
    pallas_call x2 -> x5, Pallas kernels: 11.4 us -> 17.1 us  [the longest x1 7.21 us: refine(): pl.pallas_call(functools.partial(refine_kernel, count), out_shape=jax.Sha...]
    ppermute x4, waiting for transfers between devices: 0.01 us -> 3.96 us  [shift(): lax.ppermute(value, 'x', [(i, (i + step) % count) for i in range(count)])]
    broadcast_in_dim x2 -> x0, local copies, waits for them, and re-layouts: 1.37 us -> none  [spread(): jnp.broadcast_to(block[None], (count,) + block.shape)]
    all_to_all x2, starting transfers between devices: 21.1 us -> 19.7 us  [the longest x1 11 us: per_device(): lax.all_to_all(gram.reshape(pairs, -1, 1, periods), PAIRS, 0, 0, tiled=True)]
    unnamed x6 -> x8, local copies, waits for them, and re-layouts: 0.65 us -> 1.97 us
    ppermute x4, starting transfers between devices: 13 us -> 11.8 us  [shift(): lax.ppermute(value, 'x', [(i, (i + step) % count) for i in range(count)])]
  transfers between devices with their start and end apart: 6 -> 6, of which waited for: 2 -> 2; matrix products, arithmetic and copies ran while one was open for 3% -> 2% of each run, Pallas kernels for 3% -> 10%
where the time goes in v5:
time: 101 us; the launch traced here: 99.9 us
  blocking collectives  41.4 us (41%)
  starting transfers between devices  31.5 us (31%)
  Pallas kernels  19.3 us (19%)
  waiting for transfers between devices  3.97 us (4%)
  local copies, waits for them, and re-layouts  3.65 us (4%)
    all_to_all x1, blocking collectives, per_device(): pieces = lax.all_to_all(copies, 'z', 0, 0, tiled=True)  26.7 us
    all_to_all x1, blocking collectives, per_device(): rows = lax.all_to_all(blocks, 'x', 0, 0, tiled=True)  14.7 us
    ppermute x4, starting transfers between devices, shift(): lax.ppermute(value, 'x', [(i, (i + step) % count) for i in range(count)])  11.8 us
    all_to_all x1, starting transfers between devices, per_device(): lax.all_to_all(gram.reshape(pairs, -1, 1, periods), PAIRS, 0, 0, tiled=True)  11 us
    all_to_all x1, starting transfers between devices, per_device(): lax.all_to_all(copies, ('x',) + PAIRS, 0, 0, tiled=True)  8.75 us
    pallas_call x1, Pallas kernels, refine(): pl.pallas_call(functools.partial(refine_kernel, count), out_shape=jax.Sha...  7.21 us
    pallas_call x1, Pallas kernels, project(): pl.pallas_call(project_kernel, out_shape=jax.ShapeDtypeStruct(blocks[0].s...  4.18 us
    ppermute x4, waiting for transfers between devices, shift(): lax.ppermute(value, 'x', [(i, (i + step) % count) for i in range(count)])  3.96 us
  transfers between devices with their start and end apart: 6, of which 2 were waited for; matrix products, arithmetic and copies ran while one was open for 2% of the time, Pallas kernels for 10%

profile of v5, /device:TPU:1, one launch (start us, length us, event | category | flops | bytes accessed | tf_op | source)
XLA Modules:
  0.0 99.9 jit_solution(5695143033418557308)
XLA Ops:
  0.0 2.2 %pack.1 = f32[4,32,2,8,128]{4,3,2,1,0:T(8,128)} custom-call(f32[32,2,8,512]{3,2,1,0:T(8,128)} %field_ref.1), custom_call_target="tpu_custom_call" | custom-call | tf_op jit(solution)/shard_map/pack/pallas_call | solution.py:51
  2.2 14.7 %all_to_all.20 = f32[4,512,128]{2,1,0:T(8,128)} all-to-all(f32[4,512,128]{2,1,0:T(8,128)} %bitcast.13), channel_id=1, replica_groups=mesh['y'=4,'z'=16,'c'=2,'x'=4] {'x'}, dimensions={0} | all-to-all | bytes 2097152 | tf_op jit(solution)/shard_map/all_to_all | solution.py:280
  16.9 0.0 copy-start
  16.9 2.6 %gram.1 = f32[72,128]{1,0:T(8,128)} custom-call(f32[2048,128]{1,0:T(8,128)} %bitcast.12), custom_call_target="tpu_custom_call" | custom-call | tf_op jit(solution)/shard_map/gram/pallas_call | solution.py:104
  19.5 11.0 %all-to-all-start.1 = ((f32[8,9,1,128]{3,2,1,0:T(1,128)}), f32[8,9,1,128]{3,2,1,0:T(1,128)S(1)}, u32[]{:S(2)}, u32[]{:S(2)}) async-start(f32[8,9,1,128]{3,2,1,0:T(1,128)} %bitcast.14), calls=%async_computation.1 | async-start | bytes 73728 | tf_op jit(solution)/shard_map/all_to_all | solution.py:285
  30.5 0.0 copy-done
  30.5 2.8 %collective-permute-start.1 = (f32[512,512]{1,0:T(8,128)S(1)}, f32[512,512]{1,0:T(8,128)S(1)}, u32[]{:S(2)}, u32[]{:S(2)}) collective-permute-start(f32[512,512]{1,0:T(8,128)S(1)} %bitcast.9), channel_id=1, source_target_pairs={{0,3},{1,0},{2,1},{3,2},{4,7},{5,4},{6,5},{7,6},{8,11},{9,8},{10,9... | collective-permute-start | bytes 3145736 | tf_op jit(solution)/shard_map/ppermute | solution.py:268
  33.3 2.5 %collective-permute-start = (f32[512,512]{1,0:T(8,128)S(1)}, f32[512,512]{1,0:T(8,128)S(1)}, u32[]{:S(2)}, u32[]{:S(2)}) collective-permute-start(f32[512,512]{1,0:T(8,128)S(1)} %bitcast.10), channel_id=1, source_target_pairs={{0,1},{1,2},{2,3},{3,0},{4,5},{5,6},{6,7},{7,4},{8,9},{9,10},{10,1... | collective-permute-start | bytes 3145736 | tf_op jit(solution)/shard_map/ppermute | solution.py:268
  35.8 0.0 all-to-all-done.1.pieces_ref
  35.8 0.0 copy-start.3
  35.8 0.6 copy-done.3
  36.4 1.4 %sum_and_copy.2 = f32[16,9,1,128]{3,2,1,0:T(1,128)} custom-call(f32[8,9,1,128]{3,2,1,0:T(1,128)} %copy-done.3), custom_call_target="tpu_custom_call" | custom-call | flops 40000000000 | tf_op jit(solution)/shard_map/sum_and_copy/pallas_call | solution.py:256
  37.9 26.7 %all_to_all.21.pieces_ref = f32[16,9,1,128]{3,2,1,0:T(1,128)} all-to-all(f32[16,9,1,128]{3,2,1,0:T(1,128)} %sum_and_copy.2), channel_id=1, replica_groups=mesh['y'=4,'z'=16,'c'=2,'x'=4] {'z'}, dimensions={0} | all-to-all | bytes 147456 | tf_op jit(solution)/shard_map/all_to_all | solution.py:287
  64.6 1.6 %sum_and_copy.3 = f32[32,9,1,128]{3,2,1,0:T(1,128)} custom-call(f32[16,9,1,128]{3,2,1,0:T(1,128)} %all_to_all.21.pieces_ref), custom_call_target="tpu_custom_call" | custom-call | tf_op jit(solution)/shard_map/sum_and_copy/pallas_call | solution.py:256
  66.2 8.8 %all-to-all-start.3 = ((f32[32,9,1,128]{3,2,1,0:T(1,128)}), f32[32,9,1,128]{3,2,1,0:T(1,128)S(1)}, u32[]{:S(2)}, u32[]{:S(2)}) async-start(f32[32,9,1,128]{3,2,1,0:T(1,128)} %sum_and_copy.3), calls=%async_computation.3 | async-start | bytes 294912 | tf_op jit(solution)/shard_map/all_to_all | solution.py:289
  75.0 0.0 collective-permute-done.1.refs_1_
  75.0 0.0 collective-permute-done.refs_4_
  75.0 0.9 slice.7
  75.8 0.8 slice.6
  76.7 3.3 %collective-permute-start.2 = (f32[256,512]{1,0:T(8,128)}, f32[256,512]{1,0:T(8,128)}, u32[]{:S(2)}, u32[]{:S(2)}) collective-permute-start(f32[256,512]{1,0:T(8,128)} %slice.6), channel_id=1, source_target_pairs={{0,1},{1,2},{2,3},{3,0},{4,5},{5,6},{6,7},{7,4},{8,9},{9,10},{10,1... | collective-permute-start | bytes 1572872 | tf_op jit(solution)/shard_map/ppermute | solution.py:268
  80.0 3.2 %collective-permute-start.3 = (f32[256,512]{1,0:T(8,128)}, f32[256,512]{1,0:T(8,128)}, u32[]{:S(2)}, u32[]{:S(2)}) collective-permute-start(f32[256,512]{1,0:T(8,128)} %slice.7), channel_id=1, source_target_pairs={{0,3},{1,0},{2,1},{3,2},{4,7},{5,4},{6,5},{7,6},{8,11},{9,8},{10,9... | collective-permute-start | bytes 1572872 | tf_op jit(solution)/shard_map/ppermute | solution.py:268
  83.2 0.0 all-to-all-done.3
  83.2 0.0 copy-start.2
  83.2 0.7 copy-done.2
  83.8 7.2 %refine.1.mix_ref = f32[32,128]{1,0:T(8,128)} custom-call(f32[288,128]{1,0:T(8,128)} %bitcast.15, f32[1,128]{1,0:T(1,128)} %bitcast.17, f32[32,128]{1,0:T(8,128)} %bitcast.16, s32[1]{0:T(128)} %bitcast.7.group_ref), custom_call_target="tpu_custom_call" | custom-call | flops 40000000000 | tf_op jit(solution)/shard_map/refine/pallas_call | solution.py:159
  91.1 2.3 %collective-permute-done.2.refs_2_ = f32[256,512]{1,0:T(8,128)} collective-permute-done((f32[256,512]{1,0:T(8,128)}, f32[256,512]{1,0:T(8,128)}, u32[]{:S(2)}, u32[]{:S(2)}) %collective-permute-start.2) | collective-permute-done | bytes 524320 | tf_op jit(solution)/shard_map/ppermute | solution.py:268
  93.4 1.6 %collective-permute-done.3.refs_3_ = f32[256,512]{1,0:T(8,128)} collective-permute-done((f32[256,512]{1,0:T(8,128)}, f32[256,512]{1,0:T(8,128)}, u32[]{:S(2)}, u32[]{:S(2)}) %collective-permute-start.3) | collective-permute-done | bytes 524320 | tf_op jit(solution)/shard_map/ppermute | solution.py:268
  95.0 0.0 copy-start.1
  95.0 0.7 copy-done.1
  95.7 4.2 %project.1 = f32[512,512]{1,0:T(8,128)} custom-call(f32[32,128]{1,0:T(8,128)S(1)} %copy-done.1, f32[512,512]{1,0:T(8,128)S(1)} %bitcast.11, f32[512,512]{1,0:T(8,128)S(1)} %collective-permute-done.1.refs_1_, f32[256,512]{1,0:T(8,128)} %collective-permute-done.2.refs_2_, f32[256,512]{1,0:T(8,128)} %collective-permute-done.3.refs_3_, ...), custom_call_target="tpu_custom_call" | custom-call | tf_op jit(solution)/shard_map/project/pallas_call | solution.py:231
Async XLA Ops:
  16.9 13.6 %copy-start = (f32[32,2,8,512]{3,2,1,0:T(8,128)S(1)}, f32[32,2,8,512]{3,2,1,0:T(8,128)}, u32[]{:S(2)}) copy-start(f32[32,2,8,512]{3,2,1,0:T(8,128)} %field_ref.1) | copy-start | bytes 3145732
  19.5 16.3 %all-to-all-start.1 = ((f32[8,9,1,128]{3,2,1,0:T(1,128)}), f32[8,9,1,128]{3,2,1,0:T(1,128)S(1)}, u32[]{:S(2)}, u32[]{:S(2)}) async-start(f32[8,9,1,128]{3,2,1,0:T(1,128)} %bitcast.14), calls=%async_computation.1 | async-start | bytes 73728 | tf_op jit(solution)/shard_map/all_to_all | solution.py:285
  30.5 44.5 %collective-permute-start.1 = (f32[512,512]{1,0:T(8,128)S(1)}, f32[512,512]{1,0:T(8,128)S(1)}, u32[]{:S(2)}, u32[]{:S(2)}) collective-permute-start(f32[512,512]{1,0:T(8,128)S(1)} %bitcast.9), channel_id=1, source_target_pairs={{0,3},{1,0},{2,1},{3,2},{4,7},{5,4},{6,5},{7,6},{8,11},{9,8},{10,9... | collective-permute-start | bytes 3145736 | tf_op jit(solution)/shard_map/ppermute | solution.py:268
  33.3 41.7 %collective-permute-start = (f32[512,512]{1,0:T(8,128)S(1)}, f32[512,512]{1,0:T(8,128)S(1)}, u32[]{:S(2)}, u32[]{:S(2)}) collective-permute-start(f32[512,512]{1,0:T(8,128)S(1)} %bitcast.10), channel_id=1, source_target_pairs={{0,1},{1,2},{2,3},{3,0},{4,5},{5,6},{6,7},{7,4},{8,9},{9,10},{10,1... | collective-permute-start | bytes 3145736 | tf_op jit(solution)/shard_map/ppermute | solution.py:268
  35.8 0.6 copy-start.3
  66.2 17.0 %all-to-all-start.3 = ((f32[32,9,1,128]{3,2,1,0:T(1,128)}), f32[32,9,1,128]{3,2,1,0:T(1,128)S(1)}, u32[]{:S(2)}, u32[]{:S(2)}) async-start(f32[32,9,1,128]{3,2,1,0:T(1,128)} %sum_and_copy.3), calls=%async_computation.3 | async-start | bytes 294912 | tf_op jit(solution)/shard_map/all_to_all | solution.py:289
  76.7 16.7 %collective-permute-start.2 = (f32[256,512]{1,0:T(8,128)}, f32[256,512]{1,0:T(8,128)}, u32[]{:S(2)}, u32[]{:S(2)}) collective-permute-start(f32[256,512]{1,0:T(8,128)} %slice.6), channel_id=1, source_target_pairs={{0,1},{1,2},{2,3},{3,0},{4,5},{5,6},{6,7},{7,4},{8,9},{9,10},{10,1... | collective-permute-start | bytes 1572872 | tf_op jit(solution)/shard_map/ppermute | solution.py:268
  80.0 15.0 %collective-permute-start.3 = (f32[256,512]{1,0:T(8,128)}, f32[256,512]{1,0:T(8,128)}, u32[]{:S(2)}, u32[]{:S(2)}) collective-permute-start(f32[256,512]{1,0:T(8,128)} %slice.7), channel_id=1, source_target_pairs={{0,3},{1,0},{2,1},{3,2},{4,7},{5,4},{6,5},{7,6},{8,11},{9,8},{10,9... | collective-permute-start | bytes 1572872 | tf_op jit(solution)/shard_map/ppermute | solution.py:268
  83.2 0.7 copy-start.2
  95.0 0.7 copy-start.1

commit v6 on v4

v6 whole, which is shorter than its diff:
```python
import functools

import jax
import jax.numpy as jnp
from jax import lax
from jax.experimental import pallas as pl
from jax.experimental.pallas import tpu as pltpu
from jax.sharding import Mesh, PartitionSpec as P

ITERS = 3
PIVOTS = 4
LANES = 128
HIGH = lax.Precision.HIGHEST
PAIRS = ("y", "c")
VMEM = pl.BlockSpec(memory_space=pltpu.VMEM)
ANY = pl.BlockSpec(memory_space=pl.ANY)


def dot(a, b, ca, cb, precision=HIGH):
    return lax.dot_general(
        a, b, (((ca,), (cb,)), ((), ())), precision=precision, preferred_element_type=jnp.float32
    )


def halves(value):
    high = value.astype(jnp.bfloat16)
    return high, (value - high.astype(jnp.float32)).astype(jnp.bfloat16)


def tile_copies(block, held, first, sems, at):
    lanes = held.shape[1]
    tiles = block.shape[1] // lanes
    step = held.shape[0] // tiles
    return [
        pltpu.make_async_copy(
            block.at[:, pl.ds(c * lanes, lanes)],
            held.at[pl.ds(c * step + first, block.shape[0])],
            sems.at[at + c],
        )
        for c in range(tiles)
    ]


def lines(held, tiles, first, count, stride):
    step = held.shape[0] // tiles
    return jnp.concatenate(
        [held[pl.ds(c * step + first, count, stride=stride), :] for c in range(tiles)], axis=1
    )


def fold(acc, local, at):
    high = acc[:local, at : at + local] + acc[:local, at + local : at + 2 * local]
    low = acc[local:, at : at + local] + acc[local:, at + local : at + 2 * local]
    return high + low


def gram_kernel(local, group_ref, own_ref, before_ref, top_ref, bottom_ref, out_ref, *scratch):
    own, before, across, sems = scratch
    tiles = own_ref.shape[1] // LANES
    copies = tile_copies(own_ref, own, 0, sems, 0) + tile_copies(before_ref, before, 0, sems, tiles)
    copies += tile_copies(top_ref, across, 0, sems, 2 * tiles)
    copies += tile_copies(bottom_ref, across, top_ref.shape[0], sems, 3 * tiles)
    for copy in copies:
        copy.start()
    for copy in copies:
        copy.wait()
    per_period = own_ref.shape[0] // local
    half = per_period // 2
    second = group_ref[0] >= 2
    near, far = None, None
    for s in range(half):
        pair = [lines(own, tiles, s + t * half, local, per_period) for t in range(2)]
        for t in range(2):
            mine = halves(pair[t])
            other = halves(lines(before, tiles, s + t * half, local, per_period))
            part = dot(
                jnp.concatenate(mine, axis=0), jnp.concatenate(mine + other, axis=0), 1, 1, None
            )
            near = part if near is None else near + part
        mine = jnp.concatenate(halves(jnp.where(second, pair[1], pair[0])), axis=0)
        other = jnp.concatenate(halves(lines(across, tiles, s, local, half)), axis=0)
        part = dot(mine, other, 1, 1, None)
        far = part if far is None else far + part
    out_ref[...] = jnp.concatenate(
        [
            fold(near, local, 0),
            jnp.zeros((local, local), jnp.float32),
            fold(far, local, 0),
            fold(near, local, 2 * local),
        ],
        axis=1,
    )


def gram_of(group, own, before, top, bottom, local, periods):
    shape = (own.shape[0] * own.shape[1] // LANES, LANES)
    tiles = own.shape[1] // LANES
    return pl.pallas_call(
        functools.partial(gram_kernel, local),
        out_shape=jax.ShapeDtypeStruct((local, periods), jnp.float32),
        in_specs=[pl.BlockSpec(memory_space=pltpu.SMEM)] + [ANY] * 4,
        out_specs=VMEM,
        scratch_shapes=[
            pltpu.VMEM(shape, jnp.float32),
            pltpu.VMEM(shape, jnp.float32),
            pltpu.VMEM((shape[0] // 2, LANES), jnp.float32),
            pltpu.SemaphoreType.DMA((4 * tiles,)),
        ],
        compiler_params=pltpu.CompilerParams(vmem_limit_bytes=32 * 2**20),
        name="gram",
    )(group[None], own, before, top, bottom)


def assemble(parts, local):
    lane = lax.broadcasted_iota(jnp.int32, (local, parts.shape[1]), 1)
    slabs = []
    for at in range(0, parts.shape[0], local):
        slab = parts[at : at + local]
        slab = jnp.where(lane < local, 0.5 * slab, slab)
        slabs.append(pltpu.roll(slab, at, 1) if at else slab)
    half = jnp.concatenate(slabs, axis=0)
    return half + half.T


def inverse_factor(inner):
    rank = inner.shape[0]
    row = lax.broadcasted_iota(jnp.int32, (rank, rank), 0)
    col = lax.broadcasted_iota(jnp.int32, (rank, rank), 1)
    work = jnp.concatenate([inner, jnp.where(row == col, 1.0, 0.0)], axis=1)
    shape = work.shape
    sub = lax.broadcasted_iota(jnp.int32, shape, 0)
    pivots = jnp.ones(shape, jnp.float32)
    for start in range(0, rank, PIVOTS):
        ks = range(start, start + PIVOTS)
        columns = [jnp.broadcast_to(work[:, k : k + 1], shape) for k in ks]
        lines = [work[k : k + 1, :] for k in ks]
        for j, k in enumerate(ks):
            pivot = columns[j][k : k + 1, :]
            pivots = jnp.where(sub == k, pivot, pivots)
            factor = jnp.where(sub > k, columns[j] * (1.0 / pivot), 0.0)
            for i in range(j + 1, PIVOTS):
                columns[i] = columns[i] - factor * columns[i][k : k + 1, :]
                lines[i] = lines[i] - factor[start + i : start + i + 1, :] * lines[j]
            work = work - factor * lines[j]
    return work[:, rank:] * lax.rsqrt(pivots[:, rank:])


def project_kernel(count, local, group_ref, raw_ref, gain_ref, start_ref, *refs):
    own_ref, after_ref, before_ref, top_ref, bottom_ref, rest_ref = refs[:6]
    out_ref, held, across, ready, full_ref, in_sems, out_sems = refs[6:]
    height, cells = out_ref.shape
    tiles = cells // LANES
    group = group_ref[0]
    second = jnp.where(group >= 2, 1, 0)
    fetches = []
    for i, block in enumerate((own_ref, after_ref, before_ref)):
        fetches += tile_copies(block, held, i * height, in_sems, i * tiles)
    here, there = across.at[second], across.at[1 - second]
    fetches += tile_copies(top_ref, here, 0, in_sems, 3 * tiles)
    fetches += tile_copies(bottom_ref, here, top_ref.shape[0], in_sems, 4 * tiles)
    fetches += tile_copies(rest_ref, there, 0, in_sems, 5 * tiles)
    for fetch in fetches:
        fetch.start()
    gain = gain_ref[...]
    periods = gain.shape[1]
    per_period = height // local
    half = per_period // 2
    raw = assemble(raw_ref[...], local)

    def grow(basis):
        return dot(basis * gain, raw, 1, 0) * (gain * (1.0 / count))

    grown = grow(start_ref[...])
    for _ in range(ITERS - 1):
        later = grow(grown)
        grown = dot(inverse_factor(dot(grown, grown, 1, 1)), later, 1, 0)
    basis = dot(inverse_factor(dot(grown, grown, 1, 1)), grown, 1, 0)
    full_ref[...] = dot(basis, basis, 0, 0) * gain
    first = group * local
    own = full_ref[pl.ds(pl.multiple_of(first, local), local), :]
    high, low = halves(pltpu.roll(own, lax.rem(periods - first, periods), 1))
    mix = jnp.concatenate(
        [jnp.concatenate([high, high], axis=1), jnp.concatenate([low, jnp.zeros_like(low)], axis=1)],
        axis=0,
    )
    for fetch in fetches:
        fetch.wait()
    step = held.shape[0] // tiles
    side = across.shape[1] // tiles
    sends = []
    for pair in range(0, tiles, 2):
        for s in range(per_period):
            line = jnp.concatenate(
                [
                    jnp.concatenate(
                        [
                            held[pl.ds(c * step + s, 2 * local, stride=per_period), :],
                            across[s // half, pl.ds(c * side + s % half, local, stride=half), :],
                            held[
                                pl.ds(c * step + 2 * height + s, local, stride=per_period), :
                            ],
                        ],
                        axis=0,
                    )
                    for c in range(pair, pair + 2)
                ],
                axis=1,
            )
            result = dot(mix, jnp.concatenate(halves(line), axis=0), 1, 0, None)
            result = result[:local] + result[local:]
            for c in range(2):
                ready[pl.ds((pair + c) * height + s, local, stride=per_period), :] = result[
                    :, c * LANES : (c + 1) * LANES
                ]
        for c in range(pair, pair + 2):
            sends.append(
                pltpu.make_async_copy(
                    ready.at[pl.ds(c * height, height)],
                    out_ref.at[:, pl.ds(c * LANES, LANES)],
                    out_sems.at[c],
                )
            )
            sends[-1].start()
    for send in sends:
        send.wait()


def project(raw, gain, start_basis, group, blocks, local, count):
    height, cells = blocks[0].shape
    periods = gain.shape[0]
    tiles = cells // LANES
    return pl.pallas_call(
        functools.partial(project_kernel, count, local),
        out_shape=jax.ShapeDtypeStruct((height, cells), jnp.float32),
        in_specs=[pl.BlockSpec(memory_space=pltpu.SMEM)] + [VMEM] * 3 + [ANY] * len(blocks),
        out_specs=ANY,
        scratch_shapes=[
            pltpu.VMEM((tiles * 3 * height, LANES), jnp.float32),
            pltpu.VMEM((2, tiles * height // 2, LANES), jnp.float32),
            pltpu.VMEM((tiles * height, LANES), jnp.float32),
            pltpu.VMEM((periods, periods), jnp.float32),
            pltpu.SemaphoreType.DMA((len(blocks) * tiles,)),
            pltpu.SemaphoreType.DMA((tiles,)),
        ],
        compiler_params=pltpu.CompilerParams(vmem_limit_bytes=32 * 2**20),
        name="project",
    )(group[None], raw, gain[None, :], start_basis.T, *blocks)


def shift(value, step):
    count = lax.axis_size("x")
    return lax.ppermute(value, "x", [(i, (i + step) % count) for i in range(count)])


def copies_of(pieces, count):
    piece = jnp.sum(pieces, 0)
    return lax.optimization_barrier(jnp.broadcast_to(piece[None], (count,) + piece.shape))


def per_device(field, gain, start_basis):
    groups = lax.axis_size("x")
    group = lax.axis_index("x")
    local, parts, layers, cells = field.shape
    periods = gain.shape[0]
    pairs = lax.axis_size("y") * lax.axis_size("c")
    count = float(parts * layers * cells * lax.axis_size("z") * pairs)
    own = field.reshape(-1, cells)

    def side(block, part, first, size):
        block = block.reshape(field.shape)
        return lax.dynamic_slice(
            block, (first, part, 0, 0), (size, 1, layers, cells)
        ).reshape(-1, cells)

    sent = 1 - group // 2
    before = shift(own, 1)
    top = shift(shift(side(own, sent, 0, local // 2), -1), -1)
    bottom = shift(shift(side(own, sent, local // 2, local // 2), -1), -1)
    rest = shift(side(before, 1 - (group + 1) % groups // 2, 0, local), 1)
    source, top, bottom = lax.optimization_barrier((own, top, bottom))
    after = shift(source, -1)
    gram = gram_of(group, own, before, top, bottom, local, periods)
    pieces = lax.all_to_all(gram.reshape(pairs, -1, periods), PAIRS, 0, 0, tiled=True)
    copies, rest = lax.optimization_barrier((copies_of(pieces, lax.axis_size("z")), rest))
    pieces = lax.all_to_all(copies, "z", 0, 0, tiled=True)
    copies, after = lax.optimization_barrier((copies_of(pieces, groups * pairs), after))
    raw = lax.all_to_all(copies, ("x",) + PAIRS, 0, 0, tiled=True).reshape(periods, periods)
    blocks = [own, after, before, top, bottom, rest]
    result = project(raw, gain, start_basis, group, blocks, local, count)
    return result.reshape(field.shape)


def solution(mesh):
    cells, per = mesh.devices.shape
    split = Mesh(mesh.devices.reshape(4, cells // 8, 2, per), ("y", "z", "c", "x"))
    spec = P("x", None, None, ("y", "z", "c"))
    return jax.shard_map(
        per_device, mesh=split, in_specs=(spec, P(), P()), out_specs=spec, check_vma=False
    )
```

time: 97.5 us -> 103 us (1.056)
  blocking collectives: 32.4 us -> 55.2 us
  starting transfers between devices: 34 us -> 24.4 us
  waiting for transfers between devices: 12.9 us -> 8.97 us
  Pallas kernels: 13.6 us -> 10.8 us
  local copies, waits for them, and re-layouts: 3.7 us -> 2.61 us
    all_to_all x2 -> x3, blocking collectives: 32.4 us -> 55.2 us  [the longest x1 22.5 us: per_device(): pieces = lax.all_to_all(copies, 'z', 0, 0, tiled=True)]
    all_to_all x2 -> x0, starting transfers between devices: 21.1 us -> none  [spread(): return lax.all_to_all(copies, axes, 0, 0, tiled=True)]
    all_to_all x2 -> x0, waiting for transfers between devices: 12.9 us -> none  [spread(): return lax.all_to_all(copies, axes, 0, 0, tiled=True)]
    ppermute x4 -> x7, starting transfers between devices: 13 us -> 24.4 us  [shift(): lax.ppermute(value, 'x', [(i, (i + step) % count) for i in range(count)])]
    ppermute x4 -> x7, waiting for transfers between devices: 0.01 us -> 8.97 us  [shift(): lax.ppermute(value, 'x', [(i, (i + step) % count) for i in range(count)])]
    pallas_call x3 -> x2, Pallas kernels: 13.6 us -> 10.8 us  [the longest x1 9 us: project(): pl.pallas_call(functools.partial(project_kernel, count, local), out_shape...]
    reshape x0 -> x2, local copies, waits for them, and re-layouts: none -> 1.92 us  [side(): return lax.dynamic_slice(block, (first, part, 0, 0), (size, 1, layers, ce...]
    slice x2 -> x0, local copies, waits for them, and re-layouts: 1.67 us -> none  [per_device(): opposite = [shift(before[:half], 1), shift(after[half:], -1)]]
  transfers between devices with their start and end apart: 6 -> 7, of which waited for: 2 -> 3; matrix products, arithmetic and copies ran while one was open for 3% -> 2% of each run, Pallas kernels for 3% -> 2%
where the time goes in v6:
time: 103 us; the launch traced here: 102 us
  blocking collectives  55.2 us (54%)
  starting transfers between devices  24.4 us (24%)
  Pallas kernels  10.8 us (10%)
  waiting for transfers between devices  8.97 us (9%)
  local copies, waits for them, and re-layouts  2.61 us (3%)
    ppermute x7, starting transfers between devices, shift(): lax.ppermute(value, 'x', [(i, (i + step) % count) for i in range(count)])  24.4 us
    all_to_all x1, blocking collectives, per_device(): pieces = lax.all_to_all(copies, 'z', 0, 0, tiled=True)  22.5 us
    all_to_all x1, blocking collectives, per_device(): lax.all_to_all(gram.reshape(pairs, -1, periods), PAIRS, 0, 0, tiled=True)  17.5 us
    all_to_all x1, blocking collectives, per_device(): lax.all_to_all(copies, ('x',) + PAIRS, 0, 0, tiled=True)  15.1 us
    pallas_call x1, Pallas kernels, project(): pl.pallas_call(functools.partial(project_kernel, count, local), out_shape...  9 us
    ppermute x7, waiting for transfers between devices, shift(): lax.ppermute(value, 'x', [(i, (i + step) % count) for i in range(count)])  8.97 us
  transfers between devices with their start and end apart: 7, of which 3 were waited for; matrix products, arithmetic and copies ran while one was open for 2% of the time, Pallas kernels for 2%

profile of v6, /device:TPU:1, one launch (start us, length us, event | category | flops | bytes accessed | tf_op | source)
XLA Modules:
  0.0 102.2 jit_solution(898490546037331258)
XLA Ops:
  0.0 0.0 copy-start
  0.0 4.1 %collective-permute-start = (f32[512,512]{1,0:T(8,128)}, f32[512,512]{1,0:T(8,128)S(1)}, u32[]{:S(2)}, u32[]{:S(2)}) collective-permute-start(f32[512,512]{1,0:T(8,128)} %bitcast.16), channel_id=1, source_target_pairs={{0,1},{1,2},{2,3},{3,0},{4,5},{5,6},{6,7},{7,4},{8,9},{9,10},{10,1... | collective-permute-start | bytes 3145736 | tf_op jit(solution)/shard_map/ppermute | solution.py:252
  4.1 1.1 %dynamic-slice_bitcast_fusion.1 = (f32[128,512]{1,0:T(8,128)S(1)}, f32[128,512]{1,0:T(8,128)S(1)}) fusion(f32[32,2,8,512]{3,2,1,0:T(8,128)} %param.3, s32[]{:T(128)S(6)} %select_n.22), kind=kLoop, calls=%fused_computation.1 | loop fusion | bytes 1048580 | tf_op jit(solution)/shard_map/reshape | solution.py:273
  5.2 3.2 %collective-permute-start.3 = (f32[128,512]{1,0:T(8,128)S(1)}, f32[128,512]{1,0:T(8,128)S(1)}, u32[]{:S(2)}, u32[]{:S(2)}) collective-permute-start(f32[128,512]{1,0:T(8,128)S(1)} %get-tuple-element.19), channel_id=1, source_target_pairs={{0,3},{1,0},{2,1},{3,2},{4,7},{5,4},{6,5},{7,6},{8,11},{9,8},{10,9... | collective-permute-start | bytes 786440 | tf_op jit(solution)/shard_map/ppermute | solution.py:252
  8.4 3.4 %collective-permute-start.1 = (f32[128,512]{1,0:T(8,128)S(1)}, f32[128,512]{1,0:T(8,128)S(1)}, u32[]{:S(2)}, u32[]{:S(2)}) collective-permute-start(f32[128,512]{1,0:T(8,128)S(1)} %get-tuple-element.20), channel_id=1, source_target_pairs={{0,3},{1,0},{2,1},{3,2},{4,7},{5,4},{6,5},{7,6},{8,11},{9,8},{10,9... | collective-permute-start | bytes 786440 | tf_op jit(solution)/shard_map/ppermute | solution.py:252
  11.7 0.6 collective-permute-done.3
  12.3 4.4 %collective-permute-start.4 = (f32[128,512]{1,0:T(8,128)S(1)}, f32[128,512]{1,0:T(8,128)S(1)}, u32[]{:S(2)}, u32[]{:S(2)}) collective-permute-start(f32[128,512]{1,0:T(8,128)S(1)} %collective-permute-done.3), channel_id=1, source_target_pairs={{0,3},{1,0},{2,1},{3,2},{4,7},{5,4},{6,5},{7,6},{8,11},{9,8},{10,9... | collective-permute-start | bytes 786440 | tf_op jit(solution)/shard_map/ppermute | solution.py:252
  16.7 0.0 collective-permute-done.1
  16.7 3.4 %collective-permute-start.2 = (f32[128,512]{1,0:T(8,128)S(1)}, f32[128,512]{1,0:T(8,128)S(1)}, u32[]{:S(2)}, u32[]{:S(2)}) collective-permute-start(f32[128,512]{1,0:T(8,128)S(1)} %collective-permute-done.1), channel_id=1, source_target_pairs={{0,3},{1,0},{2,1},{3,2},{4,7},{5,4},{6,5},{7,6},{8,11},{9,8},{10,9... | collective-permute-start | bytes 786440 | tf_op jit(solution)/shard_map/ppermute | solution.py:252
  20.1 2.8 %collective-permute-done.4.bottom_ref.refs_4_ = f32[128,512]{1,0:T(8,128)S(1)} collective-permute-done((f32[128,512]{1,0:T(8,128)S(1)}, f32[128,512]{1,0:T(8,128)S(1)}, u32[]{:S(2)}, u32[]{:S(2)}) %collective-permute-start.4) | collective-permute-done | bytes 262176 | tf_op jit(solution)/shard_map/ppermute | solution.py:252
  22.8 5.6 %collective-permute-done.2.top_ref.refs_3_ = f32[128,512]{1,0:T(8,128)S(1)} collective-permute-done((f32[128,512]{1,0:T(8,128)S(1)}, f32[128,512]{1,0:T(8,128)S(1)}, u32[]{:S(2)}, u32[]{:S(2)}) %collective-permute-start.2) | collective-permute-done | bytes 262176 | tf_op jit(solution)/shard_map/ppermute | solution.py:252
  28.5 0.0 copy-done
  28.5 4.2 %collective-permute-start.6 = (f32[512,512]{1,0:T(8,128)S(1)}, f32[512,512]{1,0:T(8,128)}, u32[]{:S(2)}, u32[]{:S(2)}) collective-permute-start(f32[512,512]{1,0:T(8,128)S(1)} %bitcast.17), channel_id=1, source_target_pairs={{0,3},{1,0},{2,1},{3,2},{4,7},{5,4},{6,5},{7,6},{8,11},{9,8},{10,9... | collective-permute-start | bytes 3145736 | tf_op jit(solution)/shard_map/ppermute | solution.py:252
  32.7 0.0 collective-permute-done.before_ref.refs_2_
  32.7 0.8 dynamic-slice_bitcast_fusion
  33.6 1.9 %collective-permute-start.5 = (f32[256,512]{1,0:T(8,128)}, f32[256,512]{1,0:T(8,128)S(1)}, u32[]{:S(2)}, u32[]{:S(2)}) collective-permute-start(f32[256,512]{1,0:T(8,128)} %dynamic-slice_bitcast_fusion), channel_id=1, source_target_pairs={{0,1},{1,2},{2,3},{3,0},{4,5},{5,6},{6,7},{7,4},{8,9},{9,10},{10,1... | collective-permute-start | bytes 1572872 | tf_op jit(solution)/shard_map/ppermute | solution.py:252
  35.5 1.7 %gram.1 = f32[32,128]{1,0:T(8,128)S(1)} custom-call(s32[1]{0:T(128)} %bitcast.group_ref, f32[512,512]{1,0:T(8,128)S(1)} %bitcast.18, f32[512,512]{1,0:T(8,128)S(1)} %collective-permute-done.before_ref.refs_2_, f32[128,512]{1,0:T(8,128)S(1)} %collective-permute-done.2.top_ref.refs_3_, f32[128,512]{1,0:T(8,128)S(1)} %collective-permute-done.4.bottom_ref.refs_4_), custom_call_target="tpu_custom_call" | custom-call | tf_op jit(solution)/shard_map/gram/pallas_call | solution.py:98
  37.2 17.5 %all_to_all.15 = f32[8,4,128]{2,1,0:T(4,128)S(1)} all-to-all(f32[8,4,128]{2,1,0:T(4,128)S(1)} %bitcast.22), channel_id=1, replica_groups=mesh['y'=4,'z'=16,'c'=2,'x'=4] {'y','c'}, dimensions={0} | all-to-all | bytes 32768 | tf_op jit(solution)/shard_map/all_to_all | solution.py:283
  54.8 0.0 collective-permute-done.5.refs_5_
  54.8 22.5 %all_to_all.16 = f32[16,4,128]{2,1,0:T(4,128)S(1)} all-to-all(f32[16,4,128]{2,1,0:T(4,128)S(1)} %broadcast_in_dim.9), channel_id=1, replica_groups=mesh['y'=4,'z'=16,'c'=2,'x'=4] {'z'}, dimensions={0} | all-to-all | bytes 65536 | tf_op jit(solution)/shard_map/all_to_all | solution.py:285
  77.3 0.0 collective-permute-done.6.refs_1_
  77.3 0.0 copy-start.1
  77.4 15.1 %all_to_all.17 = f32[32,4,128]{2,1,0:T(4,128)S(1)} all-to-all(f32[32,4,128]{2,1,0:T(4,128)S(1)} %broadcast_in_dim.10), channel_id=1, replica_groups=mesh['y'=4,'z'=16,'c'=2,'x'=4] {'x','y','c'}, dimensions={0} | all-to-all | bytes 131072 | tf_op jit(solution)/shard_map/all_to_all | solution.py:287
  92.5 0.0 copy-start.2
  92.5 0.0 copy-done.1
  92.5 0.7 copy-done.2
  93.2 9.0 %project.1 = f32[512,512]{1,0:T(8,128)} custom-call(s32[1]{0:T(128)} %bitcast.group_ref, f32[128,128]{1,0:T(8,128)S(1)} %bitcast.21, f32[1,128]{1,0:T(1,128)S(1)} %bitcast.24, f32[32,128]{1,0:T(8,128)S(1)} %bitcast.23, f32[512,512]{1,0:T(8,128)S(1)} %bitcast.19, f32[512,512]{1,0:T(8,128)} %collective-permute-done.6.refs_1_, ...), custom_call_target="tpu_custom_call" | custom-call | tf_op jit(solution)/shard_map/project/pallas_call | solution.py:232
  (4 shorter events, 0.1 us)
Async XLA Ops:
  0.0 28.5 %copy-start = (f32[32,2,8,512]{3,2,1,0:T(8,128)S(1)}, f32[32,2,8,512]{3,2,1,0:T(8,128)}, u32[]{:S(2)}) copy-start(f32[32,2,8,512]{3,2,1,0:T(8,128)} %param.3) | copy-start | bytes 3145732
  0.0 32.7 %collective-permute-start = (f32[512,512]{1,0:T(8,128)}, f32[512,512]{1,0:T(8,128)S(1)}, u32[]{:S(2)}, u32[]{:S(2)}) collective-permute-start(f32[512,512]{1,0:T(8,128)} %bitcast.16), channel_id=1, source_target_pairs={{0,1},{1,2},{2,3},{3,0},{4,5},{5,6},{6,7},{7,4},{8,9},{9,10},{10,1... | collective-permute-start | bytes 3145736 | tf_op jit(solution)/shard_map/ppermute | solution.py:252
  5.2 7.1 %collective-permute-start.3 = (f32[128,512]{1,0:T(8,128)S(1)}, f32[128,512]{1,0:T(8,128)S(1)}, u32[]{:S(2)}, u32[]{:S(2)}) collective-permute-start(f32[128,512]{1,0:T(8,128)S(1)} %get-tuple-element.19), channel_id=1, source_target_pairs={{0,3},{1,0},{2,1},{3,2},{4,7},{5,4},{6,5},{7,6},{8,11},{9,8},{10,9... | collective-permute-start | bytes 786440 | tf_op jit(solution)/shard_map/ppermute | solution.py:252
  8.4 8.3 %collective-permute-start.1 = (f32[128,512]{1,0:T(8,128)S(1)}, f32[128,512]{1,0:T(8,128)S(1)}, u32[]{:S(2)}, u32[]{:S(2)}) collective-permute-start(f32[128,512]{1,0:T(8,128)S(1)} %get-tuple-element.20), channel_id=1, source_target_pairs={{0,3},{1,0},{2,1},{3,2},{4,7},{5,4},{6,5},{7,6},{8,11},{9,8},{10,9... | collective-permute-start | bytes 786440 | tf_op jit(solution)/shard_map/ppermute | solution.py:252
  12.3 10.5 %collective-permute-start.4 = (f32[128,512]{1,0:T(8,128)S(1)}, f32[128,512]{1,0:T(8,128)S(1)}, u32[]{:S(2)}, u32[]{:S(2)}) collective-permute-start(f32[128,512]{1,0:T(8,128)S(1)} %collective-permute-done.3), channel_id=1, source_target_pairs={{0,3},{1,0},{2,1},{3,2},{4,7},{5,4},{6,5},{7,6},{8,11},{9,8},{10,9... | collective-permute-start | bytes 786440 | tf_op jit(solution)/shard_map/ppermute | solution.py:252
  16.7 11.8 %collective-permute-start.2 = (f32[128,512]{1,0:T(8,128)S(1)}, f32[128,512]{1,0:T(8,128)S(1)}, u32[]{:S(2)}, u32[]{:S(2)}) collective-permute-start(f32[128,512]{1,0:T(8,128)S(1)} %collective-permute-done.1), channel_id=1, source_target_pairs={{0,3},{1,0},{2,1},{3,2},{4,7},{5,4},{6,5},{7,6},{8,11},{9,8},{10,9... | collective-permute-start | bytes 786440 | tf_op jit(solution)/shard_map/ppermute | solution.py:252
  28.5 48.9 %collective-permute-start.6 = (f32[512,512]{1,0:T(8,128)S(1)}, f32[512,512]{1,0:T(8,128)}, u32[]{:S(2)}, u32[]{:S(2)}) collective-permute-start(f32[512,512]{1,0:T(8,128)S(1)} %bitcast.17), channel_id=1, source_target_pairs={{0,3},{1,0},{2,1},{3,2},{4,7},{5,4},{6,5},{7,6},{8,11},{9,8},{10,9... | collective-permute-start | bytes 3145736 | tf_op jit(solution)/shard_map/ppermute | solution.py:252
  33.6 21.2 %collective-permute-start.5 = (f32[256,512]{1,0:T(8,128)}, f32[256,512]{1,0:T(8,128)S(1)}, u32[]{:S(2)}, u32[]{:S(2)}) collective-permute-start(f32[256,512]{1,0:T(8,128)} %dynamic-slice_bitcast_fusion), channel_id=1, source_target_pairs={{0,1},{1,2},{2,3},{3,0},{4,5},{5,6},{6,7},{7,4},{8,9},{9,10},{10,1... | collective-permute-start | bytes 1572872 | tf_op jit(solution)/shard_map/ppermute | solution.py:252
  77.3 15.2 %copy-start.1 = (f32[128,32]{0,1:T(8,128)S(1)}, f32[128,32]{0,1:T(8,128)}, u32[]{:S(2)}) copy-start(f32[128,32]{0,1:T(8,128)} %param.5) | copy-start | bytes 49156
  92.5 0.7 copy-start.2

commit v7 on v6

--- a/solution.py
+++ b/solution.py
@@ -54,12 +54,12 @@
     return high + low
 
 
-def gram_kernel(local, group_ref, own_ref, before_ref, top_ref, bottom_ref, out_ref, *scratch):
-    own, before, across, sems = scratch
+def gram_kernel(local, group_ref, own_ref, before_ref, after_ref, out_ref, *scratch):
+    own, before, after, sems = scratch
     tiles = own_ref.shape[1] // LANES
-    copies = tile_copies(own_ref, own, 0, sems, 0) + tile_copies(before_ref, before, 0, sems, tiles)
-    copies += tile_copies(top_ref, across, 0, sems, 2 * tiles)
-    copies += tile_copies(bottom_ref, across, top_ref.shape[0], sems, 3 * tiles)
+    copies = []
+    for i, (block, held) in enumerate(((own_ref, own), (before_ref, before), (after_ref, after))):
+        copies += tile_copies(block, held, 0, sems, i * tiles)
     for copy in copies:
         copy.start()
     for copy in copies:
@@ -69,17 +69,15 @@
     second = group_ref[0] >= 2
     near, far = None, None
     for s in range(half):
-        pair = [lines(own, tiles, s + t * half, local, per_period) for t in range(2)]
+        left = [lines(before, tiles, s + t * half, local, per_period) for t in range(2)]
         for t in range(2):
-            mine = halves(pair[t])
-            other = halves(lines(before, tiles, s + t * half, local, per_period))
-            part = dot(
-                jnp.concatenate(mine, axis=0), jnp.concatenate(mine + other, axis=0), 1, 1, None
-            )
+            mine = halves(lines(own, tiles, s + t * half, local, per_period))
+            both = jnp.concatenate(mine + halves(left[t]), axis=0)
+            part = dot(jnp.concatenate(mine, axis=0), both, 1, 1, None)
             near = part if near is None else near + part
-        mine = jnp.concatenate(halves(jnp.where(second, pair[1], pair[0])), axis=0)
-        other = jnp.concatenate(halves(lines(across, tiles, s, local, half)), axis=0)
-        part = dot(mine, other, 1, 1, None)
+        right = jnp.concatenate(halves(lines(after, tiles, s, local, half)), axis=0)
+        left = jnp.concatenate(halves(jnp.where(second, left[1], left[0])), axis=0)
+        part = dot(left, right, 1, 1, None)
         far = part if far is None else far + part
     out_ref[...] = jnp.concatenate(
         [
@@ -92,32 +90,35 @@
     )
 
 
-def gram_of(group, own, before, top, bottom, local, periods):
+def gram_of(group, own, before, after, local, periods):
     shape = (own.shape[0] * own.shape[1] // LANES, LANES)
     tiles = own.shape[1] // LANES
     return pl.pallas_call(
         functools.partial(gram_kernel, local),
         out_shape=jax.ShapeDtypeStruct((local, periods), jnp.float32),
-        in_specs=[pl.BlockSpec(memory_space=pltpu.SMEM)] + [ANY] * 4,
+        in_specs=[pl.BlockSpec(memory_space=pltpu.SMEM)] + [ANY] * 3,
         out_specs=VMEM,
         scratch_shapes=[
             pltpu.VMEM(shape, jnp.float32),
             pltpu.VMEM(shape, jnp.float32),
             pltpu.VMEM((shape[0] // 2, LANES), jnp.float32),
-            pltpu.SemaphoreType.DMA((4 * tiles,)),
+            pltpu.SemaphoreType.DMA((3 * tiles,)),
         ],
         compiler_params=pltpu.CompilerParams(vmem_limit_bytes=32 * 2**20),
         name="gram",
-    )(group[None], own, before, top, bottom)
+    )(group[None], own, before, after)
 
 
 def assemble(parts, local):
+    groups = parts.shape[0] // local
     lane = lax.broadcasted_iota(jnp.int32, (local, parts.shape[1]), 1)
+    far = (lane >= 2 * local) & (lane < 3 * local)
+    rows = [parts[g * local : (g + 1) * local] for g in range(groups)]
     slabs = []
-    for at in range(0, parts.shape[0], local):
-        slab = parts[at : at + local]
+    for g in range(groups):
+        slab = jnp.where(far, rows[(g + 1) % groups], rows[g])
         slab = jnp.where(lane < local, 0.5 * slab, slab)
-        slabs.append(pltpu.roll(slab, at, 1) if at else slab)
+        slabs.append(pltpu.roll(slab, g * local, 1) if g else slab)
     half = jnp.concatenate(slabs, axis=0)
     return half + half.T
 
@@ -146,19 +147,18 @@
 
 
 def project_kernel(count, local, group_ref, raw_ref, gain_ref, start_ref, *refs):
-    own_ref, after_ref, before_ref, top_ref, bottom_ref, rest_ref = refs[:6]
-    out_ref, held, across, ready, full_ref, in_sems, out_sems = refs[6:]
+    own_ref, before_ref, *split_refs = refs[:6]
+    out_ref, held, after, across, ready, full_ref, in_sems, out_sems = refs[6:]
     height, cells = out_ref.shape
     tiles = cells // LANES
     group = group_ref[0]
     second = jnp.where(group >= 2, 1, 0)
-    fetches = []
-    for i, block in enumerate((own_ref, after_ref, before_ref)):
-        fetches += tile_copies(block, held, i * height, in_sems, i * tiles)
-    here, there = across.at[second], across.at[1 - second]
-    fetches += tile_copies(top_ref, here, 0, in_sems, 3 * tiles)
-    fetches += tile_copies(bottom_ref, here, top_ref.shape[0], in_sems, 4 * tiles)
-    fetches += tile_copies(rest_ref, there, 0, in_sems, 5 * tiles)
+    later = jnp.where((group == 1) | (group == 2), 1, 0)
+    fetches = tile_copies(own_ref, held, 0, in_sems, 0)
+    fetches += tile_copies(before_ref, held, height, in_sems, tiles)
+    places = (after.at[second], after.at[1 - second], across.at[later], across.at[1 - later])
+    for i, (block, place) in enumerate(zip(split_refs, places)):
+        fetches += tile_copies(block, place, 0, in_sems, (2 + i) * tiles)
     for fetch in fetches:
         fetch.start()
     gain = gain_ref[...]
@@ -194,11 +194,10 @@
                 [
                     jnp.concatenate(
                         [
-                            held[pl.ds(c * step + s, 2 * local, stride=per_period), :],
+                            held[pl.ds(c * step + s, local, stride=per_period), :],
+                            after[s // half, pl.ds(c * side + s % half, local, stride=half), :],
                             across[s // half, pl.ds(c * side + s % half, local, stride=half), :],
-                            held[
-                                pl.ds(c * step + 2 * height + s, local, stride=per_period), :
-                            ],
+                            held[pl.ds(c * step + height + s, local, stride=per_period), :],
                         ],
                         axis=0,
                     )
@@ -235,7 +234,8 @@
         in_specs=[pl.BlockSpec(memory_space=pltpu.SMEM)] + [VMEM] * 3 + [ANY] * len(blocks),
         out_specs=ANY,
         scratch_shapes=[
-            pltpu.VMEM((tiles * 3 * height, LANES), jnp.float32),
+            pltpu.VMEM((tiles * 2 * height, LANES), jnp.float32),
+            pltpu.VMEM((2, tiles * height // 2, LANES), jnp.float32),
             pltpu.VMEM((2, tiles * height // 2, LANES), jnp.float32),
             pltpu.VMEM((tiles * height, LANES), jnp.float32),
             pltpu.VMEM((periods, periods), jnp.float32),
@@ -266,26 +266,23 @@
     count = float(parts * layers * cells * lax.axis_size("z") * pairs)
     own = field.reshape(-1, cells)
 
-    def side(block, part, first, size):
-        block = block.reshape(field.shape)
-        return lax.dynamic_slice(
-            block, (first, part, 0, 0), (size, 1, layers, cells)
-        ).reshape(-1, cells)
-
-    sent = 1 - group // 2
+    def side(block, part):
+        part = lax.dynamic_index_in_dim(block.reshape(field.shape), part, 1, keepdims=False)
+        return part.reshape(-1, cells)
+
+    sent = (group + groups - 1) % groups // 2
     before = shift(own, 1)
-    top = shift(shift(side(own, sent, 0, local // 2), -1), -1)
-    bottom = shift(shift(side(own, sent, local // 2, local // 2), -1), -1)
-    rest = shift(side(before, 1 - (group + 1) % groups // 2, 0, local), 1)
-    source, top, bottom = lax.optimization_barrier((own, top, bottom))
-    after = shift(source, -1)
-    gram = gram_of(group, own, before, top, bottom, local, periods)
+    after = shift(side(own, sent), -1)
+    source, after = lax.optimization_barrier((own, after))
+    rest = [shift(side(source, 1 - sent), -1), shift(after, -1)]
+    gram = gram_of(group, own, before, after, local, periods)
+    rest.append(shift(side(before, group // 2), 1))
     pieces = lax.all_to_all(gram.reshape(pairs, -1, periods), PAIRS, 0, 0, tiled=True)
-    copies, rest = lax.optimization_barrier((copies_of(pieces, lax.axis_size("z")), rest))
+    copies = copies_of(pieces, lax.axis_size("z"))
     pieces = lax.all_to_all(copies, "z", 0, 0, tiled=True)
-    copies, after = lax.optimization_barrier((copies_of(pieces, groups * pairs), after))
+    copies, rest = lax.optimization_barrier((copies_of(pieces, groups * pairs), rest))
     raw = lax.all_to_all(copies, ("x",) + PAIRS, 0, 0, tiled=True).reshape(periods, periods)
-    blocks = [own, after, before, top, bottom, rest]
+    blocks = [own, before, after, *rest]
     result = project(raw, gain, start_basis, group, blocks, local, count)
     return result.reshape(field.shape)
 

time: 103 us -> 95 us (0.922)
  starting transfers between devices: 24.4 us -> 20 us
  blocking collectives: 55.2 us -> 52.1 us
  waiting for transfers between devices: 8.97 us -> 7.25 us
    all_to_all x1, blocking collectives: 17.5 us -> 12.7 us  [per_device(): lax.all_to_all(gram.reshape(pairs, -1, periods), PAIRS, 0, 0, tiled=True)]
    ppermute x7 -> x5, starting transfers between devices: 24.4 us -> 20 us  [shift(): lax.ppermute(value, 'x', [(i, (i + step) % count) for i in range(count)])]
    all_to_all x1, blocking collectives: 22.5 us -> 26.2 us  [per_device(): pieces = lax.all_to_all(copies, 'z', 0, 0, tiled=True)]
    all_to_all x1, blocking collectives: 15.1 us -> 13.2 us  [per_device(): lax.all_to_all(copies, ('x',) + PAIRS, 0, 0, tiled=True)]
    ppermute x7 -> x5, waiting for transfers between devices: 8.97 us -> 7.25 us  [shift(): lax.ppermute(value, 'x', [(i, (i + step) % count) for i in range(count)])]
    reshape x2 -> x3, local copies, waits for them, and re-layouts: 1.92 us -> 2.78 us  [side(): return part.reshape(-1, cells)]
  transfers between devices with their start and end apart: 7 -> 5, of which waited for: 3 -> 1; matrix products, arithmetic and copies ran while one was open for 2% -> 3% of each run, Pallas kernels for 2% -> 2%
where the time goes in v7:
time: 95 us; the launch traced here: 94.5 us
  blocking collectives  52.1 us (55%)
  starting transfers between devices  20 us (21%)
  Pallas kernels  11.5 us (12%)
  waiting for transfers between devices  7.25 us (8%)
  local copies, waits for them, and re-layouts  3.46 us (4%)
    all_to_all x1, blocking collectives, per_device(): pieces = lax.all_to_all(copies, 'z', 0, 0, tiled=True)  26.2 us
    ppermute x5, starting transfers between devices, shift(): lax.ppermute(value, 'x', [(i, (i + step) % count) for i in range(count)])  20 us
    all_to_all x1, blocking collectives, per_device(): lax.all_to_all(copies, ('x',) + PAIRS, 0, 0, tiled=True)  13.2 us
    all_to_all x1, blocking collectives, per_device(): lax.all_to_all(gram.reshape(pairs, -1, periods), PAIRS, 0, 0, tiled=True)  12.7 us
    pallas_call x1, Pallas kernels, project(): pl.pallas_call(functools.partial(project_kernel, count, local), out_shape...  9.85 us
    ppermute x5, waiting for transfers between devices, shift(): lax.ppermute(value, 'x', [(i, (i + step) % count) for i in range(count)])  7.25 us
    reshape x3, local copies, waits for them, and re-layouts, side(): return part.reshape(-1, cells)  2.78 us
  transfers between devices with their start and end apart: 5, of which 1 were waited for; matrix products, arithmetic and copies ran while one was open for 3% of the time, Pallas kernels for 2%

profile of v7, /device:TPU:1, one launch (start us, length us, event | category | flops | bytes accessed | tf_op | source)
XLA Modules:
  0.0 94.5 jit_solution(1795859345716281453)
XLA Ops:
  0.0 0.0 copy-start
  0.0 4.1 %collective-permute-start = (f32[512,512]{1,0:T(8,128)}, f32[512,512]{1,0:T(8,128)S(1)}, u32[]{:S(2)}, u32[]{:S(2)}) collective-permute-start(f32[512,512]{1,0:T(8,128)} %bitcast.19), channel_id=1, source_target_pairs={{0,1},{1,2},{2,3},{3,0},{4,5},{5,6},{6,7},{7,4},{8,9},{9,10},{10,1... | collective-permute-start | bytes 3145736 | tf_op jit(solution)/shard_map/ppermute | solution.py:252
  4.1 1.1 %dynamic-slice_bitcast_fusion.2 = f32[256,512]{1,0:T(8,128)S(1)} fusion(f32[32,2,8,512]{3,2,1,0:T(8,128)} %param.3, s32[]{:T(128)S(6)} %select_n.26), kind=kLoop, calls=%fused_computation.2 | loop fusion | bytes 1048580 | tf_op jit(solution)/shard_map/reshape | solution.py:271
  5.2 3.2 %collective-permute-start.1 = (f32[256,512]{1,0:T(8,128)S(1)}, f32[256,512]{1,0:T(8,128)S(1)}, u32[]{:S(2)}, u32[]{:S(2)}) collective-permute-start(f32[256,512]{1,0:T(8,128)S(1)} %dynamic-slice_bitcast_fusion.2), channel_id=1, source_target_pairs={{0,3},{1,0},{2,1},{3,2},{4,7},{5,4},{6,5},{7,6},{8,11},{9,8},{10,9... | collective-permute-start | bytes 1572872 | tf_op jit(solution)/shard_map/ppermute | solution.py:252
  8.4 7.2 %collective-permute-done.1.after_ref.refs_2_ = f32[256,512]{1,0:T(8,128)S(1)} collective-permute-done((f32[256,512]{1,0:T(8,128)S(1)}, f32[256,512]{1,0:T(8,128)S(1)}, u32[]{:S(2)}, u32[]{:S(2)}) %collective-permute-start.1) | collective-permute-done | bytes 524320 | tf_op jit(solution)/shard_map/ppermute | solution.py:252
  15.7 0.0 copy-done
  15.7 0.8 dynamic-slice_bitcast_fusion.1
  16.5 3.8 %collective-permute-start.2 = (f32[256,512]{1,0:T(8,128)}, f32[256,512]{1,0:T(8,128)S(1)}, u32[]{:S(2)}, u32[]{:S(2)}) collective-permute-start(f32[256,512]{1,0:T(8,128)} %dynamic-slice_bitcast_fusion.1), channel_id=1, source_target_pairs={{0,3},{1,0},{2,1},{3,2},{4,7},{5,4},{6,5},{7,6},{8,11},{9,8},{10,9... | collective-permute-start | bytes 1572872 | tf_op jit(solution)/shard_map/ppermute | solution.py:252
  20.4 4.9 %collective-permute-start.3 = (f32[256,512]{1,0:T(8,128)S(1)}, f32[256,512]{1,0:T(8,128)}, u32[]{:S(2)}, u32[]{:S(2)}) collective-permute-start(f32[256,512]{1,0:T(8,128)S(1)} %collective-permute-done.1.after_ref.refs_2_), channel_id=1, source_target_pairs={{0,3},{1,0},{2,1},{3,2},{4,7},{5,4},{6,5},{7,6},{8,11},{9,8},{10,9... | collective-permute-start | bytes 1572872 | tf_op jit(solution)/shard_map/ppermute | solution.py:252
  25.3 0.0 collective-permute-done.before_ref.refs_1_
  25.3 0.9 dynamic-slice_bitcast_fusion
  26.2 4.0 %collective-permute-start.4 = (f32[256,512]{1,0:T(8,128)}, f32[256,512]{1,0:T(8,128)}, u32[]{:S(2)}, u32[]{:S(2)}) collective-permute-start(f32[256,512]{1,0:T(8,128)} %dynamic-slice_bitcast_fusion), channel_id=1, source_target_pairs={{0,1},{1,2},{2,3},{3,0},{4,5},{5,6},{6,7},{7,4},{8,9},{9,10},{10,1... | collective-permute-start | bytes 1572872 | tf_op jit(solution)/shard_map/ppermute | solution.py:252
  30.2 1.7 %gram.1 = f32[32,128]{1,0:T(8,128)S(1)} custom-call(s32[1]{0:T(128)} %bitcast.group_ref, f32[512,512]{1,0:T(8,128)S(1)} %bitcast.20, f32[512,512]{1,0:T(8,128)S(1)} %collective-permute-done.before_ref.refs_1_, f32[256,512]{1,0:T(8,128)S(1)} %collective-permute-done.1.after_ref.refs_2_), custom_call_target="tpu_custom_call" | custom-call | tf_op jit(solution)/shard_map/gram/pallas_call | solution.py:96
  31.9 12.7 %all_to_all.15 = f32[8,4,128]{2,1,0:T(4,128)S(1)} all-to-all(f32[8,4,128]{2,1,0:T(4,128)S(1)} %bitcast.24), channel_id=1, replica_groups=mesh['y'=4,'z'=16,'c'=2,'x'=4] {'y','c'}, dimensions={0} | all-to-all | bytes 32768 | tf_op jit(solution)/shard_map/all_to_all | solution.py:280
  44.6 26.2 %all_to_all.16 = f32[16,4,128]{2,1,0:T(4,128)S(1)} all-to-all(f32[16,4,128]{2,1,0:T(4,128)S(1)} %broadcast_in_dim.9), channel_id=1, replica_groups=mesh['y'=4,'z'=16,'c'=2,'x'=4] {'z'}, dimensions={0} | all-to-all | bytes 65536 | tf_op jit(solution)/shard_map/all_to_all | solution.py:282
  70.8 0.0 collective-permute-done.2.refs_3_
  70.8 0.0 collective-permute-done.3.refs_4_
  70.8 0.0 collective-permute-done.4.refs_5_
  70.8 0.0 copy-start.1
  70.8 13.2 %all_to_all.17 = f32[32,4,128]{2,1,0:T(4,128)S(1)} all-to-all(f32[32,4,128]{2,1,0:T(4,128)S(1)} %broadcast_in_dim.10), channel_id=1, replica_groups=mesh['y'=4,'z'=16,'c'=2,'x'=4] {'x','y','c'}, dimensions={0} | all-to-all | bytes 131072 | tf_op jit(solution)/shard_map/all_to_all | solution.py:284
  84.0 0.0 copy-start.2
  84.0 0.0 copy-done.1
  84.0 0.7 copy-done.2
  84.7 9.8 %project.1 = f32[512,512]{1,0:T(8,128)} custom-call(s32[1]{0:T(128)} %bitcast.group_ref, f32[128,128]{1,0:T(8,128)S(1)} %bitcast.23, f32[1,128]{1,0:T(1,128)S(1)} %bitcast.26, f32[32,128]{1,0:T(8,128)S(1)} %bitcast.25, f32[512,512]{1,0:T(8,128)S(1)} %bitcast.21, f32[512,512]{1,0:T(8,128)S(1)} %collective-permute-done.before_ref.refs_1_, ...), custom_call_target="tpu_custom_call" | custom-call | tf_op jit(solution)/shard_map/project/pallas_call | solution.py:231
  (4 shorter events, 0.1 us)
Async XLA Ops:
  0.0 15.7 %copy-start = (f32[32,2,8,512]{3,2,1,0:T(8,128)S(1)}, f32[32,2,8,512]{3,2,1,0:T(8,128)}, u32[]{:S(2)}) copy-start(f32[32,2,8,512]{3,2,1,0:T(8,128)} %param.3) | copy-start | bytes 3145732
  0.0 25.3 %collective-permute-start = (f32[512,512]{1,0:T(8,128)}, f32[512,512]{1,0:T(8,128)S(1)}, u32[]{:S(2)}, u32[]{:S(2)}) collective-permute-start(f32[512,512]{1,0:T(8,128)} %bitcast.19), channel_id=1, source_target_pairs={{0,1},{1,2},{2,3},{3,0},{4,5},{5,6},{6,7},{7,4},{8,9},{9,10},{10,1... | collective-permute-start | bytes 3145736 | tf_op jit(solution)/shard_map/ppermute | solution.py:252
  5.2 10.5 %collective-permute-start.1 = (f32[256,512]{1,0:T(8,128)S(1)}, f32[256,512]{1,0:T(8,128)S(1)}, u32[]{:S(2)}, u32[]{:S(2)}) collective-permute-start(f32[256,512]{1,0:T(8,128)S(1)} %dynamic-slice_bitcast_fusion.2), channel_id=1, source_target_pairs={{0,3},{1,0},{2,1},{3,2},{4,7},{5,4},{6,5},{7,6},{8,11},{9,8},{10,9... | collective-permute-start | bytes 1572872 | tf_op jit(solution)/shard_map/ppermute | solution.py:252
  16.5 54.3 %collective-permute-start.2 = (f32[256,512]{1,0:T(8,128)}, f32[256,512]{1,0:T(8,128)S(1)}, u32[]{:S(2)}, u32[]{:S(2)}) collective-permute-start(f32[256,512]{1,0:T(8,128)} %dynamic-slice_bitcast_fusion.1), channel_id=1, source_target_pairs={{0,3},{1,0},{2,1},{3,2},{4,7},{5,4},{6,5},{7,6},{8,11},{9,8},{10,9... | collective-permute-start | bytes 1572872 | tf_op jit(solution)/shard_map/ppermute | solution.py:252
  20.4 50.4 %collective-permute-start.3 = (f32[256,512]{1,0:T(8,128)S(1)}, f32[256,512]{1,0:T(8,128)}, u32[]{:S(2)}, u32[]{:S(2)}) collective-permute-start(f32[256,512]{1,0:T(8,128)S(1)} %collective-permute-done.1.after_ref.refs_2_), channel_id=1, source_target_pairs={{0,3},{1,0},{2,1},{3,2},{4,7},{5,4},{6,5},{7,6},{8,11},{9,8},{10,9... | collective-permute-start | bytes 1572872 | tf_op jit(solution)/shard_map/ppermute | solution.py:252
  26.2 44.6 %collective-permute-start.4 = (f32[256,512]{1,0:T(8,128)}, f32[256,512]{1,0:T(8,128)}, u32[]{:S(2)}, u32[]{:S(2)}) collective-permute-start(f32[256,512]{1,0:T(8,128)} %dynamic-slice_bitcast_fusion), channel_id=1, source_target_pairs={{0,1},{1,2},{2,3},{3,0},{4,5},{5,6},{6,7},{7,4},{8,9},{9,10},{10,1... | collective-permute-start | bytes 1572872 | tf_op jit(solution)/shard_map/ppermute | solution.py:252
  70.8 13.2 %copy-start.1 = (f32[128,32]{0,1:T(8,128)S(1)}, f32[128,32]{0,1:T(8,128)}, u32[]{:S(2)}) copy-start(f32[128,32]{0,1:T(8,128)} %param.5) | copy-start | bytes 49156
  84.0 0.7 copy-start.2

commit v8 on v7

--- a/solution.py
+++ b/solution.py
@@ -54,12 +54,12 @@
     return high + low
 
 
-def gram_kernel(local, group_ref, own_ref, before_ref, after_ref, out_ref, *scratch):
-    own, before, after, sems = scratch
+def gram_kernel(local, group_ref, own_ref, *refs):
+    blocks, (out_ref, own, *held, sems) = refs[:3], refs[3:]
     tiles = own_ref.shape[1] // LANES
-    copies = []
-    for i, (block, held) in enumerate(((own_ref, own), (before_ref, before), (after_ref, after))):
-        copies += tile_copies(block, held, 0, sems, i * tiles)
+    copies = tile_copies(own_ref, own, 0, sems, 0)
+    for i, block in enumerate(blocks):
+        copies += tile_copies(block, held[i], 0, sems, (i + 1) * tiles)
     for copy in copies:
         copy.start()
     for copy in copies:
@@ -69,16 +69,16 @@
     second = group_ref[0] >= 2
     near, far = None, None
     for s in range(half):
-        left = [lines(before, tiles, s + t * half, local, per_period) for t in range(2)]
-        for t in range(2):
-            mine = halves(lines(own, tiles, s + t * half, local, per_period))
-            both = jnp.concatenate(mine + halves(left[t]), axis=0)
-            part = dot(jnp.concatenate(mine, axis=0), both, 1, 1, None)
-            near = part if near is None else near + part
-        right = jnp.concatenate(halves(lines(after, tiles, s, local, half)), axis=0)
-        left = jnp.concatenate(halves(jnp.where(second, left[1], left[0])), axis=0)
-        part = dot(left, right, 1, 1, None)
-        far = part if far is None else far + part
+        parts = [lines(own, tiles, s + t * half, local, per_period) for t in range(2)]
+        parts = [jnp.where(second, parts[1 - t], parts[t]) for t in range(2)]
+        first, other, after = (halves(lines(block, tiles, s, local, half)) for block in held)
+        for part, before in zip(parts, (first, other)):
+            mine = halves(part)
+            both = jnp.concatenate(mine + before, axis=0)
+            product = dot(jnp.concatenate(mine, axis=0), both, 1, 1, None)
+            near = product if near is None else near + product
+        product = dot(jnp.concatenate(first, axis=0), jnp.concatenate(after, axis=0), 1, 1, None)
+        far = product if far is None else far + product
     out_ref[...] = jnp.concatenate(
         [
             fold(near, local, 0),
@@ -90,23 +90,20 @@
     )
 
 
-def gram_of(group, own, before, after, local, periods):
+def gram_of(group, own, blocks, local, periods):
     shape = (own.shape[0] * own.shape[1] // LANES, LANES)
     tiles = own.shape[1] // LANES
     return pl.pallas_call(
         functools.partial(gram_kernel, local),
         out_shape=jax.ShapeDtypeStruct((local, periods), jnp.float32),
-        in_specs=[pl.BlockSpec(memory_space=pltpu.SMEM)] + [ANY] * 3,
+        in_specs=[pl.BlockSpec(memory_space=pltpu.SMEM)] + [ANY] * 4,
         out_specs=VMEM,
-        scratch_shapes=[
-            pltpu.VMEM(shape, jnp.float32),
-            pltpu.VMEM(shape, jnp.float32),
-            pltpu.VMEM((shape[0] // 2, LANES), jnp.float32),
-            pltpu.SemaphoreType.DMA((3 * tiles,)),
-        ],
+        scratch_shapes=[pltpu.VMEM(shape, jnp.float32)]
+        + [pltpu.VMEM((shape[0] // 2, LANES), jnp.float32)] * 3
+        + [pltpu.SemaphoreType.DMA((4 * tiles,))],
         compiler_params=pltpu.CompilerParams(vmem_limit_bytes=32 * 2**20),
         name="gram",
-    )(group[None], own, before, after)
+    )(group[None], own, *blocks)
 
 
 def assemble(parts, local):
@@ -146,22 +143,23 @@
     return work[:, rank:] * lax.rsqrt(pivots[:, rank:])
 
 
-def project_kernel(count, local, group_ref, raw_ref, gain_ref, start_ref, *refs):
-    own_ref, before_ref, *split_refs = refs[:6]
-    out_ref, held, after, across, ready, full_ref, in_sems, out_sems = refs[6:]
+def project_kernel(count, local, group_ref, raw_ref, start_ref, *refs):
+    own_ref, *split_refs = refs[:7]
+    out_ref, held, after, across, before, ready, full_ref, in_sems, out_sems = refs[7:]
     height, cells = out_ref.shape
     tiles = cells // LANES
     group = group_ref[0]
     second = jnp.where(group >= 2, 1, 0)
     later = jnp.where((group == 1) | (group == 2), 1, 0)
     fetches = tile_copies(own_ref, held, 0, in_sems, 0)
-    fetches += tile_copies(before_ref, held, height, in_sems, tiles)
-    places = (after.at[second], after.at[1 - second], across.at[later], across.at[1 - later])
+    ends = ((after, second), (across, later), (before, second))
+    places = [place.at[end] for place, first in ends for end in (first, 1 - first)]
     for i, (block, place) in enumerate(zip(split_refs, places)):
-        fetches += tile_copies(block, place, 0, in_sems, (2 + i) * tiles)
+        fetches += tile_copies(block, place, 0, in_sems, (1 + i) * tiles)
     for fetch in fetches:
         fetch.start()
-    gain = gain_ref[...]
+    rank = start_ref.shape[0] - 1
+    gain = start_ref[rank:]
     periods = gain.shape[1]
     per_period = height // local
     half = per_period // 2
@@ -170,7 +168,7 @@
     def grow(basis):
         return dot(basis * gain, raw, 1, 0) * (gain * (1.0 / count))
 
-    grown = grow(start_ref[...])
+    grown = grow(start_ref[:rank])
     for _ in range(ITERS - 1):
         later = grow(grown)
         grown = dot(inverse_factor(dot(grown, grown, 1, 1)), later, 1, 0)
@@ -195,9 +193,10 @@
                     jnp.concatenate(
                         [
                             held[pl.ds(c * step + s, local, stride=per_period), :],
-                            after[s // half, pl.ds(c * side + s % half, local, stride=half), :],
-                            across[s // half, pl.ds(c * side + s % half, local, stride=half), :],
-                            held[pl.ds(c * step + height + s, local, stride=per_period), :],
+                            *(
+                                split[s // half, pl.ds(c * side + s % half, local, stride=half), :]
+                                for split in (after, across, before)
+                            ),
                         ],
                         axis=0,
                     )
@@ -224,19 +223,18 @@
         send.wait()
 
 
-def project(raw, gain, start_basis, group, blocks, local, count):
+def project(raw, start, group, blocks, local, count):
     height, cells = blocks[0].shape
-    periods = gain.shape[0]
+    periods = start.shape[1]
     tiles = cells // LANES
     return pl.pallas_call(
         functools.partial(project_kernel, count, local),
         out_shape=jax.ShapeDtypeStruct((height, cells), jnp.float32),
-        in_specs=[pl.BlockSpec(memory_space=pltpu.SMEM)] + [VMEM] * 3 + [ANY] * len(blocks),
+        in_specs=[pl.BlockSpec(memory_space=pltpu.SMEM)] + [VMEM] * 2 + [ANY] * len(blocks),
         out_specs=ANY,
-        scratch_shapes=[
-            pltpu.VMEM((tiles * 2 * height, LANES), jnp.float32),
-            pltpu.VMEM((2, tiles * height // 2, LANES), jnp.float32),
-            pltpu.VMEM((2, tiles * height // 2, LANES), jnp.float32),
+        scratch_shapes=[pltpu.VMEM((tiles * height, LANES), jnp.float32)]
+        + [pltpu.VMEM((2, tiles * height // 2, LANES), jnp.float32)] * 3
+        + [
             pltpu.VMEM((tiles * height, LANES), jnp.float32),
             pltpu.VMEM((periods, periods), jnp.float32),
             pltpu.SemaphoreType.DMA((len(blocks) * tiles,)),
@@ -244,7 +242,7 @@
         ],
         compiler_params=pltpu.CompilerParams(vmem_limit_bytes=32 * 2**20),
         name="project",
-    )(group[None], raw, gain[None, :], start_basis.T, *blocks)
+    )(group[None], raw, start, *blocks)
 
 
 def shift(value, step):
@@ -271,19 +269,23 @@
         return part.reshape(-1, cells)
 
     sent = (group + groups - 1) % groups // 2
-    before = shift(own, 1)
-    after = shift(side(own, sent), -1)
-    source, after = lax.optimization_barrier((own, after))
-    rest = [shift(side(source, 1 - sent), -1), shift(after, -1)]
-    gram = gram_of(group, own, before, after, local, periods)
-    rest.append(shift(side(before, group // 2), 1))
+    start = jnp.concatenate([start_basis.T, gain[None]], axis=0)
+    one = side(own, 1 - sent)
+    first = shift(one, 1)
+    two = side(own, sent)
+    after = shift(two, -1)
+    second = shift(two, 1)
+    first, start = lax.optimization_barrier((first, start))
+    one, after, _ = lax.optimization_barrier((one, after, first))
+    rest = [shift(one, -1), shift(after, -1), shift(first, 1)]
+    gram = gram_of(group, own, [first, second, after], local, periods)
     pieces = lax.all_to_all(gram.reshape(pairs, -1, periods), PAIRS, 0, 0, tiled=True)
     copies = copies_of(pieces, lax.axis_size("z"))
     pieces = lax.all_to_all(copies, "z", 0, 0, tiled=True)
     copies, rest = lax.optimization_barrier((copies_of(pieces, groups * pairs), rest))
     raw = lax.all_to_all(copies, ("x",) + PAIRS, 0, 0, tiled=True).reshape(periods, periods)
-    blocks = [own, before, after, *rest]
-    result = project(raw, gain, start_basis, group, blocks, local, count)
+    blocks = [own, after, *rest, first, second]
+    result = project(raw, start, group, blocks, local, count)
     return result.reshape(field.shape)
 
 

time: 95 us -> 92 us (0.968)
  waiting for transfers between devices: 7.25 us -> 4.51 us
  blocking collectives: 52.1 us -> 53.4 us
  Pallas kernels: 11.5 us -> 10.4 us
    ppermute x5 -> x6, waiting for transfers between devices: 7.25 us -> 4.51 us  [shift(): lax.ppermute(value, 'x', [(i, (i + step) % count) for i in range(count)])]
    all_to_all x1, blocking collectives: 12.7 us -> 14.4 us  [per_device(): lax.all_to_all(gram.reshape(pairs, -1, periods), PAIRS, 0, 0, tiled=True)]
    pallas_call x1, Pallas kernels: 9.85 us -> 8.72 us  [project(): pl.pallas_call(functools.partial(project_kernel, count, local), out_shape...]
    reshape x3 -> x1, local copies, waits for them, and re-layouts: 2.78 us -> 2.15 us  [side(): return part.reshape(-1, cells)]
    ppermute x5 -> x6, starting transfers between devices: 20 us -> 20.2 us  [shift(): lax.ppermute(value, 'x', [(i, (i + step) % count) for i in range(count)])]
  transfers between devices with their start and end apart: 5 -> 6, of which waited for: 1 -> 2; matrix products, arithmetic and copies ran while one was open for 3% -> 0% of each run, Pallas kernels for 2% -> 2%
where the time goes in v8:
time: 92 us; the launch traced here: 91.6 us
  blocking collectives  53.4 us (58%)
  starting transfers between devices  20.2 us (22%)
  Pallas kernels  10.4 us (11%)
  waiting for transfers between devices  4.51 us (5%)
  local copies, waits for them, and re-layouts  2.82 us (3%)
    all_to_all x1, blocking collectives, per_device(): pieces = lax.all_to_all(copies, 'z', 0, 0, tiled=True)  26.2 us
    ppermute x6, starting transfers between devices, shift(): lax.ppermute(value, 'x', [(i, (i + step) % count) for i in range(count)])  20.2 us
    all_to_all x1, blocking collectives, per_device(): lax.all_to_all(gram.reshape(pairs, -1, periods), PAIRS, 0, 0, tiled=True)  14.4 us
    all_to_all x1, blocking collectives, per_device(): lax.all_to_all(copies, ('x',) + PAIRS, 0, 0, tiled=True)  12.8 us
    pallas_call x1, Pallas kernels, project(): pl.pallas_call(functools.partial(project_kernel, count, local), out_shape...  8.72 us
    ppermute x6, waiting for transfers between devices, shift(): lax.ppermute(value, 'x', [(i, (i + step) % count) for i in range(count)])  4.51 us
    reshape x1, local copies, waits for them, and re-layouts, side(): return part.reshape(-1, cells)  2.15 us
  transfers between devices with their start and end apart: 6, of which 2 were waited for; matrix products, arithmetic and copies ran while one was open for 0% of the time, Pallas kernels for 2%

profile of v8, /device:TPU:1, one launch (start us, length us, event | category | flops | bytes accessed | tf_op | source)
XLA Modules:
  0.0 91.6 jit_solution(9617193065562480575)
XLA Ops:
  0.0 0.0 copy-start.1
  0.0 0.0 copy-start
  0.0 2.1 %dynamic-slice_bitcast_fusion = (f32[256,512]{1,0:T(8,128)S(1)}, f32[256,512]{1,0:T(8,128)}) fusion(f32[32,2,8,512]{3,2,1,0:T(8,128)} %param.3, s32[]{:T(128)S(6)} %select_n.21, s32[]{:T(128)S(6)} %select_n.20), kind=kLoop, calls=%fused_computation | loop fusion | bytes 2097160 | tf_op jit(solution)/shard_map/reshape | solution.py:269
  2.2 3.9 %collective-permute-start = (f32[256,512]{1,0:T(8,128)}, f32[256,512]{1,0:T(8,128)S(1)}, u32[]{:S(2)}, u32[]{:S(2)}) collective-permute-start(f32[256,512]{1,0:T(8,128)} %get-tuple-element.15), channel_id=1, source_target_pairs={{0,1},{1,2},{2,3},{3,0},{4,5},{5,6},{6,7},{7,4},{8,9},{9,10},{10,1... | collective-permute-start | bytes 1572872 | tf_op jit(solution)/shard_map/ppermute | solution.py:250
  6.1 3.2 %collective-permute-start.2 = (f32[256,512]{1,0:T(8,128)S(1)}, f32[256,512]{1,0:T(8,128)S(1)}, u32[]{:S(2)}, u32[]{:S(2)}) collective-permute-start(f32[256,512]{1,0:T(8,128)S(1)} %get-tuple-element.21), channel_id=1, source_target_pairs={{0,3},{1,0},{2,1},{3,2},{4,7},{5,4},{6,5},{7,6},{8,11},{9,8},{10,9... | collective-permute-start | bytes 1572872 | tf_op jit(solution)/shard_map/ppermute | solution.py:250
  9.3 2.1 %collective-permute-start.1 = (f32[256,512]{1,0:T(8,128)S(1)}, f32[256,512]{1,0:T(8,128)S(1)}, u32[]{:S(2)}, u32[]{:S(2)}) collective-permute-start(f32[256,512]{1,0:T(8,128)S(1)} %get-tuple-element.21), channel_id=1, source_target_pairs={{0,1},{1,2},{2,3},{3,0},{4,5},{5,6},{6,7},{7,4},{8,9},{9,10},{10,1... | collective-permute-start | bytes 1572872 | tf_op jit(solution)/shard_map/ppermute | solution.py:250
  11.4 0.0 copy-start.2
  11.4 0.0 copy-done.1
  11.4 0.6 copy-done.2
  12.1 2.1 %collective-permute-done.refs_0_.refs_5_ = f32[256,512]{1,0:T(8,128)S(1)} collective-permute-done((f32[256,512]{1,0:T(8,128)}, f32[256,512]{1,0:T(8,128)S(1)}, u32[]{:S(2)}, u32[]{:S(2)}) %collective-permute-start) | collective-permute-done | bytes 524320 | tf_op jit(solution)/shard_map/ppermute | solution.py:250
  14.1 2.4 %collective-permute-done.2.refs_2_.refs_1_ = f32[256,512]{1,0:T(8,128)S(1)} collective-permute-done((f32[256,512]{1,0:T(8,128)S(1)}, f32[256,512]{1,0:T(8,128)S(1)}, u32[]{:S(2)}, u32[]{:S(2)}) %collective-permute-start.2) | collective-permute-done | bytes 524320 | tf_op jit(solution)/shard_map/ppermute | solution.py:250
  16.6 5.7 %collective-permute-start.3 = (f32[256,512]{1,0:T(8,128)}, f32[256,512]{1,0:T(8,128)S(1)}, u32[]{:S(2)}, u32[]{:S(2)}) collective-permute-start(f32[256,512]{1,0:T(8,128)} %get-tuple-element.15), channel_id=1, source_target_pairs={{0,3},{1,0},{2,1},{3,2},{4,7},{5,4},{6,5},{7,6},{8,11},{9,8},{10,9... | collective-permute-start | bytes 1572872 | tf_op jit(solution)/shard_map/ppermute | solution.py:250
  22.3 3.1 %collective-permute-start.4 = (f32[256,512]{1,0:T(8,128)S(1)}, f32[256,512]{1,0:T(8,128)}, u32[]{:S(2)}, u32[]{:S(2)}) collective-permute-start(f32[256,512]{1,0:T(8,128)S(1)} %collective-permute-done.2.refs_2_.refs_1_), channel_id=1, source_target_pairs={{0,3},{1,0},{2,1},{3,2},{4,7},{5,4},{6,5},{7,6},{8,11},{9,8},{10,9... | collective-permute-start | bytes 1572872 | tf_op jit(solution)/shard_map/ppermute | solution.py:250
  25.4 2.2 %collective-permute-start.5 = (f32[256,512]{1,0:T(8,128)S(1)}, f32[256,512]{1,0:T(8,128)}, u32[]{:S(2)}, u32[]{:S(2)}) collective-permute-start(f32[256,512]{1,0:T(8,128)S(1)} %collective-permute-done.refs_0_.refs_5_), channel_id=1, source_target_pairs={{0,1},{1,2},{2,3},{3,0},{4,5},{5,6},{6,7},{7,4},{8,9},{9,10},{10,1... | collective-permute-start | bytes 1572872 | tf_op jit(solution)/shard_map/ppermute | solution.py:250
  27.6 0.0 collective-permute-done.1.refs_1_.refs_6_
  27.6 0.0 copy-done
  27.6 1.7 %gram.1 = f32[32,128]{1,0:T(8,128)S(1)} custom-call(s32[1]{0:T(128)} %bitcast.group_ref, f32[512,512]{1,0:T(8,128)S(1)} %bitcast.11, f32[256,512]{1,0:T(8,128)S(1)} %collective-permute-done.refs_0_.refs_5_, f32[256,512]{1,0:T(8,128)S(1)} %collective-permute-done.1.refs_1_.refs_6_, f32[256,512]{1,0:T(8,128)S(1)} %collective-permute-done.2.refs_2_.refs_1_), custom_call_target="tpu_custom_call" | custom-call | tf_op jit(solution)/shard_map/gram/pallas_call | solution.py:96
  29.3 14.4 %all_to_all.15 = f32[8,4,128]{2,1,0:T(4,128)S(1)} all-to-all(f32[8,4,128]{2,1,0:T(4,128)S(1)} %bitcast.14), channel_id=1, replica_groups=mesh['y'=4,'z'=16,'c'=2,'x'=4] {'y','c'}, dimensions={0} | all-to-all | bytes 32768 | tf_op jit(solution)/shard_map/all_to_all | solution.py:282
  43.8 26.2 %all_to_all.16 = f32[16,4,128]{2,1,0:T(4,128)S(1)} all-to-all(f32[16,4,128]{2,1,0:T(4,128)S(1)} %broadcast_in_dim.10), channel_id=1, replica_groups=mesh['y'=4,'z'=16,'c'=2,'x'=4] {'z'}, dimensions={0} | all-to-all | bytes 65536 | tf_op jit(solution)/shard_map/all_to_all | solution.py:284
  70.1 0.0 collective-permute-done.3.refs_2_
  70.1 0.0 collective-permute-done.4.refs_3_
  70.1 0.0 collective-permute-done.5.refs_4_
  70.1 12.8 %all_to_all.17 = f32[32,4,128]{2,1,0:T(4,128)S(1)} all-to-all(f32[32,4,128]{2,1,0:T(4,128)S(1)} %broadcast_in_dim.22), channel_id=1, replica_groups=mesh['y'=4,'z'=16,'c'=2,'x'=4] {'x','y','c'}, dimensions={0} | all-to-all | bytes 131072 | tf_op jit(solution)/shard_map/all_to_all | solution.py:286
  82.8 8.7 %project.1 = f32[512,512]{1,0:T(8,128)} custom-call(s32[1]{0:T(128)} %bitcast.group_ref, f32[128,128]{1,0:T(8,128)S(1)} %bitcast.13, f32[33,128]{1,0:T(8,128)S(1)} %pad_maximum_fusion.start_ref, f32[512,512]{1,0:T(8,128)S(1)} %bitcast.12, f32[256,512]{1,0:T(8,128)S(1)} %collective-permute-done.2.refs_2_.refs_1_, ...), custom_call_target="tpu_custom_call" | custom-call | tf_op jit(solution)/shard_map/project/pallas_call | solution.py:230
  (5 shorter events, 0.1 us)
Async XLA Ops:
  0.0 11.4 %copy-start.1 = (f32[128,32]{0,1:T(8,128)S(1)}, f32[128,32]{0,1:T(8,128)}, u32[]{:S(2)}) copy-start(f32[128,32]{0,1:T(8,128)} %param.5) | copy-start | bytes 49156
  0.0 27.6 %copy-start = (f32[32,2,8,512]{3,2,1,0:T(8,128)S(1)}, f32[32,2,8,512]{3,2,1,0:T(8,128)}, u32[]{:S(2)}) copy-start(f32[32,2,8,512]{3,2,1,0:T(8,128)} %param.3) | copy-start | bytes 3145732
  2.2 12.0 %collective-permute-start = (f32[256,512]{1,0:T(8,128)}, f32[256,512]{1,0:T(8,128)S(1)}, u32[]{:S(2)}, u32[]{:S(2)}) collective-permute-start(f32[256,512]{1,0:T(8,128)} %get-tuple-element.15), channel_id=1, source_target_pairs={{0,1},{1,2},{2,3},{3,0},{4,5},{5,6},{6,7},{7,4},{8,9},{9,10},{10,1... | collective-permute-start | bytes 1572872 | tf_op jit(solution)/shard_map/ppermute | solution.py:250
  6.1 10.5 %collective-permute-start.2 = (f32[256,512]{1,0:T(8,128)S(1)}, f32[256,512]{1,0:T(8,128)S(1)}, u32[]{:S(2)}, u32[]{:S(2)}) collective-permute-start(f32[256,512]{1,0:T(8,128)S(1)} %get-tuple-element.21), channel_id=1, source_target_pairs={{0,3},{1,0},{2,1},{3,2},{4,7},{5,4},{6,5},{7,6},{8,11},{9,8},{10,9... | collective-permute-start | bytes 1572872 | tf_op jit(solution)/shard_map/ppermute | solution.py:250
  9.3 18.3 %collective-permute-start.1 = (f32[256,512]{1,0:T(8,128)S(1)}, f32[256,512]{1,0:T(8,128)S(1)}, u32[]{:S(2)}, u32[]{:S(2)}) collective-permute-start(f32[256,512]{1,0:T(8,128)S(1)} %get-tuple-element.21), channel_id=1, source_target_pairs={{0,1},{1,2},{2,3},{3,0},{4,5},{5,6},{6,7},{7,4},{8,9},{9,10},{10,1... | collective-permute-start | bytes 1572872 | tf_op jit(solution)/shard_map/ppermute | solution.py:250
  11.4 0.7 copy-start.2
  16.6 53.5 %collective-permute-start.3 = (f32[256,512]{1,0:T(8,128)}, f32[256,512]{1,0:T(8,128)S(1)}, u32[]{:S(2)}, u32[]{:S(2)}) collective-permute-start(f32[256,512]{1,0:T(8,128)} %get-tuple-element.15), channel_id=1, source_target_pairs={{0,3},{1,0},{2,1},{3,2},{4,7},{5,4},{6,5},{7,6},{8,11},{9,8},{10,9... | collective-permute-start | bytes 1572872 | tf_op jit(solution)/shard_map/ppermute | solution.py:250
  22.3 47.8 %collective-permute-start.4 = (f32[256,512]{1,0:T(8,128)S(1)}, f32[256,512]{1,0:T(8,128)}, u32[]{:S(2)}, u32[]{:S(2)}) collective-permute-start(f32[256,512]{1,0:T(8,128)S(1)} %collective-permute-done.2.refs_2_.refs_1_), channel_id=1, source_target_pairs={{0,3},{1,0},{2,1},{3,2},{4,7},{5,4},{6,5},{7,6},{8,11},{9,8},{10,9... | collective-permute-start | bytes 1572872 | tf_op jit(solution)/shard_map/ppermute | solution.py:250
  25.4 44.7 %collective-permute-start.5 = (f32[256,512]{1,0:T(8,128)S(1)}, f32[256,512]{1,0:T(8,128)}, u32[]{:S(2)}, u32[]{:S(2)}) collective-permute-start(f32[256,512]{1,0:T(8,128)S(1)} %collective-permute-done.refs_0_.refs_5_), channel_id=1, source_target_pairs={{0,1},{1,2},{2,3},{3,0},{4,5},{5,6},{6,7},{7,4},{8,9},{9,10},{10,1... | collective-permute-start | bytes 1572872 | tf_op jit(solution)/shard_map/ppermute | solution.py:250

commit v9 on v8

--- a/solution.py
+++ b/solution.py
@@ -8,7 +8,7 @@
 from jax.sharding import Mesh, PartitionSpec as P
 
 ITERS = 3
-PIVOTS = 4
+PIVOTS = 16
 LANES = 128
 HIGH = lax.Precision.HIGHEST
 PAIRS = ("y", "c")
@@ -271,8 +271,9 @@
     sent = (group + groups - 1) % groups // 2
     start = jnp.concatenate([start_basis.T, gain[None]], axis=0)
     one = side(own, 1 - sent)
+    source, one = lax.optimization_barrier((own, one))
     first = shift(one, 1)
-    two = side(own, sent)
+    two = side(source, sent)
     after = shift(two, -1)
     second = shift(two, 1)
     first, start = lax.optimization_barrier((first, start))

time: 92 us -> 89.3 us (0.971)
  Pallas kernels: 10.4 us -> 8.68 us
  local copies, waits for them, and re-layouts: 2.82 us -> 1.89 us
    pallas_call x1, Pallas kernels: 8.72 us -> 6.95 us  [project(): pl.pallas_call(functools.partial(project_kernel, count, local), out_shape...]
    reshape x1 -> x2, local copies, waits for them, and re-layouts: 2.15 us -> 1.21 us  [side(): return part.reshape(-1, cells)]
where the time goes in v9:
time: 89.3 us; the launch traced here: 88.9 us
  blocking collectives  53.5 us (60%)
  starting transfers between devices  20.1 us (23%)
  Pallas kernels  8.68 us (10%)
  waiting for transfers between devices  4.51 us (5%)
  local copies, waits for them, and re-layouts  1.89 us (2%)
    all_to_all x1, blocking collectives, per_device(): pieces = lax.all_to_all(copies, 'z', 0, 0, tiled=True)  26.3 us
    ppermute x6, starting transfers between devices, shift(): lax.ppermute(value, 'x', [(i, (i + step) % count) for i in range(count)])  20.1 us
    all_to_all x1, blocking collectives, per_device(): lax.all_to_all(gram.reshape(pairs, -1, periods), PAIRS, 0, 0, tiled=True)  14.5 us
    all_to_all x1, blocking collectives, per_device(): lax.all_to_all(copies, ('x',) + PAIRS, 0, 0, tiled=True)  12.8 us
    pallas_call x1, Pallas kernels, project(): pl.pallas_call(functools.partial(project_kernel, count, local), out_shape...  6.95 us
    ppermute x6, waiting for transfers between devices, shift(): lax.ppermute(value, 'x', [(i, (i + step) % count) for i in range(count)])  4.51 us
  transfers between devices with their start and end apart: 6, of which 2 were waited for; matrix products, arithmetic and copies ran while one was open for 0% of the time, Pallas kernels for 2%

profile of v9, /device:TPU:1, one launch (start us, length us, event | category | flops | bytes accessed | tf_op | source)
XLA Modules:
  0.0 88.9 jit_solution(4590748544274653074)
XLA Ops:
  0.0 0.0 copy-start
  0.0 1.2 %dynamic-slice_bitcast_fusion.1 = f32[256,512]{1,0:T(8,128)S(1)} fusion(f32[32,2,8,512]{3,2,1,0:T(8,128)} %param.3, s32[]{:T(128)S(6)} %select_n.20), kind=kLoop, calls=%fused_computation.1 | loop fusion | bytes 1048580 | tf_op jit(solution)/shard_map/reshape | solution.py:269
  1.2 0.0 copy-start.1
  1.2 3.9 %collective-permute-start = (f32[256,512]{1,0:T(8,128)S(1)}, f32[256,512]{1,0:T(8,128)S(1)}, u32[]{:S(2)}, u32[]{:S(2)}) collective-permute-start(f32[256,512]{1,0:T(8,128)S(1)} %dynamic-slice_bitcast_fusion.1), channel_id=1, source_target_pairs={{0,1},{1,2},{2,3},{3,0},{4,5},{5,6},{6,7},{7,4},{8,9},{9,10},{10,1... | collective-permute-start | bytes 1572872 | tf_op jit(solution)/shard_map/ppermute | solution.py:250
  5.1 0.0 copy-done
  5.2 0.0 copy-start.2
  5.2 0.0 copy-done.1
  5.2 3.2 %collective-permute-start.2 = (f32[256,512]{1,0:T(8,128)S(1)}, f32[256,512]{1,0:T(8,128)S(1)}, u32[]{:S(2)}, u32[]{:S(2)}) collective-permute-start(f32[256,512]{1,0:T(8,128)S(1)} %dynamic-slice_bitcast_fusion), channel_id=1, source_target_pairs={{0,3},{1,0},{2,1},{3,2},{4,7},{5,4},{6,5},{7,6},{8,11},{9,8},{10,9... | collective-permute-start | bytes 1572872 | tf_op jit(solution)/shard_map/ppermute | solution.py:250
  8.4 2.1 %collective-permute-start.1 = (f32[256,512]{1,0:T(8,128)S(1)}, f32[256,512]{1,0:T(8,128)S(1)}, u32[]{:S(2)}, u32[]{:S(2)}) collective-permute-start(f32[256,512]{1,0:T(8,128)S(1)} %dynamic-slice_bitcast_fusion), channel_id=1, source_target_pairs={{0,1},{1,2},{2,3},{3,0},{4,5},{5,6},{6,7},{7,4},{8,9},{9,10},{10,1... | collective-permute-start | bytes 1572872 | tf_op jit(solution)/shard_map/ppermute | solution.py:250
  10.5 0.0 copy-start.3
  10.5 0.0 copy-done.2
  10.6 0.6 copy-done.3
  11.2 1.8 %collective-permute-done.refs_0_.refs_5_ = f32[256,512]{1,0:T(8,128)S(1)} collective-permute-done((f32[256,512]{1,0:T(8,128)S(1)}, f32[256,512]{1,0:T(8,128)S(1)}, u32[]{:S(2)}, u32[]{:S(2)}) %collective-permute-start) | collective-permute-done | bytes 524320 | tf_op jit(solution)/shard_map/ppermute | solution.py:250
  13.0 2.7 %collective-permute-done.2.refs_2_.refs_1_ = f32[256,512]{1,0:T(8,128)S(1)} collective-permute-done((f32[256,512]{1,0:T(8,128)S(1)}, f32[256,512]{1,0:T(8,128)S(1)}, u32[]{:S(2)}, u32[]{:S(2)}) %collective-permute-start.2) | collective-permute-done | bytes 524320 | tf_op jit(solution)/shard_map/ppermute | solution.py:250
  15.7 5.4 %collective-permute-start.3 = (f32[256,512]{1,0:T(8,128)}, f32[256,512]{1,0:T(8,128)S(1)}, u32[]{:S(2)}, u32[]{:S(2)}) collective-permute-start(f32[256,512]{1,0:T(8,128)} %copy-done.1), channel_id=1, source_target_pairs={{0,3},{1,0},{2,1},{3,2},{4,7},{5,4},{6,5},{7,6},{8,11},{9,8},{10,9... | collective-permute-start | bytes 1572872 | tf_op jit(solution)/shard_map/ppermute | solution.py:250
  21.1 3.4 %collective-permute-start.4 = (f32[256,512]{1,0:T(8,128)S(1)}, f32[256,512]{1,0:T(8,128)}, u32[]{:S(2)}, u32[]{:S(2)}) collective-permute-start(f32[256,512]{1,0:T(8,128)S(1)} %collective-permute-done.2.refs_2_.refs_1_), channel_id=1, source_target_pairs={{0,3},{1,0},{2,1},{3,2},{4,7},{5,4},{6,5},{7,6},{8,11},{9,8},{10,9... | collective-permute-start | bytes 1572872 | tf_op jit(solution)/shard_map/ppermute | solution.py:250
  24.5 2.1 %collective-permute-start.5 = (f32[256,512]{1,0:T(8,128)S(1)}, f32[256,512]{1,0:T(8,128)}, u32[]{:S(2)}, u32[]{:S(2)}) collective-permute-start(f32[256,512]{1,0:T(8,128)S(1)} %collective-permute-done.refs_0_.refs_5_), channel_id=1, source_target_pairs={{0,1},{1,2},{2,3},{3,0},{4,5},{5,6},{6,7},{7,4},{8,9},{9,10},{10,1... | collective-permute-start | bytes 1572872 | tf_op jit(solution)/shard_map/ppermute | solution.py:250
  26.6 0.0 collective-permute-done.1.refs_1_.refs_6_
  26.6 1.7 %gram.1 = f32[32,128]{1,0:T(8,128)S(1)} custom-call(s32[1]{0:T(128)} %bitcast.group_ref, f32[512,512]{1,0:T(8,128)S(1)} %bitcast.14, f32[256,512]{1,0:T(8,128)S(1)} %collective-permute-done.refs_0_.refs_5_, f32[256,512]{1,0:T(8,128)S(1)} %collective-permute-done.1.refs_1_.refs_6_, f32[256,512]{1,0:T(8,128)S(1)} %collective-permute-done.2.refs_2_.refs_1_), custom_call_target="tpu_custom_call" | custom-call | tf_op jit(solution)/shard_map/gram/pallas_call | solution.py:96
  28.3 14.5 %all_to_all.15 = f32[8,4,128]{2,1,0:T(4,128)S(1)} all-to-all(f32[8,4,128]{2,1,0:T(4,128)S(1)} %bitcast.17), channel_id=1, replica_groups=mesh['y'=4,'z'=16,'c'=2,'x'=4] {'y','c'}, dimensions={0} | all-to-all | bytes 32768 | tf_op jit(solution)/shard_map/all_to_all | solution.py:283
  42.9 26.3 %all_to_all.16 = f32[16,4,128]{2,1,0:T(4,128)S(1)} all-to-all(f32[16,4,128]{2,1,0:T(4,128)S(1)} %broadcast_in_dim.10), channel_id=1, replica_groups=mesh['y'=4,'z'=16,'c'=2,'x'=4] {'z'}, dimensions={0} | all-to-all | bytes 65536 | tf_op jit(solution)/shard_map/all_to_all | solution.py:285
  69.2 0.0 collective-permute-done.3.refs_2_
  69.2 0.0 collective-permute-done.4.refs_3_
  69.2 0.0 collective-permute-done.5.refs_4_
  69.2 12.8 %all_to_all.17 = f32[32,4,128]{2,1,0:T(4,128)S(1)} all-to-all(f32[32,4,128]{2,1,0:T(4,128)S(1)} %broadcast_in_dim.22), channel_id=1, replica_groups=mesh['y'=4,'z'=16,'c'=2,'x'=4] {'x','y','c'}, dimensions={0} | all-to-all | bytes 131072 | tf_op jit(solution)/shard_map/all_to_all | solution.py:287
  82.0 6.9 %project.1 = f32[512,512]{1,0:T(8,128)} custom-call(s32[1]{0:T(128)} %bitcast.group_ref, f32[128,128]{1,0:T(8,128)S(1)} %bitcast.16, f32[33,128]{1,0:T(8,128)S(1)} %pad_maximum_fusion.start_ref, f32[512,512]{1,0:T(8,128)S(1)} %bitcast.15, f32[256,512]{1,0:T(8,128)S(1)} %collective-permute-done.2.refs_2_.refs_1_, ...), custom_call_target="tpu_custom_call" | custom-call | tf_op jit(solution)/shard_map/project/pallas_call | solution.py:230
  (6 shorter events, 0.1 us)
Async XLA Ops:
  0.0 5.1 %copy-start = (f32[32,2,8,512]{3,2,1,0:T(8,128)S(1)}, f32[32,2,8,512]{3,2,1,0:T(8,128)}, u32[]{:S(2)}) copy-start(f32[32,2,8,512]{3,2,1,0:T(8,128)} %param.3) | copy-start | bytes 3145732
  1.2 4.1 %copy-start.1 = (f32[256,512]{1,0:T(8,128)}, f32[256,512]{1,0:T(8,128)S(1)}, u32[]{:S(2)}) copy-start(f32[256,512]{1,0:T(8,128)S(1)} %dynamic-slice_bitcast_fusion.1) | copy-start | bytes 1572868
  1.2 11.8 %collective-permute-start = (f32[256,512]{1,0:T(8,128)S(1)}, f32[256,512]{1,0:T(8,128)S(1)}, u32[]{:S(2)}, u32[]{:S(2)}) collective-permute-start(f32[256,512]{1,0:T(8,128)S(1)} %dynamic-slice_bitcast_fusion.1), channel_id=1, source_target_pairs={{0,1},{1,2},{2,3},{3,0},{4,5},{5,6},{6,7},{7,4},{8,9},{9,10},{10,1... | collective-permute-start | bytes 1572872 | tf_op jit(solution)/shard_map/ppermute | solution.py:250
  5.2 5.4 %copy-start.2 = (f32[128,32]{0,1:T(8,128)S(1)}, f32[128,32]{0,1:T(8,128)}, u32[]{:S(2)}) copy-start(f32[128,32]{0,1:T(8,128)} %param.5) | copy-start | bytes 49156
  5.2 10.5 %collective-permute-start.2 = (f32[256,512]{1,0:T(8,128)S(1)}, f32[256,512]{1,0:T(8,128)S(1)}, u32[]{:S(2)}, u32[]{:S(2)}) collective-permute-start(f32[256,512]{1,0:T(8,128)S(1)} %dynamic-slice_bitcast_fusion), channel_id=1, source_target_pairs={{0,3},{1,0},{2,1},{3,2},{4,7},{5,4},{6,5},{7,6},{8,11},{9,8},{10,9... | collective-permute-start | bytes 1572872 | tf_op jit(solution)/shard_map/ppermute | solution.py:250
  8.4 18.1 %collective-permute-start.1 = (f32[256,512]{1,0:T(8,128)S(1)}, f32[256,512]{1,0:T(8,128)S(1)}, u32[]{:S(2)}, u32[]{:S(2)}) collective-permute-start(f32[256,512]{1,0:T(8,128)S(1)} %dynamic-slice_bitcast_fusion), channel_id=1, source_target_pairs={{0,1},{1,2},{2,3},{3,0},{4,5},{5,6},{6,7},{7,4},{8,9},{9,10},{10,1... | collective-permute-start | bytes 1572872 | tf_op jit(solution)/shard_map/ppermute | solution.py:250
  10.5 0.7 copy-start.3
  15.7 53.5 %collective-permute-start.3 = (f32[256,512]{1,0:T(8,128)}, f32[256,512]{1,0:T(8,128)S(1)}, u32[]{:S(2)}, u32[]{:S(2)}) collective-permute-start(f32[256,512]{1,0:T(8,128)} %copy-done.1), channel_id=1, source_target_pairs={{0,3},{1,0},{2,1},{3,2},{4,7},{5,4},{6,5},{7,6},{8,11},{9,8},{10,9... | collective-permute-start | bytes 1572872 | tf_op jit(solution)/shard_map/ppermute | solution.py:250
  21.1 48.1 %collective-permute-start.4 = (f32[256,512]{1,0:T(8,128)S(1)}, f32[256,512]{1,0:T(8,128)}, u32[]{:S(2)}, u32[]{:S(2)}) collective-permute-start(f32[256,512]{1,0:T(8,128)S(1)} %collective-permute-done.2.refs_2_.refs_1_), channel_id=1, source_target_pairs={{0,3},{1,0},{2,1},{3,2},{4,7},{5,4},{6,5},{7,6},{8,11},{9,8},{10,9... | collective-permute-start | bytes 1572872 | tf_op jit(solution)/shard_map/ppermute | solution.py:250
  24.5 44.7 %collective-permute-start.5 = (f32[256,512]{1,0:T(8,128)S(1)}, f32[256,512]{1,0:T(8,128)}, u32[]{:S(2)}, u32[]{:S(2)}) collective-permute-start(f32[256,512]{1,0:T(8,128)S(1)} %collective-permute-done.refs_0_.refs_5_), channel_id=1, source_target_pairs={{0,1},{1,2},{2,3},{3,0},{4,5},{5,6},{6,7},{7,4},{8,9},{9,10},{10,1... | collective-permute-start | bytes 1572872 | tf_op jit(solution)/shard_map/ppermute | solution.py:250

commit v10 on v9

--- a/solution.py
+++ b/solution.py
@@ -106,11 +106,11 @@
     )(group[None], own, *blocks)
 
 
-def assemble(parts, local):
-    groups = parts.shape[0] // local
-    lane = lax.broadcasted_iota(jnp.int32, (local, parts.shape[1]), 1)
+def assemble(rows):
+    groups = len(rows)
+    local = rows[0].shape[0]
+    lane = lax.broadcasted_iota(jnp.int32, rows[0].shape, 1)
     far = (lane >= 2 * local) & (lane < 3 * local)
-    rows = [parts[g * local : (g + 1) * local] for g in range(groups)]
     slabs = []
     for g in range(groups):
         slab = jnp.where(far, rows[(g + 1) % groups], rows[g])
@@ -145,7 +145,7 @@
 
 def project_kernel(count, local, group_ref, raw_ref, start_ref, *refs):
     own_ref, *split_refs = refs[:7]
-    out_ref, held, after, across, before, ready, full_ref, in_sems, out_sems = refs[7:]
+    out_ref, held, after, across, before, ready, in_sems, out_sems = refs[7:]
     height, cells = out_ref.shape
     tiles = cells // LANES
     group = group_ref[0]
@@ -159,24 +159,24 @@
     for fetch in fetches:
         fetch.start()
     rank = start_ref.shape[0] - 1
-    gain = start_ref[rank:]
-    periods = gain.shape[1]
+    periods = start_ref.shape[1]
+    groups = periods // local
+    start = pltpu.roll(start_ref[...], lax.rem(periods - group * local, periods), 1)
+    gain = start[rank:]
     per_period = height // local
     half = per_period // 2
-    raw = assemble(raw_ref[...], local)
+    firsts = [pl.multiple_of(lax.rem(group + g, groups) * local, local) for g in range(groups)]
+    raw = assemble([raw_ref[pl.ds(first, local), :] for first in firsts])
 
     def grow(basis):
         return dot(basis * gain, raw, 1, 0) * (gain * (1.0 / count))
 
-    grown = grow(start_ref[:rank])
+    grown = grow(start[:rank])
     for _ in range(ITERS - 1):
         later = grow(grown)
         grown = dot(inverse_factor(dot(grown, grown, 1, 1)), later, 1, 0)
     basis = dot(inverse_factor(dot(grown, grown, 1, 1)), grown, 1, 0)
-    full_ref[...] = dot(basis, basis, 0, 0) * gain
-    first = group * local
-    own = full_ref[pl.ds(pl.multiple_of(first, local), local), :]
-    high, low = halves(pltpu.roll(own, lax.rem(periods - first, periods), 1))
+    high, low = halves(dot(basis[:, :local], basis * gain, 0, 0))
     mix = jnp.concatenate(
         [jnp.concatenate([high, high], axis=1), jnp.concatenate([low, jnp.zeros_like(low)], axis=1)],
         axis=0,
@@ -236,7 +236,6 @@
         + [pltpu.VMEM((2, tiles * height // 2, LANES), jnp.float32)] * 3
         + [
             pltpu.VMEM((tiles * height, LANES), jnp.float32),
-            pltpu.VMEM((periods, periods), jnp.float32),
             pltpu.SemaphoreType.DMA((len(blocks) * tiles,)),
             pltpu.SemaphoreType.DMA((tiles,)),
         ],

time: 89.3 us -> 89.2 us (level)
  no operation moved by 1% of the time
where the time goes in v10:
time: 89.2 us; the launch traced here: 88.8 us
  blocking collectives  53.5 us (60%)
  starting transfers between devices  20.1 us (23%)
  Pallas kernels  8.56 us (10%)
  waiting for transfers between devices  4.51 us (5%)
  local copies, waits for them, and re-layouts  1.89 us (2%)
    all_to_all x1, blocking collectives, per_device(): pieces = lax.all_to_all(copies, 'z', 0, 0, tiled=True)  26.3 us
    ppermute x6, starting transfers between devices, shift(): lax.ppermute(value, 'x', [(i, (i + step) % count) for i in range(count)])  20.1 us
    all_to_all x1, blocking collectives, per_device(): lax.all_to_all(gram.reshape(pairs, -1, periods), PAIRS, 0, 0, tiled=True)  14.5 us
    all_to_all x1, blocking collectives, per_device(): lax.all_to_all(copies, ('x',) + PAIRS, 0, 0, tiled=True)  12.8 us
    pallas_call x1, Pallas kernels, project(): pl.pallas_call(functools.partial(project_kernel, count, local), out_shape...  6.83 us
    ppermute x6, waiting for transfers between devices, shift(): lax.ppermute(value, 'x', [(i, (i + step) % count) for i in range(count)])  4.51 us
  transfers between devices with their start and end apart: 6, of which 2 were waited for; matrix products, arithmetic and copies ran while one was open for 0% of the time, Pallas kernels for 2%

profile of v10, /device:TPU:1, one launch (start us, length us, event | category | flops | bytes accessed | tf_op | source)
XLA Modules:
  0.0 88.8 jit_solution(14476508687469314958)
XLA Ops:
  0.0 0.0 copy-start
  0.0 1.2 %dynamic-slice_bitcast_fusion.1 = f32[256,512]{1,0:T(8,128)S(1)} fusion(f32[32,2,8,512]{3,2,1,0:T(8,128)} %param.3, s32[]{:T(128)S(6)} %select_n.20), kind=kLoop, calls=%fused_computation.1 | loop fusion | bytes 1048580 | tf_op jit(solution)/shard_map/reshape | solution.py:268
  1.2 0.0 copy-start.1
  1.2 3.9 %collective-permute-start = (f32[256,512]{1,0:T(8,128)S(1)}, f32[256,512]{1,0:T(8,128)S(1)}, u32[]{:S(2)}, u32[]{:S(2)}) collective-permute-start(f32[256,512]{1,0:T(8,128)S(1)} %dynamic-slice_bitcast_fusion.1), channel_id=1, source_target_pairs={{0,1},{1,2},{2,3},{3,0},{4,5},{5,6},{6,7},{7,4},{8,9},{9,10},{10,1... | collective-permute-start | bytes 1572872 | tf_op jit(solution)/shard_map/ppermute | solution.py:249
  5.1 0.0 copy-done
  5.2 0.0 copy-start.2
  5.2 0.0 copy-done.1
  5.2 3.2 %collective-permute-start.2 = (f32[256,512]{1,0:T(8,128)S(1)}, f32[256,512]{1,0:T(8,128)S(1)}, u32[]{:S(2)}, u32[]{:S(2)}) collective-permute-start(f32[256,512]{1,0:T(8,128)S(1)} %dynamic-slice_bitcast_fusion), channel_id=1, source_target_pairs={{0,3},{1,0},{2,1},{3,2},{4,7},{5,4},{6,5},{7,6},{8,11},{9,8},{10,9... | collective-permute-start | bytes 1572872 | tf_op jit(solution)/shard_map/ppermute | solution.py:249
  8.4 2.1 %collective-permute-start.1 = (f32[256,512]{1,0:T(8,128)S(1)}, f32[256,512]{1,0:T(8,128)S(1)}, u32[]{:S(2)}, u32[]{:S(2)}) collective-permute-start(f32[256,512]{1,0:T(8,128)S(1)} %dynamic-slice_bitcast_fusion), channel_id=1, source_target_pairs={{0,1},{1,2},{2,3},{3,0},{4,5},{5,6},{6,7},{7,4},{8,9},{9,10},{10,1... | collective-permute-start | bytes 1572872 | tf_op jit(solution)/shard_map/ppermute | solution.py:249
  10.5 0.0 copy-start.3
  10.5 0.0 copy-done.2
  10.6 0.6 copy-done.3
  11.2 1.8 %collective-permute-done.refs_0_.refs_5_ = f32[256,512]{1,0:T(8,128)S(1)} collective-permute-done((f32[256,512]{1,0:T(8,128)S(1)}, f32[256,512]{1,0:T(8,128)S(1)}, u32[]{:S(2)}, u32[]{:S(2)}) %collective-permute-start) | collective-permute-done | bytes 524320 | tf_op jit(solution)/shard_map/ppermute | solution.py:249
  13.0 2.7 %collective-permute-done.2.refs_2_.refs_1_ = f32[256,512]{1,0:T(8,128)S(1)} collective-permute-done((f32[256,512]{1,0:T(8,128)S(1)}, f32[256,512]{1,0:T(8,128)S(1)}, u32[]{:S(2)}, u32[]{:S(2)}) %collective-permute-start.2) | collective-permute-done | bytes 524320 | tf_op jit(solution)/shard_map/ppermute | solution.py:249
  15.7 5.4 %collective-permute-start.3 = (f32[256,512]{1,0:T(8,128)}, f32[256,512]{1,0:T(8,128)S(1)}, u32[]{:S(2)}, u32[]{:S(2)}) collective-permute-start(f32[256,512]{1,0:T(8,128)} %copy-done.1), channel_id=1, source_target_pairs={{0,3},{1,0},{2,1},{3,2},{4,7},{5,4},{6,5},{7,6},{8,11},{9,8},{10,9... | collective-permute-start | bytes 1572872 | tf_op jit(solution)/shard_map/ppermute | solution.py:249
  21.1 3.4 %collective-permute-start.4 = (f32[256,512]{1,0:T(8,128)S(1)}, f32[256,512]{1,0:T(8,128)}, u32[]{:S(2)}, u32[]{:S(2)}) collective-permute-start(f32[256,512]{1,0:T(8,128)S(1)} %collective-permute-done.2.refs_2_.refs_1_), channel_id=1, source_target_pairs={{0,3},{1,0},{2,1},{3,2},{4,7},{5,4},{6,5},{7,6},{8,11},{9,8},{10,9... | collective-permute-start | bytes 1572872 | tf_op jit(solution)/shard_map/ppermute | solution.py:249
  24.5 2.1 %collective-permute-start.5 = (f32[256,512]{1,0:T(8,128)S(1)}, f32[256,512]{1,0:T(8,128)}, u32[]{:S(2)}, u32[]{:S(2)}) collective-permute-start(f32[256,512]{1,0:T(8,128)S(1)} %collective-permute-done.refs_0_.refs_5_), channel_id=1, source_target_pairs={{0,1},{1,2},{2,3},{3,0},{4,5},{5,6},{6,7},{7,4},{8,9},{9,10},{10,1... | collective-permute-start | bytes 1572872 | tf_op jit(solution)/shard_map/ppermute | solution.py:249
  26.6 0.0 collective-permute-done.1.refs_1_.refs_6_
  26.6 1.7 %gram.1 = f32[32,128]{1,0:T(8,128)S(1)} custom-call(s32[1]{0:T(128)} %bitcast.group_ref, f32[512,512]{1,0:T(8,128)S(1)} %bitcast.14, f32[256,512]{1,0:T(8,128)S(1)} %collective-permute-done.refs_0_.refs_5_, f32[256,512]{1,0:T(8,128)S(1)} %collective-permute-done.1.refs_1_.refs_6_, f32[256,512]{1,0:T(8,128)S(1)} %collective-permute-done.2.refs_2_.refs_1_), custom_call_target="tpu_custom_call" | custom-call | tf_op jit(solution)/shard_map/gram/pallas_call | solution.py:96
  28.3 14.5 %all_to_all.15 = f32[8,4,128]{2,1,0:T(4,128)S(1)} all-to-all(f32[8,4,128]{2,1,0:T(4,128)S(1)} %bitcast.17), channel_id=1, replica_groups=mesh['y'=4,'z'=16,'c'=2,'x'=4] {'y','c'}, dimensions={0} | all-to-all | bytes 32768 | tf_op jit(solution)/shard_map/all_to_all | solution.py:282
  42.9 26.3 %all_to_all.16 = f32[16,4,128]{2,1,0:T(4,128)S(1)} all-to-all(f32[16,4,128]{2,1,0:T(4,128)S(1)} %broadcast_in_dim.10), channel_id=1, replica_groups=mesh['y'=4,'z'=16,'c'=2,'x'=4] {'z'}, dimensions={0} | all-to-all | bytes 65536 | tf_op jit(solution)/shard_map/all_to_all | solution.py:284
  69.2 0.0 collective-permute-done.3.refs_2_
  69.2 0.0 collective-permute-done.4.refs_3_
  69.2 0.0 collective-permute-done.5.refs_4_
  69.2 12.8 %all_to_all.17 = f32[32,4,128]{2,1,0:T(4,128)S(1)} all-to-all(f32[32,4,128]{2,1,0:T(4,128)S(1)} %broadcast_in_dim.22), channel_id=1, replica_groups=mesh['y'=4,'z'=16,'c'=2,'x'=4] {'x','y','c'}, dimensions={0} | all-to-all | bytes 131072 | tf_op jit(solution)/shard_map/all_to_all | solution.py:286
  82.0 6.8 %project.1 = f32[512,512]{1,0:T(8,128)} custom-call(s32[1]{0:T(128)} %bitcast.group_ref, f32[128,128]{1,0:T(8,128)S(1)} %bitcast.16, f32[33,128]{1,0:T(8,128)S(1)} %pad_maximum_fusion.start_ref, f32[512,512]{1,0:T(8,128)S(1)} %bitcast.15, f32[256,512]{1,0:T(8,128)S(1)} %collective-permute-done.2.refs_2_.refs_1_, ...), custom_call_target="tpu_custom_call" | custom-call | tf_op jit(solution)/shard_map/project/pallas_call | solution.py:230
  (6 shorter events, 0.1 us)
Async XLA Ops:
  0.0 5.1 %copy-start = (f32[32,2,8,512]{3,2,1,0:T(8,128)S(1)}, f32[32,2,8,512]{3,2,1,0:T(8,128)}, u32[]{:S(2)}) copy-start(f32[32,2,8,512]{3,2,1,0:T(8,128)} %param.3) | copy-start | bytes 3145732
  1.2 4.1 %copy-start.1 = (f32[256,512]{1,0:T(8,128)}, f32[256,512]{1,0:T(8,128)S(1)}, u32[]{:S(2)}) copy-start(f32[256,512]{1,0:T(8,128)S(1)} %dynamic-slice_bitcast_fusion.1) | copy-start | bytes 1572868
  1.2 11.8 %collective-permute-start = (f32[256,512]{1,0:T(8,128)S(1)}, f32[256,512]{1,0:T(8,128)S(1)}, u32[]{:S(2)}, u32[]{:S(2)}) collective-permute-start(f32[256,512]{1,0:T(8,128)S(1)} %dynamic-slice_bitcast_fusion.1), channel_id=1, source_target_pairs={{0,1},{1,2},{2,3},{3,0},{4,5},{5,6},{6,7},{7,4},{8,9},{9,10},{10,1... | collective-permute-start | bytes 1572872 | tf_op jit(solution)/shard_map/ppermute | solution.py:249
  5.2 5.4 %copy-start.2 = (f32[128,32]{0,1:T(8,128)S(1)}, f32[128,32]{0,1:T(8,128)}, u32[]{:S(2)}) copy-start(f32[128,32]{0,1:T(8,128)} %param.5) | copy-start | bytes 49156
  5.2 10.5 %collective-permute-start.2 = (f32[256,512]{1,0:T(8,128)S(1)}, f32[256,512]{1,0:T(8,128)S(1)}, u32[]{:S(2)}, u32[]{:S(2)}) collective-permute-start(f32[256,512]{1,0:T(8,128)S(1)} %dynamic-slice_bitcast_fusion), channel_id=1, source_target_pairs={{0,3},{1,0},{2,1},{3,2},{4,7},{5,4},{6,5},{7,6},{8,11},{9,8},{10,9... | collective-permute-start | bytes 1572872 | tf_op jit(solution)/shard_map/ppermute | solution.py:249
  8.4 18.1 %collective-permute-start.1 = (f32[256,512]{1,0:T(8,128)S(1)}, f32[256,512]{1,0:T(8,128)S(1)}, u32[]{:S(2)}, u32[]{:S(2)}) collective-permute-start(f32[256,512]{1,0:T(8,128)S(1)} %dynamic-slice_bitcast_fusion), channel_id=1, source_target_pairs={{0,1},{1,2},{2,3},{3,0},{4,5},{5,6},{6,7},{7,4},{8,9},{9,10},{10,1... | collective-permute-start | bytes 1572872 | tf_op jit(solution)/shard_map/ppermute | solution.py:249
  10.5 0.7 copy-start.3
  15.7 53.5 %collective-permute-start.3 = (f32[256,512]{1,0:T(8,128)}, f32[256,512]{1,0:T(8,128)S(1)}, u32[]{:S(2)}, u32[]{:S(2)}) collective-permute-start(f32[256,512]{1,0:T(8,128)} %copy-done.1), channel_id=1, source_target_pairs={{0,3},{1,0},{2,1},{3,2},{4,7},{5,4},{6,5},{7,6},{8,11},{9,8},{10,9... | collective-permute-start | bytes 1572872 | tf_op jit(solution)/shard_map/ppermute | solution.py:249
  21.1 48.1 %collective-permute-start.4 = (f32[256,512]{1,0:T(8,128)S(1)}, f32[256,512]{1,0:T(8,128)}, u32[]{:S(2)}, u32[]{:S(2)}) collective-permute-start(f32[256,512]{1,0:T(8,128)S(1)} %collective-permute-done.2.refs_2_.refs_1_), channel_id=1, source_target_pairs={{0,3},{1,0},{2,1},{3,2},{4,7},{5,4},{6,5},{7,6},{8,11},{9,8},{10,9... | collective-permute-start | bytes 1572872 | tf_op jit(solution)/shard_map/ppermute | solution.py:249
  24.5 44.7 %collective-permute-start.5 = (f32[256,512]{1,0:T(8,128)S(1)}, f32[256,512]{1,0:T(8,128)}, u32[]{:S(2)}, u32[]{:S(2)}) collective-permute-start(f32[256,512]{1,0:T(8,128)S(1)} %collective-permute-done.refs_0_.refs_5_), channel_id=1, source_target_pairs={{0,1},{1,2},{2,3},{3,0},{4,5},{5,6},{6,7},{7,4},{8,9},{9,10},{10,1... | collective-permute-start | bytes 1572872 | tf_op jit(solution)/shard_map/ppermute | solution.py:249

commit v11 on v10

--- a/solution.py
+++ b/solution.py
@@ -54,7 +54,7 @@
     return high + low
 
 
-def gram_kernel(local, group_ref, own_ref, *refs):
+def gram_kernel(local, place_ref, own_ref, *refs):
     blocks, (out_ref, own, *held, sems) = refs[:3], refs[3:]
     tiles = own_ref.shape[1] // LANES
     copies = tile_copies(own_ref, own, 0, sems, 0)
@@ -66,7 +66,8 @@
         copy.wait()
     per_period = own_ref.shape[0] // local
     half = per_period // 2
-    second = group_ref[0] >= 2
+    second = place_ref[1] >= 2
+    mirrored = place_ref[2] > 0
     near, far = None, None
     for s in range(half):
         parts = [lines(own, tiles, s + t * half, local, per_period) for t in range(2)]
@@ -79,18 +80,20 @@
             near = product if near is None else near + product
         product = dot(jnp.concatenate(first, axis=0), jnp.concatenate(after, axis=0), 1, 1, None)
         far = product if far is None else far + product
+    far = fold(far, local, 0)
+    side = fold(near, local, 2 * local)
     out_ref[...] = jnp.concatenate(
         [
             fold(near, local, 0),
-            jnp.zeros((local, local), jnp.float32),
-            fold(far, local, 0),
-            fold(near, local, 2 * local),
+            jnp.where(mirrored, side, 0.0),
+            jnp.where(mirrored, far.T, far),
+            jnp.where(mirrored, 0.0, side),
         ],
         axis=1,
     )
 
 
-def gram_of(group, own, blocks, local, periods):
+def gram_of(place, own, blocks, local, periods):
     shape = (own.shape[0] * own.shape[1] // LANES, LANES)
     tiles = own.shape[1] // LANES
     return pl.pallas_call(
@@ -103,7 +106,7 @@
         + [pltpu.SemaphoreType.DMA((4 * tiles,))],
         compiler_params=pltpu.CompilerParams(vmem_limit_bytes=32 * 2**20),
         name="gram",
-    )(group[None], own, *blocks)
+    )(place, own, *blocks)
 
 
 def assemble(rows):
@@ -143,17 +146,17 @@
     return work[:, rank:] * lax.rsqrt(pivots[:, rank:])
 
 
-def project_kernel(count, local, group_ref, raw_ref, start_ref, *refs):
+def project_kernel(count, local, place_ref, raw_ref, start_ref, *refs):
     own_ref, *split_refs = refs[:7]
-    out_ref, held, after, across, before, ready, in_sems, out_sems = refs[7:]
+    out_ref, held, others, ready, in_sems, out_sems = refs[7:]
     height, cells = out_ref.shape
     tiles = cells // LANES
-    group = group_ref[0]
-    second = jnp.where(group >= 2, 1, 0)
-    later = jnp.where((group == 1) | (group == 2), 1, 0)
+    group, ring, mirrored = (place_ref[i] for i in range(3))
+    second = jnp.where(ring >= 2, 1, 0)
+    later = jnp.where((ring == 1) | (ring == 2), 1, 0)
     fetches = tile_copies(own_ref, held, 0, in_sems, 0)
-    ends = ((after, second), (across, later), (before, second))
-    places = [place.at[end] for place, first in ends for end in (first, 1 - first)]
+    ends = ((4 * mirrored, second), (2, later), (4 - 4 * mirrored, second))
+    places = [others.at[at + end] for at, first in ends for end in (first, 1 - first)]
     for i, (block, place) in enumerate(zip(split_refs, places)):
         fetches += tile_copies(block, place, 0, in_sems, (1 + i) * tiles)
     for fetch in fetches:
@@ -184,7 +187,7 @@
     for fetch in fetches:
         fetch.wait()
     step = held.shape[0] // tiles
-    side = across.shape[1] // tiles
+    side = others.shape[1] // tiles
     sends = []
     for pair in range(0, tiles, 2):
         for s in range(per_period):
@@ -194,8 +197,10 @@
                         [
                             held[pl.ds(c * step + s, local, stride=per_period), :],
                             *(
-                                split[s // half, pl.ds(c * side + s % half, local, stride=half), :]
-                                for split in (after, across, before)
+                                others[
+                                    at + s // half, pl.ds(c * side + s % half, local, stride=half), :
+                                ]
+                                for at in (0, 2, 4)
                             ),
                         ],
                         axis=0,
@@ -223,7 +228,7 @@
         send.wait()
 
 
-def project(raw, start, group, blocks, local, count):
+def project(raw, start, place, blocks, local, count):
     height, cells = blocks[0].shape
     periods = start.shape[1]
     tiles = cells // LANES
@@ -233,20 +238,26 @@
         in_specs=[pl.BlockSpec(memory_space=pltpu.SMEM)] + [VMEM] * 2 + [ANY] * len(blocks),
         out_specs=ANY,
         scratch_shapes=[pltpu.VMEM((tiles * height, LANES), jnp.float32)]
-        + [pltpu.VMEM((2, tiles * height // 2, LANES), jnp.float32)] * 3
         + [
+            pltpu.VMEM((6, tiles * height // 2, LANES), jnp.float32),
             pltpu.VMEM((tiles * height, LANES), jnp.float32),
             pltpu.SemaphoreType.DMA((len(blocks) * tiles,)),
             pltpu.SemaphoreType.DMA((tiles,)),
         ],
         compiler_params=pltpu.CompilerParams(vmem_limit_bytes=32 * 2**20),
         name="project",
-    )(group[None], raw, start, *blocks)
+    )(place, raw, start, *blocks)
 
 
 def shift(value, step):
     count = lax.axis_size("x")
-    return lax.ppermute(value, "x", [(i, (i + step) % count) for i in range(count)])
+    cores = lax.axis_size("c")
+    pairs = [
+        (c * count + i, c * count + (i + (step if c == 0 else -step)) % count)
+        for c in range(cores)
+        for i in range(count)
+    ]
+    return lax.ppermute(value, ("c", "x"), pairs)
 
 
 def copies_of(pieces, count):
@@ -257,6 +268,9 @@
 def per_device(field, gain, start_basis):
     groups = lax.axis_size("x")
     group = lax.axis_index("x")
+    core = lax.axis_index("c")
+    ring = jnp.where(core == 0, group, (groups - group) % groups)
+    place = jnp.stack([group, ring, core]).astype(jnp.int32)
     local, parts, layers, cells = field.shape
     periods = gain.shape[0]
     pairs = lax.axis_size("y") * lax.axis_size("c")
@@ -267,7 +281,7 @@
         part = lax.dynamic_index_in_dim(block.reshape(field.shape), part, 1, keepdims=False)
         return part.reshape(-1, cells)
 
-    sent = (group + groups - 1) % groups // 2
+    sent = (ring + groups - 1) % groups // 2
     start = jnp.concatenate([start_basis.T, gain[None]], axis=0)
     one = side(own, 1 - sent)
     source, one = lax.optimization_barrier((own, one))
@@ -278,14 +292,14 @@
     first, start = lax.optimization_barrier((first, start))
     one, after, _ = lax.optimization_barrier((one, after, first))
     rest = [shift(one, -1), shift(after, -1), shift(first, 1)]
-    gram = gram_of(group, own, [first, second, after], local, periods)
+    gram = gram_of(place, own, [first, second, after], local, periods)
     pieces = lax.all_to_all(gram.reshape(pairs, -1, periods), PAIRS, 0, 0, tiled=True)
     copies = copies_of(pieces, lax.axis_size("z"))
     pieces = lax.all_to_all(copies, "z", 0, 0, tiled=True)
     copies, rest = lax.optimization_barrier((copies_of(pieces, groups * pairs), rest))
     raw = lax.all_to_all(copies, ("x",) + PAIRS, 0, 0, tiled=True).reshape(periods, periods)
     blocks = [own, after, *rest, first, second]
-    result = project(raw, start, group, blocks, local, count)
+    result = project(raw, start, place, blocks, local, count)
     return result.reshape(field.shape)
 
 

time: 89.2 us -> 91.9 us (1.030)
  waiting for transfers between devices: 4.51 us -> 7.79 us
  blocking collectives: 53.5 us -> 51.7 us
  Pallas kernels: 8.56 us -> 9.72 us
    ppermute x6, waiting for transfers between devices: 4.51 us -> 7.79 us  [shift(): return lax.ppermute(value, ('c', 'x'), pairs)]
    all_to_all x1, blocking collectives: 26.3 us -> 25.2 us  [per_device(): pieces = lax.all_to_all(copies, 'z', 0, 0, tiled=True)]
  transfers between devices with their start and end apart: 6 -> 6, of which waited for: 2 -> 1; matrix products, arithmetic and copies ran while one was open for 0% -> 0% of each run, Pallas kernels for 2% -> 3%
where the time goes in v11:
time: 91.9 us; the launch traced here: 91.5 us
  blocking collectives  51.7 us (56%)
  starting transfers between devices  20.1 us (22%)
  Pallas kernels  9.72 us (11%)
  waiting for transfers between devices  7.79 us (8%)
  local copies, waits for them, and re-layouts  1.89 us (2%)
    all_to_all x1, blocking collectives, per_device(): pieces = lax.all_to_all(copies, 'z', 0, 0, tiled=True)  25.2 us
    ppermute x6, starting transfers between devices, shift(): return lax.ppermute(value, ('c', 'x'), pairs)  20.1 us
    all_to_all x1, blocking collectives, per_device(): lax.all_to_all(gram.reshape(pairs, -1, periods), PAIRS, 0, 0, tiled=True)  13.8 us
    all_to_all x1, blocking collectives, per_device(): lax.all_to_all(copies, ('x',) + PAIRS, 0, 0, tiled=True)  12.8 us
    ppermute x6, waiting for transfers between devices, shift(): return lax.ppermute(value, ('c', 'x'), pairs)  7.79 us
    pallas_call x1, Pallas kernels, project(): pl.pallas_call(functools.partial(project_kernel, count, local), out_shape...  7.39 us
    pallas_call x1, Pallas kernels, gram_of(): pl.pallas_call(functools.partial(gram_kernel, local), out_shape=jax.Shape...  2.34 us
  transfers between devices with their start and end apart: 6, of which 1 were waited for; matrix products, arithmetic and copies ran while one was open for 0% of the time, Pallas kernels for 3%

profile of v11, /device:TPU:1, one launch (start us, length us, event | category | flops | bytes accessed | tf_op | source)
XLA Modules:
  0.0 91.5 jit_solution(6343401887197195607)
XLA Ops:
  0.0 0.0 copy-start
  0.0 1.2 %dynamic-slice_bitcast_fusion.1 = f32[256,512]{1,0:T(8,128)S(1)} fusion(f32[32,2,8,512]{3,2,1,0:T(8,128)} %param.3, s32[]{:T(128)S(6)} %select_n.29), kind=kLoop, calls=%fused_computation.1 | loop fusion | bytes 1048580 | tf_op jit(solution)/shard_map/reshape | solution.py:282
  1.2 0.0 copy-start.1
  1.2 5.2 %collective-permute-start = (f32[256,512]{1,0:T(8,128)S(1)}, f32[256,512]{1,0:T(8,128)S(1)}, u32[]{:S(2)}, u32[]{:S(2)}) collective-permute-start(f32[256,512]{1,0:T(8,128)S(1)} %dynamic-slice_bitcast_fusion.1), channel_id=1, source_target_pairs={{0,1},{1,2},{2,3},{3,0},{4,7},{5,4},{6,5},{7,6},{8,9},{9,10},{10,1... | collective-permute-start | bytes 1572872 | tf_op jit(solution)/shard_map/ppermute | solution.py:260
  6.4 0.0 copy-done
  6.4 0.0 copy-start.2
  6.5 0.0 copy-done.1
  6.5 1.9 %collective-permute-start.2 = (f32[256,512]{1,0:T(8,128)S(1)}, f32[256,512]{1,0:T(8,128)S(1)}, u32[]{:S(2)}, u32[]{:S(2)}) collective-permute-start(f32[256,512]{1,0:T(8,128)S(1)} %dynamic-slice_bitcast_fusion), channel_id=1, source_target_pairs={{0,3},{1,0},{2,1},{3,2},{4,5},{5,6},{6,7},{7,4},{8,11},{9,8},{10,9... | collective-permute-start | bytes 1572872 | tf_op jit(solution)/shard_map/ppermute | solution.py:260
  8.4 4.6 %collective-permute-start.1 = (f32[256,512]{1,0:T(8,128)S(1)}, f32[256,512]{1,0:T(8,128)S(1)}, u32[]{:S(2)}, u32[]{:S(2)}) collective-permute-start(f32[256,512]{1,0:T(8,128)S(1)} %dynamic-slice_bitcast_fusion), channel_id=1, source_target_pairs={{0,1},{1,2},{2,3},{3,0},{4,7},{5,4},{6,5},{7,6},{8,9},{9,10},{10,1... | collective-permute-start | bytes 1572872 | tf_op jit(solution)/shard_map/ppermute | solution.py:260
  13.0 0.0 copy-start.3
  13.0 0.0 copy-done.2
  13.0 0.6 copy-done.3
  13.7 0.0 collective-permute-done.refs_0_.refs_5_
  13.7 7.8 %collective-permute-done.2.refs_2_.refs_1_ = f32[256,512]{1,0:T(8,128)S(1)} collective-permute-done((f32[256,512]{1,0:T(8,128)S(1)}, f32[256,512]{1,0:T(8,128)S(1)}, u32[]{:S(2)}, u32[]{:S(2)}) %collective-permute-start.2) | collective-permute-done | bytes 524320 | tf_op jit(solution)/shard_map/ppermute | solution.py:260
  21.5 1.9 %collective-permute-start.3 = (f32[256,512]{1,0:T(8,128)}, f32[256,512]{1,0:T(8,128)S(1)}, u32[]{:S(2)}, u32[]{:S(2)}) collective-permute-start(f32[256,512]{1,0:T(8,128)} %copy-done.1), channel_id=1, source_target_pairs={{0,3},{1,0},{2,1},{3,2},{4,5},{5,6},{6,7},{7,4},{8,11},{9,8},{10,9... | collective-permute-start | bytes 1572872 | tf_op jit(solution)/shard_map/ppermute | solution.py:260
  23.4 3.0 %collective-permute-start.4 = (f32[256,512]{1,0:T(8,128)S(1)}, f32[256,512]{1,0:T(8,128)}, u32[]{:S(2)}, u32[]{:S(2)}) collective-permute-start(f32[256,512]{1,0:T(8,128)S(1)} %collective-permute-done.2.refs_2_.refs_1_), channel_id=1, source_target_pairs={{0,3},{1,0},{2,1},{3,2},{4,5},{5,6},{6,7},{7,4},{8,11},{9,8},{10,9... | collective-permute-start | bytes 1572872 | tf_op jit(solution)/shard_map/ppermute | solution.py:260
  26.4 3.5 %collective-permute-start.5 = (f32[256,512]{1,0:T(8,128)S(1)}, f32[256,512]{1,0:T(8,128)}, u32[]{:S(2)}, u32[]{:S(2)}) collective-permute-start(f32[256,512]{1,0:T(8,128)S(1)} %collective-permute-done.refs_0_.refs_5_), channel_id=1, source_target_pairs={{0,1},{1,2},{2,3},{3,0},{4,7},{5,4},{6,5},{7,6},{8,9},{9,10},{10,1... | collective-permute-start | bytes 1572872 | tf_op jit(solution)/shard_map/ppermute | solution.py:260
  29.9 0.1 pad_add_fusion.place_ref
  30.0 0.0 collective-permute-done.1.refs_1_.refs_6_
  30.0 2.3 %gram.1 = f32[32,128]{1,0:T(8,128)S(1)} custom-call(s32[3]{0:T(128)S(1)} %pad_add_fusion.place_ref, f32[512,512]{1,0:T(8,128)S(1)} %bitcast.16, f32[256,512]{1,0:T(8,128)S(1)} %collective-permute-done.refs_0_.refs_5_, f32[256,512]{1,0:T(8,128)S(1)} %collective-permute-done.1.refs_1_.refs_6_, f32[256,512]{1,0:T(8,128)S(1)} %collective-permute-done.2.refs_2_.refs_1_), custom_call_target="tpu_custom_call" | custom-call | tf_op jit(solution)/shard_map/gram/pallas_call | solution.py:99
  32.3 13.8 %all_to_all.15 = f32[8,4,128]{2,1,0:T(4,128)S(1)} all-to-all(f32[8,4,128]{2,1,0:T(4,128)S(1)} %bitcast.19), channel_id=1, replica_groups=mesh['y'=4,'z'=16,'c'=2,'x'=4] {'y','c'}, dimensions={0} | all-to-all | bytes 32768 | tf_op jit(solution)/shard_map/all_to_all | solution.py:296
  46.1 25.2 %all_to_all.16 = f32[16,4,128]{2,1,0:T(4,128)S(1)} all-to-all(f32[16,4,128]{2,1,0:T(4,128)S(1)} %broadcast_in_dim.7), channel_id=1, replica_groups=mesh['y'=4,'z'=16,'c'=2,'x'=4] {'z'}, dimensions={0} | all-to-all | bytes 65536 | tf_op jit(solution)/shard_map/all_to_all | solution.py:298
  71.3 0.0 collective-permute-done.3.refs_2_
  71.3 0.0 collective-permute-done.4.refs_3_
  71.3 0.0 collective-permute-done.5.refs_4_
  71.4 12.8 %all_to_all.17 = f32[32,4,128]{2,1,0:T(4,128)S(1)} all-to-all(f32[32,4,128]{2,1,0:T(4,128)S(1)} %broadcast_in_dim.8), channel_id=1, replica_groups=mesh['y'=4,'z'=16,'c'=2,'x'=4] {'x','y','c'}, dimensions={0} | all-to-all | bytes 131072 | tf_op jit(solution)/shard_map/all_to_all | solution.py:300
  84.1 7.4 %project.1 = f32[512,512]{1,0:T(8,128)} custom-call(s32[3]{0:T(128)S(1)} %pad_add_fusion.place_ref, f32[128,128]{1,0:T(8,128)S(1)} %bitcast.18, f32[33,128]{1,0:T(8,128)S(1)} %pad_maximum_fusion.start_ref, f32[512,512]{1,0:T(8,128)S(1)} %bitcast.17, f32[256,512]{1,0:T(8,128)S(1)} %collective-permute-done.2.refs_2_.refs_1_, ...), custom_call_target="tpu_custom_call" | custom-call | tf_op jit(solution)/shard_map/project/pallas_call | solution.py:235
  (6 shorter events, 0.1 us)
Async XLA Ops:
  0.0 6.4 %copy-start = (f32[32,2,8,512]{3,2,1,0:T(8,128)S(1)}, f32[32,2,8,512]{3,2,1,0:T(8,128)}, u32[]{:S(2)}) copy-start(f32[32,2,8,512]{3,2,1,0:T(8,128)} %param.3) | copy-start | bytes 3145732
  1.2 5.3 %copy-start.1 = (f32[256,512]{1,0:T(8,128)}, f32[256,512]{1,0:T(8,128)S(1)}, u32[]{:S(2)}) copy-start(f32[256,512]{1,0:T(8,128)S(1)} %dynamic-slice_bitcast_fusion.1) | copy-start | bytes 1572868
  1.2 12.5 %collective-permute-start = (f32[256,512]{1,0:T(8,128)S(1)}, f32[256,512]{1,0:T(8,128)S(1)}, u32[]{:S(2)}, u32[]{:S(2)}) collective-permute-start(f32[256,512]{1,0:T(8,128)S(1)} %dynamic-slice_bitcast_fusion.1), channel_id=1, source_target_pairs={{0,1},{1,2},{2,3},{3,0},{4,7},{5,4},{6,5},{7,6},{8,9},{9,10},{10,1... | collective-permute-start | bytes 1572872 | tf_op jit(solution)/shard_map/ppermute | solution.py:260
  6.4 6.6 %copy-start.2 = (f32[128,32]{0,1:T(8,128)S(1)}, f32[128,32]{0,1:T(8,128)}, u32[]{:S(2)}) copy-start(f32[128,32]{0,1:T(8,128)} %param.5) | copy-start | bytes 49156
  6.5 15.0 %collective-permute-start.2 = (f32[256,512]{1,0:T(8,128)S(1)}, f32[256,512]{1,0:T(8,128)S(1)}, u32[]{:S(2)}, u32[]{:S(2)}) collective-permute-start(f32[256,512]{1,0:T(8,128)S(1)} %dynamic-slice_bitcast_fusion), channel_id=1, source_target_pairs={{0,3},{1,0},{2,1},{3,2},{4,5},{5,6},{6,7},{7,4},{8,11},{9,8},{10,9... | collective-permute-start | bytes 1572872 | tf_op jit(solution)/shard_map/ppermute | solution.py:260
  8.4 21.5 %collective-permute-start.1 = (f32[256,512]{1,0:T(8,128)S(1)}, f32[256,512]{1,0:T(8,128)S(1)}, u32[]{:S(2)}, u32[]{:S(2)}) collective-permute-start(f32[256,512]{1,0:T(8,128)S(1)} %dynamic-slice_bitcast_fusion), channel_id=1, source_target_pairs={{0,1},{1,2},{2,3},{3,0},{4,7},{5,4},{6,5},{7,6},{8,9},{9,10},{10,1... | collective-permute-start | bytes 1572872 | tf_op jit(solution)/shard_map/ppermute | solution.py:260
  13.0 0.7 copy-start.3
  21.5 49.9 %collective-permute-start.3 = (f32[256,512]{1,0:T(8,128)}, f32[256,512]{1,0:T(8,128)S(1)}, u32[]{:S(2)}, u32[]{:S(2)}) collective-permute-start(f32[256,512]{1,0:T(8,128)} %copy-done.1), channel_id=1, source_target_pairs={{0,3},{1,0},{2,1},{3,2},{4,5},{5,6},{6,7},{7,4},{8,11},{9,8},{10,9... | collective-permute-start | bytes 1572872 | tf_op jit(solution)/shard_map/ppermute | solution.py:260
  23.4 48.0 %collective-permute-start.4 = (f32[256,512]{1,0:T(8,128)S(1)}, f32[256,512]{1,0:T(8,128)}, u32[]{:S(2)}, u32[]{:S(2)}) collective-permute-start(f32[256,512]{1,0:T(8,128)S(1)} %collective-permute-done.2.refs_2_.refs_1_), channel_id=1, source_target_pairs={{0,3},{1,0},{2,1},{3,2},{4,5},{5,6},{6,7},{7,4},{8,11},{9,8},{10,9... | collective-permute-start | bytes 1572872 | tf_op jit(solution)/shard_map/ppermute | solution.py:260
  26.4 45.0 %collective-permute-start.5 = (f32[256,512]{1,0:T(8,128)S(1)}, f32[256,512]{1,0:T(8,128)}, u32[]{:S(2)}, u32[]{:S(2)}) collective-permute-start(f32[256,512]{1,0:T(8,128)S(1)} %collective-permute-done.refs_0_.refs_5_), channel_id=1, source_target_pairs={{0,1},{1,2},{2,3},{3,0},{4,7},{5,4},{6,5},{7,6},{8,9},{9,10},{10,1... | collective-permute-start | bytes 1572872 | tf_op jit(solution)/shard_map/ppermute | solution.py:260

commit v12 on v11

--- a/solution.py
+++ b/solution.py
@@ -54,6 +54,12 @@
     return high + low
 
 
+def decode(place, groups):
+    core = jnp.where(place >= groups, 1, 0)
+    group = place - core * groups
+    return group, jnp.where((core > 0) & (group > 0), groups - group, group), core
+
+
 def gram_kernel(local, place_ref, own_ref, *refs):
     blocks, (out_ref, own, *held, sems) = refs[:3], refs[3:]
     tiles = own_ref.shape[1] // LANES
@@ -66,8 +72,9 @@
         copy.wait()
     per_period = own_ref.shape[0] // local
     half = per_period // 2
-    second = place_ref[1] >= 2
-    mirrored = place_ref[2] > 0
+    _, ring, core = decode(place_ref[0], out_ref.shape[1] // local)
+    second = ring >= 2
+    mirrored = core > 0
     near, far = None, None
     for s in range(half):
         parts = [lines(own, tiles, s + t * half, local, per_period) for t in range(2)]
@@ -106,7 +113,7 @@
         + [pltpu.SemaphoreType.DMA((4 * tiles,))],
         compiler_params=pltpu.CompilerParams(vmem_limit_bytes=32 * 2**20),
         name="gram",
-    )(place, own, *blocks)
+    )(place[None], own, *blocks)
 
 
 def assemble(rows):
@@ -151,7 +158,7 @@
     out_ref, held, others, ready, in_sems, out_sems = refs[7:]
     height, cells = out_ref.shape
     tiles = cells // LANES
-    group, ring, mirrored = (place_ref[i] for i in range(3))
+    group, ring, mirrored = decode(place_ref[0], start_ref.shape[1] // local)
     second = jnp.where(ring >= 2, 1, 0)
     later = jnp.where((ring == 1) | (ring == 2), 1, 0)
     fetches = tile_copies(own_ref, held, 0, in_sems, 0)
@@ -246,7 +253,7 @@
         ],
         compiler_params=pltpu.CompilerParams(vmem_limit_bytes=32 * 2**20),
         name="project",
-    )(place, raw, start, *blocks)
+    )(place[None], raw, start, *blocks)
 
 
 def shift(value, step):
@@ -269,8 +276,8 @@
     groups = lax.axis_size("x")
     group = lax.axis_index("x")
     core = lax.axis_index("c")
-    ring = jnp.where(core == 0, group, (groups - group) % groups)
-    place = jnp.stack([group, ring, core]).astype(jnp.int32)
+    place = core * groups + group
+    ring = decode(place, groups)[1]
     local, parts, layers, cells = field.shape
     periods = gain.shape[0]
     pairs = lax.axis_size("y") * lax.axis_size("c")
@@ -290,7 +297,7 @@
     after = shift(two, -1)
     second = shift(two, 1)
     first, start = lax.optimization_barrier((first, start))
-    one, after, _ = lax.optimization_barrier((one, after, first))
+    one, first = lax.optimization_barrier((one, first))
     rest = [shift(one, -1), shift(after, -1), shift(first, 1)]
     gram = gram_of(place, own, [first, second, after], local, periods)
     pieces = lax.all_to_all(gram.reshape(pairs, -1, periods), PAIRS, 0, 0, tiled=True)

time: 91.9 us -> 88.5 us (0.963)
  waiting for transfers between devices: 7.79 us -> 5.21 us
  Pallas kernels: 9.72 us -> 8.63 us
    all_to_all x1, blocking collectives: 25.2 us -> 21.1 us  [per_device(): pieces = lax.all_to_all(copies, 'z', 0, 0, tiled=True)]
    ppermute x6, waiting for transfers between devices: 7.79 us -> 5.21 us  [shift(): return lax.ppermute(value, ('c', 'x'), pairs)]
    all_to_all x1, blocking collectives: 13.8 us -> 16.4 us  [per_device(): lax.all_to_all(gram.reshape(pairs, -1, periods), PAIRS, 0, 0, tiled=True)]
    all_to_all x1, blocking collectives: 12.8 us -> 14 us  [per_device(): lax.all_to_all(copies, ('x',) + PAIRS, 0, 0, tiled=True)]
  transfers between devices with their start and end apart: 6 -> 6, of which waited for: 1 -> 1; matrix products, arithmetic and copies ran while one was open for 0% -> 0% of each run, Pallas kernels for 3% -> 2%
where the time goes in v12:
time: 88.5 us; the launch traced here: 88.1 us
  blocking collectives  51.4 us (58%)
  starting transfers between devices  20.8 us (24%)
  Pallas kernels  8.63 us (10%)
  waiting for transfers between devices  5.21 us (6%)
  local copies, waits for them, and re-layouts  1.89 us (2%)
    all_to_all x1, blocking collectives, per_device(): pieces = lax.all_to_all(copies, 'z', 0, 0, tiled=True)  21.1 us
    ppermute x6, starting transfers between devices, shift(): return lax.ppermute(value, ('c', 'x'), pairs)  20.8 us
    all_to_all x1, blocking collectives, per_device(): lax.all_to_all(gram.reshape(pairs, -1, periods), PAIRS, 0, 0, tiled=True)  16.4 us
    all_to_all x1, blocking collectives, per_device(): lax.all_to_all(copies, ('x',) + PAIRS, 0, 0, tiled=True)  14 us
    pallas_call x1, Pallas kernels, project(): pl.pallas_call(functools.partial(project_kernel, count, local), out_shape...  6.83 us
    ppermute x6, waiting for transfers between devices, shift(): return lax.ppermute(value, ('c', 'x'), pairs)  5.21 us
    pallas_call x1, Pallas kernels, gram_of(): pl.pallas_call(functools.partial(gram_kernel, local), out_shape=jax.Shape...  1.79 us
  transfers between devices with their start and end apart: 6, of which 1 were waited for; matrix products, arithmetic and copies ran while one was open for 0% of the time, Pallas kernels for 2%

profile of v12, /device:TPU:1, one launch (start us, length us, event | category | flops | bytes accessed | tf_op | source)
XLA Modules:
  0.0 88.1 jit_solution(2448955235671407497)
XLA Ops:
  0.0 0.0 copy-start
  0.0 1.2 %dynamic-slice_bitcast_fusion.1 = f32[256,512]{1,0:T(8,128)S(1)} fusion(f32[32,2,8,512]{3,2,1,0:T(8,128)} %param.3, s32[]{:T(128)S(6)} %select_n.29), kind=kLoop, calls=%fused_computation.1 | loop fusion | bytes 1048580 | tf_op jit(solution)/shard_map/reshape | solution.py:289
  1.2 0.0 copy-start.1
  1.2 5.2 %collective-permute-start = (f32[256,512]{1,0:T(8,128)S(1)}, f32[256,512]{1,0:T(8,128)S(1)}, u32[]{:S(2)}, u32[]{:S(2)}) collective-permute-start(f32[256,512]{1,0:T(8,128)S(1)} %dynamic-slice_bitcast_fusion.1), channel_id=1, source_target_pairs={{0,1},{1,2},{2,3},{3,0},{4,7},{5,4},{6,5},{7,6},{8,9},{9,10},{10,1... | collective-permute-start | bytes 1572872 | tf_op jit(solution)/shard_map/ppermute | solution.py:267
  6.4 0.0 copy-done
  6.4 0.0 copy-start.2
  6.5 0.0 copy-done.1
  6.5 1.9 %collective-permute-start.2 = (f32[256,512]{1,0:T(8,128)S(1)}, f32[256,512]{1,0:T(8,128)S(1)}, u32[]{:S(2)}, u32[]{:S(2)}) collective-permute-start(f32[256,512]{1,0:T(8,128)S(1)} %dynamic-slice_bitcast_fusion), channel_id=1, source_target_pairs={{0,3},{1,0},{2,1},{3,2},{4,5},{5,6},{6,7},{7,4},{8,11},{9,8},{10,9... | collective-permute-start | bytes 1572872 | tf_op jit(solution)/shard_map/ppermute | solution.py:267
  8.4 4.6 %collective-permute-start.1 = (f32[256,512]{1,0:T(8,128)S(1)}, f32[256,512]{1,0:T(8,128)S(1)}, u32[]{:S(2)}, u32[]{:S(2)}) collective-permute-start(f32[256,512]{1,0:T(8,128)S(1)} %dynamic-slice_bitcast_fusion), channel_id=1, source_target_pairs={{0,1},{1,2},{2,3},{3,0},{4,7},{5,4},{6,5},{7,6},{8,9},{9,10},{10,1... | collective-permute-start | bytes 1572872 | tf_op jit(solution)/shard_map/ppermute | solution.py:267
  13.0 0.0 copy-start.3
  13.0 0.0 copy-done.2
  13.0 0.6 copy-done.3
  13.7 0.0 collective-permute-done.refs_0_.refs_5_
  13.7 2.6 %collective-permute-start.3 = (f32[256,512]{1,0:T(8,128)}, f32[256,512]{1,0:T(8,128)S(1)}, u32[]{:S(2)}, u32[]{:S(2)}) collective-permute-start(f32[256,512]{1,0:T(8,128)} %copy-done.1), channel_id=1, source_target_pairs={{0,3},{1,0},{2,1},{3,2},{4,5},{5,6},{6,7},{7,4},{8,11},{9,8},{10,9... | collective-permute-start | bytes 1572872 | tf_op jit(solution)/shard_map/ppermute | solution.py:267
  16.3 5.2 %collective-permute-done.2.refs_2_.refs_1_ = f32[256,512]{1,0:T(8,128)S(1)} collective-permute-done((f32[256,512]{1,0:T(8,128)S(1)}, f32[256,512]{1,0:T(8,128)S(1)}, u32[]{:S(2)}, u32[]{:S(2)}) %collective-permute-start.2) | collective-permute-done | bytes 524320 | tf_op jit(solution)/shard_map/ppermute | solution.py:267
  21.5 1.9 %collective-permute-start.4 = (f32[256,512]{1,0:T(8,128)S(1)}, f32[256,512]{1,0:T(8,128)}, u32[]{:S(2)}, u32[]{:S(2)}) collective-permute-start(f32[256,512]{1,0:T(8,128)S(1)} %collective-permute-done.2.refs_2_.refs_1_), channel_id=1, source_target_pairs={{0,3},{1,0},{2,1},{3,2},{4,5},{5,6},{6,7},{7,4},{8,11},{9,8},{10,9... | collective-permute-start | bytes 1572872 | tf_op jit(solution)/shard_map/ppermute | solution.py:267
  23.4 4.6 %collective-permute-start.5 = (f32[256,512]{1,0:T(8,128)S(1)}, f32[256,512]{1,0:T(8,128)}, u32[]{:S(2)}, u32[]{:S(2)}) collective-permute-start(f32[256,512]{1,0:T(8,128)S(1)} %collective-permute-done.refs_0_.refs_5_), channel_id=1, source_target_pairs={{0,1},{1,2},{2,3},{3,0},{4,7},{5,4},{6,5},{7,6},{8,9},{9,10},{10,1... | collective-permute-start | bytes 1572872 | tf_op jit(solution)/shard_map/ppermute | solution.py:267
  28.0 0.0 collective-permute-done.1.refs_1_.refs_6_
  28.0 1.8 %gram.1 = f32[32,128]{1,0:T(8,128)S(1)} custom-call(s32[1]{0:T(128)} %bitcast.place_ref, f32[512,512]{1,0:T(8,128)S(1)} %bitcast.14, f32[256,512]{1,0:T(8,128)S(1)} %collective-permute-done.refs_0_.refs_5_, f32[256,512]{1,0:T(8,128)S(1)} %collective-permute-done.1.refs_1_.refs_6_, f32[256,512]{1,0:T(8,128)S(1)} %collective-permute-done.2.refs_2_.refs_1_), custom_call_target="tpu_custom_call" | custom-call | tf_op jit(solution)/shard_map/gram/pallas_call | solution.py:106
  29.8 16.4 %all_to_all.15 = f32[8,4,128]{2,1,0:T(4,128)S(1)} all-to-all(f32[8,4,128]{2,1,0:T(4,128)S(1)} %bitcast.17), channel_id=1, replica_groups=mesh['y'=4,'z'=16,'c'=2,'x'=4] {'y','c'}, dimensions={0} | all-to-all | bytes 32768 | tf_op jit(solution)/shard_map/all_to_all | solution.py:303
  46.2 21.1 %all_to_all.16 = f32[16,4,128]{2,1,0:T(4,128)S(1)} all-to-all(f32[16,4,128]{2,1,0:T(4,128)S(1)} %broadcast_in_dim.10), channel_id=1, replica_groups=mesh['y'=4,'z'=16,'c'=2,'x'=4] {'z'}, dimensions={0} | all-to-all | bytes 65536 | tf_op jit(solution)/shard_map/all_to_all | solution.py:305
  67.3 0.0 collective-permute-done.4.refs_3_
  67.3 0.0 collective-permute-done.3.refs_2_
  67.3 0.0 collective-permute-done.5.refs_4_
  67.3 14.0 %all_to_all.17 = f32[32,4,128]{2,1,0:T(4,128)S(1)} all-to-all(f32[32,4,128]{2,1,0:T(4,128)S(1)} %broadcast_in_dim.22), channel_id=1, replica_groups=mesh['y'=4,'z'=16,'c'=2,'x'=4] {'x','y','c'}, dimensions={0} | all-to-all | bytes 131072 | tf_op jit(solution)/shard_map/all_to_all | solution.py:307
  81.3 6.8 %project.1 = f32[512,512]{1,0:T(8,128)} custom-call(s32[1]{0:T(128)} %bitcast.place_ref, f32[128,128]{1,0:T(8,128)S(1)} %bitcast.16, f32[33,128]{1,0:T(8,128)S(1)} %pad_maximum_fusion.start_ref, f32[512,512]{1,0:T(8,128)S(1)} %bitcast.15, f32[256,512]{1,0:T(8,128)S(1)} %collective-permute-done.2.refs_2_.refs_1_, ...), custom_call_target="tpu_custom_call" | custom-call | tf_op jit(solution)/shard_map/project/pallas_call | solution.py:242
  (6 shorter events, 0.1 us)
Async XLA Ops:
  0.0 6.4 %copy-start = (f32[32,2,8,512]{3,2,1,0:T(8,128)S(1)}, f32[32,2,8,512]{3,2,1,0:T(8,128)}, u32[]{:S(2)}) copy-start(f32[32,2,8,512]{3,2,1,0:T(8,128)} %param.3) | copy-start | bytes 3145732
  1.2 5.3 %copy-start.1 = (f32[256,512]{1,0:T(8,128)}, f32[256,512]{1,0:T(8,128)S(1)}, u32[]{:S(2)}) copy-start(f32[256,512]{1,0:T(8,128)S(1)} %dynamic-slice_bitcast_fusion.1) | copy-start | bytes 1572868
  1.2 12.5 %collective-permute-start = (f32[256,512]{1,0:T(8,128)S(1)}, f32[256,512]{1,0:T(8,128)S(1)}, u32[]{:S(2)}, u32[]{:S(2)}) collective-permute-start(f32[256,512]{1,0:T(8,128)S(1)} %dynamic-slice_bitcast_fusion.1), channel_id=1, source_target_pairs={{0,1},{1,2},{2,3},{3,0},{4,7},{5,4},{6,5},{7,6},{8,9},{9,10},{10,1... | collective-permute-start | bytes 1572872 | tf_op jit(solution)/shard_map/ppermute | solution.py:267
  6.4 6.6 %copy-start.2 = (f32[128,32]{0,1:T(8,128)S(1)}, f32[128,32]{0,1:T(8,128)}, u32[]{:S(2)}) copy-start(f32[128,32]{0,1:T(8,128)} %param.5) | copy-start | bytes 49156
  6.5 15.0 %collective-permute-start.2 = (f32[256,512]{1,0:T(8,128)S(1)}, f32[256,512]{1,0:T(8,128)S(1)}, u32[]{:S(2)}, u32[]{:S(2)}) collective-permute-start(f32[256,512]{1,0:T(8,128)S(1)} %dynamic-slice_bitcast_fusion), channel_id=1, source_target_pairs={{0,3},{1,0},{2,1},{3,2},{4,5},{5,6},{6,7},{7,4},{8,11},{9,8},{10,9... | collective-permute-start | bytes 1572872 | tf_op jit(solution)/shard_map/ppermute | solution.py:267
  8.4 19.5 %collective-permute-start.1 = (f32[256,512]{1,0:T(8,128)S(1)}, f32[256,512]{1,0:T(8,128)S(1)}, u32[]{:S(2)}, u32[]{:S(2)}) collective-permute-start(f32[256,512]{1,0:T(8,128)S(1)} %dynamic-slice_bitcast_fusion), channel_id=1, source_target_pairs={{0,1},{1,2},{2,3},{3,0},{4,7},{5,4},{6,5},{7,6},{8,9},{9,10},{10,1... | collective-permute-start | bytes 1572872 | tf_op jit(solution)/shard_map/ppermute | solution.py:267
  13.0 0.7 copy-start.3
  13.7 53.6 %collective-permute-start.3 = (f32[256,512]{1,0:T(8,128)}, f32[256,512]{1,0:T(8,128)S(1)}, u32[]{:S(2)}, u32[]{:S(2)}) collective-permute-start(f32[256,512]{1,0:T(8,128)} %copy-done.1), channel_id=1, source_target_pairs={{0,3},{1,0},{2,1},{3,2},{4,5},{5,6},{6,7},{7,4},{8,11},{9,8},{10,9... | collective-permute-start | bytes 1572872 | tf_op jit(solution)/shard_map/ppermute | solution.py:267
  21.5 45.8 %collective-permute-start.4 = (f32[256,512]{1,0:T(8,128)S(1)}, f32[256,512]{1,0:T(8,128)}, u32[]{:S(2)}, u32[]{:S(2)}) collective-permute-start(f32[256,512]{1,0:T(8,128)S(1)} %collective-permute-done.2.refs_2_.refs_1_), channel_id=1, source_target_pairs={{0,3},{1,0},{2,1},{3,2},{4,5},{5,6},{6,7},{7,4},{8,11},{9,8},{10,9... | collective-permute-start | bytes 1572872 | tf_op jit(solution)/shard_map/ppermute | solution.py:267
  23.4 43.9 %collective-permute-start.5 = (f32[256,512]{1,0:T(8,128)S(1)}, f32[256,512]{1,0:T(8,128)}, u32[]{:S(2)}, u32[]{:S(2)}) collective-permute-start(f32[256,512]{1,0:T(8,128)S(1)} %collective-permute-done.refs_0_.refs_5_), channel_id=1, source_target_pairs={{0,1},{1,2},{2,3},{3,0},{4,7},{5,4},{6,5},{7,6},{8,9},{9,10},{10,1... | collective-permute-start | bytes 1572872 | tf_op jit(solution)/shard_map/ppermute | solution.py:267

commit v13 on v12

--- a/solution.py
+++ b/solution.py
@@ -301,7 +301,9 @@
     rest = [shift(one, -1), shift(after, -1), shift(first, 1)]
     gram = gram_of(place, own, [first, second, after], local, periods)
     pieces = lax.all_to_all(gram.reshape(pairs, -1, periods), PAIRS, 0, 0, tiled=True)
-    copies = copies_of(pieces, lax.axis_size("z"))
+    copies, rest[0], rest[2] = lax.optimization_barrier(
+        (copies_of(pieces, lax.axis_size("z")), rest[0], rest[2])
+    )
     pieces = lax.all_to_all(copies, "z", 0, 0, tiled=True)
     copies, rest = lax.optimization_barrier((copies_of(pieces, groups * pairs), rest))
     raw = lax.all_to_all(copies, ("x",) + PAIRS, 0, 0, tiled=True).reshape(periods, periods)

time: 88.5 us -> 90 us (1.017)
  blocking collectives: 51.4 us -> 57.4 us
  waiting for transfers between devices: 5.21 us -> 1.28 us
    all_to_all x1, blocking collectives: 16.4 us -> 20.9 us  [per_device(): lax.all_to_all(gram.reshape(pairs, -1, periods), PAIRS, 0, 0, tiled=True)]
    ppermute x6, waiting for transfers between devices: 5.21 us -> 1.28 us  [shift(): return lax.ppermute(value, ('c', 'x'), pairs)]
    all_to_all x1, blocking collectives: 14 us -> 16 us  [per_device(): lax.all_to_all(copies, ('x',) + PAIRS, 0, 0, tiled=True)]
where the time goes in v13:
time: 90 us; the launch traced here: 89.6 us
  blocking collectives  57.4 us (64%)
  starting transfers between devices  20.1 us (22%)
  Pallas kernels  8.63 us (10%)
  local copies, waits for them, and re-layouts  1.89 us (2%)
  waiting for transfers between devices  1.28 us (1%)
    all_to_all x1, blocking collectives, per_device(): lax.all_to_all(gram.reshape(pairs, -1, periods), PAIRS, 0, 0, tiled=True)  20.9 us
    all_to_all x1, blocking collectives, per_device(): pieces = lax.all_to_all(copies, 'z', 0, 0, tiled=True)  20.4 us
    ppermute x6, starting transfers between devices, shift(): return lax.ppermute(value, ('c', 'x'), pairs)  20.1 us
    all_to_all x1, blocking collectives, per_device(): lax.all_to_all(copies, ('x',) + PAIRS, 0, 0, tiled=True)  16 us
    pallas_call x1, Pallas kernels, project(): pl.pallas_call(functools.partial(project_kernel, count, local), out_shape...  6.83 us
  transfers between devices with their start and end apart: 6, of which 1 were waited for; matrix products, arithmetic and copies ran while one was open for 0% of the time, Pallas kernels for 2%

profile of v13, /device:TPU:1, one launch (start us, length us, event | category | flops | bytes accessed | tf_op | source)
XLA Modules:
  0.0 89.6 jit_solution(4198717901172944365)
XLA Ops:
  0.0 0.0 copy-start
  0.0 1.2 %dynamic-slice_bitcast_fusion.1 = f32[256,512]{1,0:T(8,128)S(1)} fusion(f32[32,2,8,512]{3,2,1,0:T(8,128)} %param.3, s32[]{:T(128)S(6)} %select_n.29), kind=kLoop, calls=%fused_computation.1 | loop fusion | bytes 1048580 | tf_op jit(solution)/shard_map/reshape | solution.py:289
  1.2 0.0 copy-start.1
  1.2 5.2 %collective-permute-start = (f32[256,512]{1,0:T(8,128)S(1)}, f32[256,512]{1,0:T(8,128)S(1)}, u32[]{:S(2)}, u32[]{:S(2)}) collective-permute-start(f32[256,512]{1,0:T(8,128)S(1)} %dynamic-slice_bitcast_fusion.1), channel_id=1, source_target_pairs={{0,1},{1,2},{2,3},{3,0},{4,7},{5,4},{6,5},{7,6},{8,9},{9,10},{10,1... | collective-permute-start | bytes 1572872 | tf_op jit(solution)/shard_map/ppermute | solution.py:267
  6.4 0.0 copy-done
  6.4 0.0 copy-start.2
  6.5 0.0 copy-done.1
  6.5 1.9 %collective-permute-start.2 = (f32[256,512]{1,0:T(8,128)S(1)}, f32[256,512]{1,0:T(8,128)S(1)}, u32[]{:S(2)}, u32[]{:S(2)}) collective-permute-start(f32[256,512]{1,0:T(8,128)S(1)} %dynamic-slice_bitcast_fusion), channel_id=1, source_target_pairs={{0,3},{1,0},{2,1},{3,2},{4,5},{5,6},{6,7},{7,4},{8,11},{9,8},{10,9... | collective-permute-start | bytes 1572872 | tf_op jit(solution)/shard_map/ppermute | solution.py:267
  8.4 4.6 %collective-permute-start.1 = (f32[256,512]{1,0:T(8,128)S(1)}, f32[256,512]{1,0:T(8,128)S(1)}, u32[]{:S(2)}, u32[]{:S(2)}) collective-permute-start(f32[256,512]{1,0:T(8,128)S(1)} %dynamic-slice_bitcast_fusion), channel_id=1, source_target_pairs={{0,1},{1,2},{2,3},{3,0},{4,7},{5,4},{6,5},{7,6},{8,9},{9,10},{10,1... | collective-permute-start | bytes 1572872 | tf_op jit(solution)/shard_map/ppermute | solution.py:267
  13.0 0.0 copy-start.3
  13.0 0.0 copy-done.2
  13.0 0.6 copy-done.3
  13.7 0.0 collective-permute-done.refs_0_.refs_5_
  13.7 2.6 %collective-permute-start.3 = (f32[256,512]{1,0:T(8,128)}, f32[256,512]{1,0:T(8,128)S(1)}, u32[]{:S(2)}, u32[]{:S(2)}) collective-permute-start(f32[256,512]{1,0:T(8,128)} %copy-done.1), channel_id=1, source_target_pairs={{0,3},{1,0},{2,1},{3,2},{4,5},{5,6},{6,7},{7,4},{8,11},{9,8},{10,9... | collective-permute-start | bytes 1572872 | tf_op jit(solution)/shard_map/ppermute | solution.py:267
  16.3 3.9 %collective-permute-start.4 = (f32[256,512]{1,0:T(8,128)S(1)}, f32[256,512]{1,0:T(8,128)}, u32[]{:S(2)}, u32[]{:S(2)}) collective-permute-start(f32[256,512]{1,0:T(8,128)S(1)} %collective-permute-done.refs_0_.refs_5_), channel_id=1, source_target_pairs={{0,1},{1,2},{2,3},{3,0},{4,7},{5,4},{6,5},{7,6},{8,9},{9,10},{10,1... | collective-permute-start | bytes 1572872 | tf_op jit(solution)/shard_map/ppermute | solution.py:267
  20.2 1.3 %collective-permute-done.2.refs_2_.refs_1_ = f32[256,512]{1,0:T(8,128)S(1)} collective-permute-done((f32[256,512]{1,0:T(8,128)S(1)}, f32[256,512]{1,0:T(8,128)S(1)}, u32[]{:S(2)}, u32[]{:S(2)}) %collective-permute-start.2) | collective-permute-done | bytes 524320 | tf_op jit(solution)/shard_map/ppermute | solution.py:267
  21.5 1.9 %collective-permute-start.5 = (f32[256,512]{1,0:T(8,128)S(1)}, f32[256,512]{1,0:T(8,128)}, u32[]{:S(2)}, u32[]{:S(2)}) collective-permute-start(f32[256,512]{1,0:T(8,128)S(1)} %collective-permute-done.2.refs_2_.refs_1_), channel_id=1, source_target_pairs={{0,3},{1,0},{2,1},{3,2},{4,5},{5,6},{6,7},{7,4},{8,11},{9,8},{10,9... | collective-permute-start | bytes 1572872 | tf_op jit(solution)/shard_map/ppermute | solution.py:267
  23.4 0.0 collective-permute-done.1.refs_1_.refs_6_
  23.4 1.8 %gram.1 = f32[32,128]{1,0:T(8,128)S(1)} custom-call(s32[1]{0:T(128)} %bitcast.place_ref, f32[512,512]{1,0:T(8,128)S(1)} %bitcast.14, f32[256,512]{1,0:T(8,128)S(1)} %collective-permute-done.refs_0_.refs_5_, f32[256,512]{1,0:T(8,128)S(1)} %collective-permute-done.1.refs_1_.refs_6_, f32[256,512]{1,0:T(8,128)S(1)} %collective-permute-done.2.refs_2_.refs_1_), custom_call_target="tpu_custom_call" | custom-call | tf_op jit(solution)/shard_map/gram/pallas_call | solution.py:106
  25.2 20.9 %all_to_all.15 = f32[8,4,128]{2,1,0:T(4,128)S(1)} all-to-all(f32[8,4,128]{2,1,0:T(4,128)S(1)} %bitcast.17), channel_id=1, replica_groups=mesh['y'=4,'z'=16,'c'=2,'x'=4] {'y','c'}, dimensions={0} | all-to-all | bytes 32768 | tf_op jit(solution)/shard_map/all_to_all | solution.py:303
  46.2 0.0 collective-permute-done.3.refs_2_
  46.2 0.0 collective-permute-done.4.refs_4_
  46.2 20.4 %all_to_all.16 = f32[16,4,128]{2,1,0:T(4,128)S(1)} all-to-all(f32[16,4,128]{2,1,0:T(4,128)S(1)} %broadcast_in_dim.10), channel_id=1, replica_groups=mesh['y'=4,'z'=16,'c'=2,'x'=4] {'z'}, dimensions={0} | all-to-all | bytes 65536 | tf_op jit(solution)/shard_map/all_to_all | solution.py:307
  66.7 0.0 collective-permute-done.5.refs_3_
  66.7 16.0 %all_to_all.17 = f32[32,4,128]{2,1,0:T(4,128)S(1)} all-to-all(f32[32,4,128]{2,1,0:T(4,128)S(1)} %broadcast_in_dim.22), channel_id=1, replica_groups=mesh['y'=4,'z'=16,'c'=2,'x'=4] {'x','y','c'}, dimensions={0} | all-to-all | bytes 131072 | tf_op jit(solution)/shard_map/all_to_all | solution.py:309
  82.7 6.8 %project.1 = f32[512,512]{1,0:T(8,128)} custom-call(s32[1]{0:T(128)} %bitcast.place_ref, f32[128,128]{1,0:T(8,128)S(1)} %bitcast.16, f32[33,128]{1,0:T(8,128)S(1)} %pad_maximum_fusion.start_ref, f32[512,512]{1,0:T(8,128)S(1)} %bitcast.15, f32[256,512]{1,0:T(8,128)S(1)} %collective-permute-done.2.refs_2_.refs_1_, ...), custom_call_target="tpu_custom_call" | custom-call | tf_op jit(solution)/shard_map/project/pallas_call | solution.py:242
  (6 shorter events, 0.1 us)
Async XLA Ops:
  0.0 6.4 %copy-start = (f32[32,2,8,512]{3,2,1,0:T(8,128)S(1)}, f32[32,2,8,512]{3,2,1,0:T(8,128)}, u32[]{:S(2)}) copy-start(f32[32,2,8,512]{3,2,1,0:T(8,128)} %param.3) | copy-start | bytes 3145732
  1.2 5.3 %copy-start.1 = (f32[256,512]{1,0:T(8,128)}, f32[256,512]{1,0:T(8,128)S(1)}, u32[]{:S(2)}) copy-start(f32[256,512]{1,0:T(8,128)S(1)} %dynamic-slice_bitcast_fusion.1) | copy-start | bytes 1572868
  1.2 12.5 %collective-permute-start = (f32[256,512]{1,0:T(8,128)S(1)}, f32[256,512]{1,0:T(8,128)S(1)}, u32[]{:S(2)}, u32[]{:S(2)}) collective-permute-start(f32[256,512]{1,0:T(8,128)S(1)} %dynamic-slice_bitcast_fusion.1), channel_id=1, source_target_pairs={{0,1},{1,2},{2,3},{3,0},{4,7},{5,4},{6,5},{7,6},{8,9},{9,10},{10,1... | collective-permute-start | bytes 1572872 | tf_op jit(solution)/shard_map/ppermute | solution.py:267
  6.4 6.6 %copy-start.2 = (f32[128,32]{0,1:T(8,128)S(1)}, f32[128,32]{0,1:T(8,128)}, u32[]{:S(2)}) copy-start(f32[128,32]{0,1:T(8,128)} %param.5) | copy-start | bytes 49156
  6.5 15.0 %collective-permute-start.2 = (f32[256,512]{1,0:T(8,128)S(1)}, f32[256,512]{1,0:T(8,128)S(1)}, u32[]{:S(2)}, u32[]{:S(2)}) collective-permute-start(f32[256,512]{1,0:T(8,128)S(1)} %dynamic-slice_bitcast_fusion), channel_id=1, source_target_pairs={{0,3},{1,0},{2,1},{3,2},{4,5},{5,6},{6,7},{7,4},{8,11},{9,8},{10,9... | collective-permute-start | bytes 1572872 | tf_op jit(solution)/shard_map/ppermute | solution.py:267
  8.4 15.0 %collective-permute-start.1 = (f32[256,512]{1,0:T(8,128)S(1)}, f32[256,512]{1,0:T(8,128)S(1)}, u32[]{:S(2)}, u32[]{:S(2)}) collective-permute-start(f32[256,512]{1,0:T(8,128)S(1)} %dynamic-slice_bitcast_fusion), channel_id=1, source_target_pairs={{0,1},{1,2},{2,3},{3,0},{4,7},{5,4},{6,5},{7,6},{8,9},{9,10},{10,1... | collective-permute-start | bytes 1572872 | tf_op jit(solution)/shard_map/ppermute | solution.py:267
  13.0 0.7 copy-start.3
  13.7 32.5 %collective-permute-start.3 = (f32[256,512]{1,0:T(8,128)}, f32[256,512]{1,0:T(8,128)S(1)}, u32[]{:S(2)}, u32[]{:S(2)}) collective-permute-start(f32[256,512]{1,0:T(8,128)} %copy-done.1), channel_id=1, source_target_pairs={{0,3},{1,0},{2,1},{3,2},{4,5},{5,6},{6,7},{7,4},{8,11},{9,8},{10,9... | collective-permute-start | bytes 1572872 | tf_op jit(solution)/shard_map/ppermute | solution.py:267
  16.3 29.9 %collective-permute-start.4 = (f32[256,512]{1,0:T(8,128)S(1)}, f32[256,512]{1,0:T(8,128)}, u32[]{:S(2)}, u32[]{:S(2)}) collective-permute-start(f32[256,512]{1,0:T(8,128)S(1)} %collective-permute-done.refs_0_.refs_5_), channel_id=1, source_target_pairs={{0,1},{1,2},{2,3},{3,0},{4,7},{5,4},{6,5},{7,6},{8,9},{9,10},{10,1... | collective-permute-start | bytes 1572872 | tf_op jit(solution)/shard_map/ppermute | solution.py:267
  21.5 45.2 %collective-permute-start.5 = (f32[256,512]{1,0:T(8,128)S(1)}, f32[256,512]{1,0:T(8,128)}, u32[]{:S(2)}, u32[]{:S(2)}) collective-permute-start(f32[256,512]{1,0:T(8,128)S(1)} %collective-permute-done.2.refs_2_.refs_1_), channel_id=1, source_target_pairs={{0,3},{1,0},{2,1},{3,2},{4,5},{5,6},{6,7},{7,4},{8,11},{9,8},{10,9... | collective-permute-start | bytes 1572872 | tf_op jit(solution)/shard_map/ppermute | solution.py:267

commit v14 on v12

--- a/solution.py
+++ b/solution.py
@@ -301,7 +301,7 @@
     rest = [shift(one, -1), shift(after, -1), shift(first, 1)]
     gram = gram_of(place, own, [first, second, after], local, periods)
     pieces = lax.all_to_all(gram.reshape(pairs, -1, periods), PAIRS, 0, 0, tiled=True)
-    copies = copies_of(pieces, lax.axis_size("z"))
+    copies, rest[2] = lax.optimization_barrier((copies_of(pieces, lax.axis_size("z")), rest[2]))
     pieces = lax.all_to_all(copies, "z", 0, 0, tiled=True)
     copies, rest = lax.optimization_barrier((copies_of(pieces, groups * pairs), rest))
     raw = lax.all_to_all(copies, ("x",) + PAIRS, 0, 0, tiled=True).reshape(periods, periods)

time: 88.5 us -> 87.3 us (0.986)
  waiting for transfers between devices: 5.21 us -> 3.94 us
    all_to_all x1, blocking collectives: 21.1 us -> 23.1 us  [per_device(): pieces = lax.all_to_all(copies, 'z', 0, 0, tiled=True)]
    ppermute x6, waiting for transfers between devices: 5.21 us -> 3.94 us  [shift(): return lax.ppermute(value, ('c', 'x'), pairs)]
    all_to_all x1, blocking collectives: 14 us -> 13 us  [per_device(): lax.all_to_all(copies, ('x',) + PAIRS, 0, 0, tiled=True)]
where the time goes in v14:
time: 87.3 us; the launch traced here: 86.9 us
  blocking collectives  51.8 us (59%)
  starting transfers between devices  20.5 us (23%)
  Pallas kernels  8.62 us (10%)
  waiting for transfers between devices  3.94 us (5%)
  local copies, waits for them, and re-layouts  1.89 us (2%)
    all_to_all x1, blocking collectives, per_device(): pieces = lax.all_to_all(copies, 'z', 0, 0, tiled=True)  23.1 us
    ppermute x6, starting transfers between devices, shift(): return lax.ppermute(value, ('c', 'x'), pairs)  20.5 us
    all_to_all x1, blocking collectives, per_device(): lax.all_to_all(gram.reshape(pairs, -1, periods), PAIRS, 0, 0, tiled=True)  15.7 us
    all_to_all x1, blocking collectives, per_device(): lax.all_to_all(copies, ('x',) + PAIRS, 0, 0, tiled=True)  13 us
    pallas_call x1, Pallas kernels, project(): pl.pallas_call(functools.partial(project_kernel, count, local), out_shape...  6.83 us
    ppermute x6, waiting for transfers between devices, shift(): return lax.ppermute(value, ('c', 'x'), pairs)  3.94 us
    pallas_call x1, Pallas kernels, gram_of(): pl.pallas_call(functools.partial(gram_kernel, local), out_shape=jax.Shape...  1.79 us
  transfers between devices with their start and end apart: 6, of which 1 were waited for; matrix products, arithmetic and copies ran while one was open for 0% of the time, Pallas kernels for 2%

profile of v14, /device:TPU:1, one launch (start us, length us, event | category | flops | bytes accessed | tf_op | source)
XLA Modules:
  0.0 86.9 jit_solution(9689857508386163838)
XLA Ops:
  0.0 0.0 copy-start
  0.0 1.2 %dynamic-slice_bitcast_fusion.1 = f32[256,512]{1,0:T(8,128)S(1)} fusion(f32[32,2,8,512]{3,2,1,0:T(8,128)} %param.3, s32[]{:T(128)S(6)} %select_n.29), kind=kLoop, calls=%fused_computation.1 | loop fusion | bytes 1048580 | tf_op jit(solution)/shard_map/reshape | solution.py:289
  1.2 0.0 copy-start.1
  1.2 5.2 %collective-permute-start = (f32[256,512]{1,0:T(8,128)S(1)}, f32[256,512]{1,0:T(8,128)S(1)}, u32[]{:S(2)}, u32[]{:S(2)}) collective-permute-start(f32[256,512]{1,0:T(8,128)S(1)} %dynamic-slice_bitcast_fusion.1), channel_id=1, source_target_pairs={{0,1},{1,2},{2,3},{3,0},{4,7},{5,4},{6,5},{7,6},{8,9},{9,10},{10,1... | collective-permute-start | bytes 1572872 | tf_op jit(solution)/shard_map/ppermute | solution.py:267
  6.4 0.0 copy-done
  6.4 0.0 copy-start.2
  6.5 0.0 copy-done.1
  6.5 1.9 %collective-permute-start.2 = (f32[256,512]{1,0:T(8,128)S(1)}, f32[256,512]{1,0:T(8,128)S(1)}, u32[]{:S(2)}, u32[]{:S(2)}) collective-permute-start(f32[256,512]{1,0:T(8,128)S(1)} %dynamic-slice_bitcast_fusion), channel_id=1, source_target_pairs={{0,3},{1,0},{2,1},{3,2},{4,5},{5,6},{6,7},{7,4},{8,11},{9,8},{10,9... | collective-permute-start | bytes 1572872 | tf_op jit(solution)/shard_map/ppermute | solution.py:267
  8.4 4.6 %collective-permute-start.1 = (f32[256,512]{1,0:T(8,128)S(1)}, f32[256,512]{1,0:T(8,128)S(1)}, u32[]{:S(2)}, u32[]{:S(2)}) collective-permute-start(f32[256,512]{1,0:T(8,128)S(1)} %dynamic-slice_bitcast_fusion), channel_id=1, source_target_pairs={{0,1},{1,2},{2,3},{3,0},{4,7},{5,4},{6,5},{7,6},{8,9},{9,10},{10,1... | collective-permute-start | bytes 1572872 | tf_op jit(solution)/shard_map/ppermute | solution.py:267
  13.0 0.0 copy-start.3
  13.0 0.0 copy-done.2
  13.0 0.6 copy-done.3
  13.7 0.0 collective-permute-done.refs_0_.refs_5_
  13.7 3.8 %collective-permute-start.3 = (f32[256,512]{1,0:T(8,128)S(1)}, f32[256,512]{1,0:T(8,128)S(1)}, u32[]{:S(2)}, u32[]{:S(2)}) collective-permute-start(f32[256,512]{1,0:T(8,128)S(1)} %collective-permute-done.refs_0_.refs_5_), channel_id=1, source_target_pairs={{0,1},{1,2},{2,3},{3,0},{4,7},{5,4},{6,5},{7,6},{8,9},{9,10},{10,1... | collective-permute-start | bytes 1572872 | tf_op jit(solution)/shard_map/ppermute | solution.py:267
  17.5 3.9 %collective-permute-done.2.refs_2_.refs_1_ = f32[256,512]{1,0:T(8,128)S(1)} collective-permute-done((f32[256,512]{1,0:T(8,128)S(1)}, f32[256,512]{1,0:T(8,128)S(1)}, u32[]{:S(2)}, u32[]{:S(2)}) %collective-permute-start.2) | collective-permute-done | bytes 524320 | tf_op jit(solution)/shard_map/ppermute | solution.py:267
  21.5 1.9 %collective-permute-start.5 = (f32[256,512]{1,0:T(8,128)S(1)}, f32[256,512]{1,0:T(8,128)}, u32[]{:S(2)}, u32[]{:S(2)}) collective-permute-start(f32[256,512]{1,0:T(8,128)S(1)} %collective-permute-done.2.refs_2_.refs_1_), channel_id=1, source_target_pairs={{0,3},{1,0},{2,1},{3,2},{4,5},{5,6},{6,7},{7,4},{8,11},{9,8},{10,9... | collective-permute-start | bytes 1572872 | tf_op jit(solution)/shard_map/ppermute | solution.py:267
  23.4 3.0 %collective-permute-start.4 = (f32[256,512]{1,0:T(8,128)}, f32[256,512]{1,0:T(8,128)}, u32[]{:S(2)}, u32[]{:S(2)}) collective-permute-start(f32[256,512]{1,0:T(8,128)} %copy-done.1), channel_id=1, source_target_pairs={{0,3},{1,0},{2,1},{3,2},{4,5},{5,6},{6,7},{7,4},{8,11},{9,8},{10,9... | collective-permute-start | bytes 1572872 | tf_op jit(solution)/shard_map/ppermute | solution.py:267
  26.4 0.0 collective-permute-done.1.refs_1_.refs_6_
  26.4 1.8 %gram.1 = f32[32,128]{1,0:T(8,128)S(1)} custom-call(s32[1]{0:T(128)} %bitcast.place_ref, f32[512,512]{1,0:T(8,128)S(1)} %bitcast.14, f32[256,512]{1,0:T(8,128)S(1)} %collective-permute-done.refs_0_.refs_5_, f32[256,512]{1,0:T(8,128)S(1)} %collective-permute-done.1.refs_1_.refs_6_, f32[256,512]{1,0:T(8,128)S(1)} %collective-permute-done.2.refs_2_.refs_1_), custom_call_target="tpu_custom_call" | custom-call | tf_op jit(solution)/shard_map/gram/pallas_call | solution.py:106
  28.2 15.7 %all_to_all.15 = f32[8,4,128]{2,1,0:T(4,128)S(1)} all-to-all(f32[8,4,128]{2,1,0:T(4,128)S(1)} %bitcast.17), channel_id=1, replica_groups=mesh['y'=4,'z'=16,'c'=2,'x'=4] {'y','c'}, dimensions={0} | all-to-all | bytes 32768 | tf_op jit(solution)/shard_map/all_to_all | solution.py:303
  44.0 0.0 collective-permute-done.3.refs_4_
  44.0 23.1 %all_to_all.16 = f32[16,4,128]{2,1,0:T(4,128)S(1)} all-to-all(f32[16,4,128]{2,1,0:T(4,128)S(1)} %broadcast_in_dim.10), channel_id=1, replica_groups=mesh['y'=4,'z'=16,'c'=2,'x'=4] {'z'}, dimensions={0} | all-to-all | bytes 65536 | tf_op jit(solution)/shard_map/all_to_all | solution.py:305
  67.1 0.0 collective-permute-done.5.refs_3_
  67.1 0.0 collective-permute-done.4.refs_2_
  67.1 13.0 %all_to_all.17 = f32[32,4,128]{2,1,0:T(4,128)S(1)} all-to-all(f32[32,4,128]{2,1,0:T(4,128)S(1)} %broadcast_in_dim.22), channel_id=1, replica_groups=mesh['y'=4,'z'=16,'c'=2,'x'=4] {'x','y','c'}, dimensions={0} | all-to-all | bytes 131072 | tf_op jit(solution)/shard_map/all_to_all | solution.py:307
  80.0 6.8 %project.1 = f32[512,512]{1,0:T(8,128)} custom-call(s32[1]{0:T(128)} %bitcast.place_ref, f32[128,128]{1,0:T(8,128)S(1)} %bitcast.16, f32[33,128]{1,0:T(8,128)S(1)} %pad_maximum_fusion.start_ref, f32[512,512]{1,0:T(8,128)S(1)} %bitcast.15, f32[256,512]{1,0:T(8,128)S(1)} %collective-permute-done.2.refs_2_.refs_1_, f32[256,512]{1,0:T(8,128)} %collective-permute-done.4.refs_2_, ...), custom_call_target="tpu_custom_call" | custom-call | tf_op jit(solution)/shard_map/project/pallas_call | solution.py:242
  (6 shorter events, 0.1 us)
Async XLA Ops:
  0.0 6.4 %copy-start = (f32[32,2,8,512]{3,2,1,0:T(8,128)S(1)}, f32[32,2,8,512]{3,2,1,0:T(8,128)}, u32[]{:S(2)}) copy-start(f32[32,2,8,512]{3,2,1,0:T(8,128)} %param.3) | copy-start | bytes 3145732
  1.2 5.3 %copy-start.1 = (f32[256,512]{1,0:T(8,128)}, f32[256,512]{1,0:T(8,128)S(1)}, u32[]{:S(2)}) copy-start(f32[256,512]{1,0:T(8,128)S(1)} %dynamic-slice_bitcast_fusion.1) | copy-start | bytes 1572868
  1.2 12.5 %collective-permute-start = (f32[256,512]{1,0:T(8,128)S(1)}, f32[256,512]{1,0:T(8,128)S(1)}, u32[]{:S(2)}, u32[]{:S(2)}) collective-permute-start(f32[256,512]{1,0:T(8,128)S(1)} %dynamic-slice_bitcast_fusion.1), channel_id=1, source_target_pairs={{0,1},{1,2},{2,3},{3,0},{4,7},{5,4},{6,5},{7,6},{8,9},{9,10},{10,1... | collective-permute-start | bytes 1572872 | tf_op jit(solution)/shard_map/ppermute | solution.py:267
  6.4 6.6 %copy-start.2 = (f32[128,32]{0,1:T(8,128)S(1)}, f32[128,32]{0,1:T(8,128)}, u32[]{:S(2)}) copy-start(f32[128,32]{0,1:T(8,128)} %param.5) | copy-start | bytes 49156
  6.5 15.0 %collective-permute-start.2 = (f32[256,512]{1,0:T(8,128)S(1)}, f32[256,512]{1,0:T(8,128)S(1)}, u32[]{:S(2)}, u32[]{:S(2)}) collective-permute-start(f32[256,512]{1,0:T(8,128)S(1)} %dynamic-slice_bitcast_fusion), channel_id=1, source_target_pairs={{0,3},{1,0},{2,1},{3,2},{4,5},{5,6},{6,7},{7,4},{8,11},{9,8},{10,9... | collective-permute-start | bytes 1572872 | tf_op jit(solution)/shard_map/ppermute | solution.py:267
  8.4 17.9 %collective-permute-start.1 = (f32[256,512]{1,0:T(8,128)S(1)}, f32[256,512]{1,0:T(8,128)S(1)}, u32[]{:S(2)}, u32[]{:S(2)}) collective-permute-start(f32[256,512]{1,0:T(8,128)S(1)} %dynamic-slice_bitcast_fusion), channel_id=1, source_target_pairs={{0,1},{1,2},{2,3},{3,0},{4,7},{5,4},{6,5},{7,6},{8,9},{9,10},{10,1... | collective-permute-start | bytes 1572872 | tf_op jit(solution)/shard_map/ppermute | solution.py:267
  13.0 0.7 copy-start.3
  13.7 30.3 %collective-permute-start.3 = (f32[256,512]{1,0:T(8,128)S(1)}, f32[256,512]{1,0:T(8,128)S(1)}, u32[]{:S(2)}, u32[]{:S(2)}) collective-permute-start(f32[256,512]{1,0:T(8,128)S(1)} %collective-permute-done.refs_0_.refs_5_), channel_id=1, source_target_pairs={{0,1},{1,2},{2,3},{3,0},{4,7},{5,4},{6,5},{7,6},{8,9},{9,10},{10,1... | collective-permute-start | bytes 1572872 | tf_op jit(solution)/shard_map/ppermute | solution.py:267
  21.5 45.6 %collective-permute-start.5 = (f32[256,512]{1,0:T(8,128)S(1)}, f32[256,512]{1,0:T(8,128)}, u32[]{:S(2)}, u32[]{:S(2)}) collective-permute-start(f32[256,512]{1,0:T(8,128)S(1)} %collective-permute-done.2.refs_2_.refs_1_), channel_id=1, source_target_pairs={{0,3},{1,0},{2,1},{3,2},{4,5},{5,6},{6,7},{7,4},{8,11},{9,8},{10,9... | collective-permute-start | bytes 1572872 | tf_op jit(solution)/shard_map/ppermute | solution.py:267
  23.4 43.7 %collective-permute-start.4 = (f32[256,512]{1,0:T(8,128)}, f32[256,512]{1,0:T(8,128)}, u32[]{:S(2)}, u32[]{:S(2)}) collective-permute-start(f32[256,512]{1,0:T(8,128)} %copy-done.1), channel_id=1, source_target_pairs={{0,3},{1,0},{2,1},{3,2},{4,5},{5,6},{6,7},{7,4},{8,11},{9,8},{10,9... | collective-permute-start | bytes 1572872 | tf_op jit(solution)/shard_map/ppermute | solution.py:267
